TPU v7x, 32 devices: a whole 2x2x4 slice. The times are simulated.
32 devices in a mesh: item: 4 (over x, core), seq: 2 (over y), mp: 4 (over z).
Axes of the slice: x: 2, y: 2, z: 4, core: 2. Of those that a mesh axis runs over, the one named last changes fastest.
Arguments:
- hidden_in: bfloat16 [4, 2560, 2048], P('item', 'seq'), may hold values from -6 to 6
- cotangent: bfloat16 [4, 2560, 2048], P('item', 'seq'), may hold values from -6 to 6
- seg_lengths: int32 [4, 2], P('item'), may hold values from 640 to 1230, as said below
- pre_gain: float32 [2048], replicated, may hold values from 0.1 to 1.9
- pre_shift: float32 [2048], replicated, may hold values from -2 to 2
- qkv_weight: bfloat16 [2048, 3, 2048], P(('item', 'seq'), None, 'mp'), may hold values from -0.125 to 0.125
- qv_bias: float32 [2, 2048], P(None, 'mp'), may hold values from -2 to 2
- out_weight: bfloat16 [2048, 2048], P('mp', ('item', 'seq')), may hold values from -0.5 to 0.5
- out_bias: float32 [2048], replicated, may hold values from -2 to 2
- mid_gain: float32 [2048], replicated, may hold values from 0.1 to 1.9
- mid_shift: float32 [2048], replicated, may hold values from -2 to 2
- up_weight: bfloat16 [2048, 8192], P(('item', 'seq'), 'mp'), may hold values from -0.125 to 0.125
- up_bias: float32 [8192], P('mp'), may hold values from -3 to 3
- down_weight: bfloat16 [8192, 2048], P('mp', ('item', 'seq')), may hold values from -0.0625 to 0.0625
- down_bias: float32 [2048], replicated, may hold values from -2 to 2
Outputs:
- hidden_out: bfloat16 [4, 2560, 2048], P('item', 'seq')
- input_grad: float32 [4, 2560, 2048], P('item', 'seq')
- pre_gain_grad: float32 [2048], replicated
- pre_shift_grad: float32 [2048], replicated
- qkv_grad: float32 [2048, 3, 2048], P(('item', 'seq'), None, 'mp')
- qv_bias_grad: float32 [2, 2048], P(None, 'mp')
- out_grad: float32 [2048, 2048], P('mp', ('item', 'seq'))
- out_bias_grad: float32 [2048], replicated
- mid_gain_grad: float32 [2048], replicated
- mid_shift_grad: float32 [2048], replicated
- up_grad: float32 [2048, 8192], P(('item', 'seq'), 'mp')
- up_bias_grad: float32 [8192], P('mp')
- down_grad: float32 [8192, 2048], P('mp', ('item', 'seq'))
- down_bias_grad: float32 [2048], replicated
Inputs may be any that keep to these rules, and one draw needn't show every extreme that they name: `seg_lengths`: in every item at least one segment has 1230 content tokens.
All inputs are finite; a program needn't handle non-finite values.
Results may differ from a plain program's by a relative error of at most 0.012.
Values may be sent and summed in bfloat16 or wider, within the bound.
A program may use at most 320 MiB of HBM per device.

v0:
```python
import math

import jax
import jax.numpy as jnp
from jax import lax
from jax.sharding import PartitionSpec as P

HDIM = 64
SLOT = 1280
SEGS = 2
SUMM = 50
TOKENS = 2560


eps = 1e-05


def norm_parts(values, gain, shift):
    center = jnp.mean(values, axis=-1, keepdims=True)
    centered = values - center
    inverse = lax.rsqrt(jnp.mean(centered * centered, axis=-1, keepdims=True) + eps)
    normed = centered * inverse
    return (normed * gain + shift, normed, inverse)


def norm_back(grad_out, normed, inverse, gain):
    scaled = grad_out * gain
    centered = scaled - jnp.mean(scaled, axis=-1, keepdims=True)
    grad_in = inverse * (centered - normed * jnp.mean(scaled * normed, axis=-1, keepdims=True))
    return (grad_in, jnp.sum(grad_out * normed, axis=0), jnp.sum(grad_out, axis=0))


def row_layout(row_index, lengths):
    segment = row_index // SLOT
    offset = row_index % SLOT
    picked = segment[:, None] == jnp.arange(SEGS, dtype=jnp.int32)[None, :]
    content = jnp.sum(jnp.where(picked, lengths[None, :], 0), axis=1)
    is_live = offset < content + SUMM
    is_summary = is_live & (offset >= content)
    return (segment, offset, is_live, is_summary)


def allowed(query_layout, key_layout):
    query_segment, query_offset, query_live, query_summary = query_layout
    key_segment, key_offset, key_live, key_summary = key_layout
    same = (query_segment[:, None] == key_segment[None, :]) & (
        key_offset[None, :] <= query_offset[:, None]
    )
    earlier = key_summary[None, :] & (key_segment[None, :] < query_segment[:, None])
    return key_live[None, :] & (same | earlier)


def smooth_gate(values):
    return jax.nn.gelu(values, approximate=True)


def body(
    hidden_in,
    cotangent,
    seg_lengths,
    pre_gain,
    pre_shift,
    qkv_weight,
    qv_bias,
    out_weight,
    out_bias,
    mid_gain,
    mid_shift,
    up_weight,
    up_bias,
    down_weight,
    down_bias,
):
    scale = 1.0 / math.sqrt(HDIM)
    qkv_full, up_full, out_full, down_full = (
        lax.all_gather(qkv_weight, ("item", "seq"), axis=0, tiled=True),
        lax.all_gather(up_weight, ("item", "seq"), axis=0, tiled=True),
        lax.all_gather(out_weight, ("item", "seq"), axis=1, tiled=True),
        lax.all_gather(down_weight, ("item", "seq"), axis=1, tiled=True),
    )
    hidden = hidden_in[0].astype(jnp.float32)
    lengths = seg_lengths[0]
    local_rows = hidden.shape[0]
    width = qkv_weight.shape[2]
    local_heads = width // HDIM
    query_rows = lax.axis_index("seq") * local_rows + jnp.arange(local_rows, dtype=jnp.int32)
    query_layout = row_layout(query_rows, lengths)
    block_rows = math.gcd(TOKENS, 512)
    block_count = TOKENS // block_rows
    block_ids = jnp.arange(block_count, dtype=jnp.int32)
    pre_out, pre_normed, pre_inverse = norm_parts(hidden, pre_gain, pre_shift)
    normed = pre_out.astype(jnp.bfloat16)
    projected = jnp.einsum("td,djc->tjc", normed, qkv_full, preferred_element_type=jnp.float32)
    queries = (projected[:, 0] + qv_bias[0]).astype(jnp.bfloat16)
    keys_local = projected[:, 1].astype(jnp.bfloat16)
    values_local = (projected[:, 2] + qv_bias[1]).astype(jnp.bfloat16)
    keys_all, values_all = (
        lax.all_gather(keys_local, "seq", axis=0, tiled=True),
        lax.all_gather(values_local, "seq", axis=0, tiled=True),
    )
    query_heads = queries.reshape(local_rows, local_heads, HDIM)

    def blocked(table):
        return table.reshape(block_count, block_rows, local_heads, HDIM)

    def block_mask(block_index):
        key_rows = block_index * block_rows + jnp.arange(block_rows, dtype=jnp.int32)
        return allowed(query_layout, row_layout(key_rows, lengths))

    def masked_scores(key_block, permitted):
        raw_scores = jnp.einsum(
            "qhd,khd->hqk", query_heads, key_block, preferred_element_type=jnp.float32
        )
        return jnp.where(permitted[None], raw_scores * scale, -1e30)

    key_blocks = blocked(keys_all)
    value_blocks = blocked(values_all)

    def stats_step(carry, pieces):
        key_block, block_index = pieces
        permitted = block_mask(block_index)

        def stats_update(state):
            running_max, running_sum = state
            scores = masked_scores(key_block, permitted)
            new_max = jnp.maximum(running_max, jnp.max(scores, axis=-1))
            new_sum = running_sum * jnp.exp(running_max - new_max) + jnp.sum(
                jnp.exp(scores - new_max[..., None]), axis=-1
            )
            return (new_max, new_sum)

        return (lax.cond(jnp.any(permitted), stats_update, lambda state: state, carry), None)

    start_max = jnp.full((local_heads, local_rows), -1e30, jnp.float32)
    start_sum = jnp.zeros((local_heads, local_rows), jnp.float32)
    (row_max, row_total), _ = lax.scan(stats_step, (start_max, start_sum), (key_blocks, block_ids))
    log_total = row_max + jnp.log(row_total)

    def block_probs(key_block, permitted):
        return jnp.exp(masked_scores(key_block, permitted) - log_total[..., None])

    def mix_step(total, pieces):
        key_block, value_block, block_index = pieces
        permitted = block_mask(block_index)

        def mix_update(running):
            attn_probs = block_probs(key_block, permitted).astype(jnp.bfloat16)
            return running + jnp.einsum(
                "hqk,khd->qhd", attn_probs, value_block, preferred_element_type=jnp.float32
            )

        return (lax.cond(jnp.any(permitted), mix_update, lambda running: running, total), None)

    mixed, _ = lax.scan(
        mix_step,
        jnp.zeros((local_rows, local_heads, HDIM), jnp.float32),
        (key_blocks, value_blocks, block_ids),
    )
    attended = mixed.reshape(local_rows, width).astype(jnp.bfloat16)
    branch = lax.psum(jnp.dot(attended, out_full, preferred_element_type=jnp.float32), "mp")
    residual = hidden + branch + out_bias
    mid_out, mid_normed, mid_inverse = norm_parts(residual, mid_gain, mid_shift)
    mid_low = mid_out.astype(jnp.bfloat16)
    pre_act = jnp.dot(mid_low, up_full, preferred_element_type=jnp.float32) + up_bias
    activated, gate_pull = jax.vjp(smooth_gate, pre_act)
    act_low = activated.astype(jnp.bfloat16)
    feed = lax.psum(
        jnp.dot(act_low, down_full, preferred_element_type=jnp.float32).astype(jnp.bfloat16), "mp"
    ).astype(jnp.float32)
    hidden_out = (residual + feed + down_bias).astype(jnp.bfloat16)
    grad_out = cotangent[0].astype(jnp.float32)
    grad_down = cotangent[0]
    down_grad = jnp.einsum("tf,td->fd", act_low, grad_down, preferred_element_type=jnp.float32)
    grad_act = jnp.einsum("td,fd->tf", grad_down, down_full, preferred_element_type=jnp.float32)
    grad_pre = gate_pull(grad_act)[0].astype(jnp.bfloat16)
    up_grad = jnp.einsum("td,tf->df", mid_low, grad_pre, preferred_element_type=jnp.float32)
    grad_mid = lax.psum(
        jnp.einsum("tf,df->td", grad_pre, up_full, preferred_element_type=jnp.float32), "mp"
    )
    grad_residual, mid_gain_grad, mid_shift_grad = norm_back(
        grad_mid, mid_normed, mid_inverse, mid_gain
    )
    grad_residual = grad_residual + grad_out
    grad_branch = grad_residual.astype(jnp.bfloat16)
    out_grad = jnp.einsum("tc,td->cd", attended, grad_branch, preferred_element_type=jnp.float32)
    grad_attended = jnp.einsum(
        "td,cd->tc", grad_branch, out_full, preferred_element_type=jnp.float32
    ).astype(jnp.bfloat16)
    grad_heads = grad_attended.reshape(local_rows, local_heads, HDIM)

    def delta_step(total, pieces):
        key_block, value_block, block_index = pieces
        permitted = block_mask(block_index)

        def delta_update(running):
            attn_probs = block_probs(key_block, permitted)
            grad_probs = jnp.einsum(
                "qhd,khd->hqk", grad_heads, value_block, preferred_element_type=jnp.float32
            )
            return running + jnp.sum(attn_probs * grad_probs, axis=-1)

        return (lax.cond(jnp.any(permitted), delta_update, lambda running: running, total), None)

    delta, _ = lax.scan(
        delta_step,
        jnp.zeros((local_heads, local_rows), jnp.float32),
        (key_blocks, value_blocks, block_ids),
    )

    def grad_step(total, pieces):
        key_block, value_block, block_index = pieces
        permitted = block_mask(block_index)

        def grad_update(running):
            attn_probs = block_probs(key_block, permitted)
            grad_probs = jnp.einsum(
                "qhd,khd->hqk", grad_heads, value_block, preferred_element_type=jnp.float32
            )
            grad_raw = (attn_probs * (grad_probs - delta[..., None]) * scale).astype(jnp.bfloat16)
            running = running + jnp.einsum(
                "hqk,khd->qhd", grad_raw, key_block, preferred_element_type=jnp.float32
            )
            key_part = jnp.einsum(
                "hqk,qhd->khd", grad_raw, query_heads, preferred_element_type=jnp.float32
            )
            value_part = jnp.einsum(
                "hqk,qhd->khd",
                attn_probs.astype(jnp.bfloat16),
                grad_heads,
                preferred_element_type=jnp.float32,
            )
            return (running, key_part, value_part)

        def passing(running):
            empty = jnp.zeros((block_rows, local_heads, HDIM), jnp.float32)
            return (running, empty, empty)

        running, key_part, value_part = lax.cond(jnp.any(permitted), grad_update, passing, total)
        return (running, (key_part, value_part))

    grad_queries, (key_parts, value_parts) = lax.scan(
        grad_step,
        jnp.zeros((local_rows, local_heads, HDIM), jnp.float32),
        (key_blocks, value_blocks, block_ids),
    )
    grad_keys, grad_values = (
        lax.psum_scatter(
            key_parts.reshape(TOKENS, width).astype(jnp.bfloat16),
            "seq",
            scatter_dimension=0,
            tiled=True,
        ).astype(jnp.float32),
        lax.psum_scatter(
            value_parts.reshape(TOKENS, width).astype(jnp.bfloat16),
            "seq",
            scatter_dimension=0,
            tiled=True,
        ).astype(jnp.float32),
    )
    grad_projected = jnp.stack(
        [grad_queries.reshape(local_rows, width), grad_keys, grad_values], axis=1
    ).astype(jnp.bfloat16)
    qkv_grad = jnp.einsum("td,tjc->djc", normed, grad_projected, preferred_element_type=jnp.float32)
    qv_bias_grad = jnp.sum(grad_projected[:, 0::2].astype(jnp.float32), axis=0)
    grad_normed = lax.psum(
        jnp.einsum("tjc,djc->td", grad_projected, qkv_full, preferred_element_type=jnp.float32),
        "mp",
    )
    grad_input, pre_gain_grad, pre_shift_grad = norm_back(
        grad_normed, pre_normed, pre_inverse, pre_gain
    )
    grad_input = grad_input + grad_residual
    summed = (
        lax.psum_scatter(qkv_grad, ("item", "seq"), scatter_dimension=0, tiled=True),
        lax.psum_scatter(up_grad, ("item", "seq"), scatter_dimension=0, tiled=True),
        lax.psum_scatter(out_grad, ("item", "seq"), scatter_dimension=1, tiled=True),
        lax.psum_scatter(down_grad, ("item", "seq"), scatter_dimension=1, tiled=True),
    )
    small = lax.psum(
        (
            pre_gain_grad,
            pre_shift_grad,
            qv_bias_grad,
            jnp.sum(grad_residual, axis=0),
            mid_gain_grad,
            mid_shift_grad,
            jnp.sum(grad_pre.astype(jnp.float32), axis=0),
            jnp.sum(grad_out, axis=0),
        ),
        ("item", "seq"),
    )
    return (
        hidden_out[None],
        grad_input[None],
        small[0],
        small[1],
        summed[0],
        small[2],
        summed[2],
        small[3],
        small[4],
        small[5],
        summed[1],
        small[6],
        summed[3],
        small[7],
    )


def solution(mesh):
    return jax.shard_map(
        body,
        mesh=mesh,
        in_specs=(
            P("item", "seq", None),
            P("item", "seq", None),
            P("item", None),
            P(),
            P(),
            P(("item", "seq"), None, "mp"),
            P(None, "mp"),
            P("mp", ("item", "seq")),
            P(),
            P(),
            P(),
            P(("item", "seq"), "mp"),
            P("mp"),
            P("mp", ("item", "seq")),
            P(),
        ),
        out_specs=(
            P("item", "seq", None),
            P("item", "seq", None),
            P(),
            P(),
            P(("item", "seq"), None, "mp"),
            P(None, "mp"),
            P("mp", ("item", "seq")),
            P(),
            P(),
            P(),
            P(("item", "seq"), "mp"),
            P("mp"),
            P("mp", ("item", "seq")),
            P(),
        ),
        check_vma=False,
    )
```

profile of v0, /device:TPU:0, one launch (start us, length us, event | category | flops | bytes accessed | tf_op | source)
XLA Modules:
  0.0 2566.3 jit_solution(10367387097974228224)
XLA Ops:
  16.9 43.0 %all-gather.8.cloned.1.call-done = bf16[2048,3,512]{0,2,1:T(8,128)(2,1)} async-done(((bf16[256,3,512]{0,2,1:T(8,128)(2,1)}), bf16[2048,3,512]{0,2,1:T(8,128)(2,1)}) %all-gather.8.cloned.1.call-update) | async-done | bytes 6291472 | tf_op jit(solution)/shard_map/all_gather | solution.py:76
  59.9 12.4 fusion.152
  83.0 32.9 %all-gather.18.cloned.1.call-done = bf16[2560,1,512]{0,2,1:T(8,128)(2,1)} async-done(((bf16[1280,1,512]{0,2,1:T(8,128)(2,1)}), bf16[2560,1,512]{0,2,1:T(8,128)(2,1)}) %all-gather.18.cloned.1.call-update) | async-done | bytes 2621456 | tf_op jit(solution)/shard_map/all_gather | solution.py:98
  128.1 35.3 %while.71 = (s32[]{:T(128)}, f32[8,1280]{1,0:T(8,128)S(1)}, f32[8,1280]{1,0:T(8,128)S(1)}, s32[5]{0:T(128)S(1)}, s32[1,2]{1,0:T(1,128)S(1)}, /*index=5*/bf16[5,5...) while((s32[]{:T(128)}, f32[8,1280]{1,0:T(8,128)S(1)}, ...), condition=%wide.region_9.10_spmd.clone.clone, body=%wide.region_2.9_spmd.clone.clone.sunk | while | flops 702597888 | bytes 45658864 | solution.py:136
  176.8 41.3 %while.72 = (s32[]{:T(128)}, f32[1280,8,64]{0,2,1:T(8,128)}, s32[5]{0:T(128)S(1)}, s32[1,2]{1,0:T(1,128)S(1)}, bf16[5,512,8,64]{1,3,2,0:T(8,128)(2,1)}, /*index=...) while((s32[]{:T(128)}, f32[1280,8,64]{0,2,1:T(8,128)}, ...), condition=%wide.region_15.16_spmd.clone.clone, body=%wide.region_10.15_spmd.clone.clone.sunk | while | flops 1369078528 | bytes 8991967 | solution.py:154
  181.3 10.5 conditional.17
  181.3 10.5 fusion.28
  195.7 10.5 conditional.17
  195.7 10.5 fusion.28
  230.9 393.3 %all-reduce.6.cloned.1.call-done = f32[1280,2048]{1,0:T(8,128)} async-done(((f32[1280,2048]{1,0:T(8,128)}), f32[1280,2048]{1,0:T(8,128)}) %all-reduce.6.cloned.1.call-update) | async-done | bytes 10485776 | tf_op jit(solution)/shard_map/psum | solution.py:160
  624.1 11.2 fusion.161
  640.5 38.8 %all-gather.14.cloned.1.call-done = bf16[2048,2048]{1,0:T(8,128)(2,1)} async-done(((bf16[256,2048]{1,0:T(8,128)(2,1)}), bf16[2048,2048]{1,0:T(8,128)(2,1)}) %all-gather.14.cloned.1.call-update) | async-done | bytes 8388624 | tf_op jit(solution)/shard_map/all_gather | solution.py:77
  679.3 19.0 fusion.155
  698.3 38.9 %all-gather.16.cloned.1.call-done = bf16[2048,2048]{1,0:T(8,128)(2,1)} async-done(((bf16[2048,256]{1,0:T(8,128)(2,1)}), bf16[2048,2048]{1,0:T(8,128)(2,1)}) %all-gather.16.cloned.1.call-update) | async-done | bytes 8388624 | tf_op jit(solution)/shard_map/all_gather | solution.py:79
  737.1 25.5 convert_reduce_fusion.2
  762.6 14.8 fusion.166
  777.5 18.8 convolution_convert_fusion
  796.4 339.7 %all-reduce.10.cloned.1.call-done = f32[1280,2048]{1,0:T(8,128)} async-done(((f32[1280,2048]{1,0:T(8,128)}), f32[1280,2048]{1,0:T(8,128)}) %all-reduce.10.cloned.1.call-update) | async-done | bytes 10485776 | tf_op jit(solution)/shard_map/psum | solution.py:177
  1136.0 11.0 multiply_reduce_fusion
  1147.1 179.9 %all-reduce.8.cloned.1.call-done = bf16[1280,2048]{1,0:T(8,128)(2,1)} async-done(((bf16[1280,2048]{1,0:T(8,128)(2,1)}), bf16[1280,2048]{1,0:T(8,128)(2,1)}) %all-reduce.8.cloned.1.call-update) | async-done | bytes 5242896 | tf_op jit(solution)/shard_map/psum | solution.py:167
  1327.0 16.3 fusion.160
  1347.8 64.5 %while.73 = (s32[]{:T(128)}, f32[8,1280]{1,0:T(8,128)S(1)}, s32[5]{0:T(128)S(1)}, s32[1,2]{1,0:T(1,128)S(1)}, bf16[5,512,8,64]{1,3,2,0:T(8,128)(2,1)}, /*index=5...) while((s32[]{:T(128)}, f32[8,1280]{1,0:T(8,128)S(1)}, ...), condition=%wide.region_29.30_spmd.clone.clone, body=%wide.region_23.29_spmd.clone.clone.sunk | while | flops 1373666048 | bytes 47166704 | solution.py:204
  1351.7 22.3 conditional.18
  1351.8 11.4 fusion.42
  1363.1 10.9 fusion.39
  1378.0 22.3 conditional.18
  1378.0 11.4 fusion.42
  1389.4 10.9 fusion.39
  1412.5 144.1 %while.74 = (s32[]{:T(128)}, f32[1280,8,64]{0,2,1:T(8,128)S(1)}, bf16[5,512,8,64]{1,3,2,0:T(8,128)(2,1)}, bf16[5,512,8,64]{1,3,2,0:T(8,128)(2,1)}, s32[5]{0:T(12...) while((s32[]{:T(128)}, f32[1280,8,64]{0,2,1:T(8,128)S(1)}, ...), condition=%wide.region_35.36_spmd.clone.clone, body=%wide.region_30.35_spmd.clone.clone.sunk | while | flops 3403315968 | bytes 163437488 | solution.py:241
  1417.4 52.1 %conditional.19 = (f32[1280,8,64]{0,2,1:T(8,128)S(1)}, bf16[1,512,8,64]{1,3,2,0:T(8,128)(2,1)S(1)}, bf16[1,512,8,64]{1,3,2,0:T(8,128)(2,1)}) conditional(s32[]{:T(128)} %convert_element_type.237, f32[1280,8,64]{0,2,1:T(8,128)S(1)} %get-tuple-element.1777, (pred[1280,512]{0,1:T(8,128)(4,1)}, bf16[5,512,8,64]{1,3,2,0:T(8,128)(2,1)}, s32[]{:T(128)}, ...), branch_computations={%region_33.33_spmd, %region_34.34_spmd} | conditional | flops 3398041600 | bytes 160646816 | solution.py:238
  1417.4 14.6 fusion.52
  1432.0 14.4 fusion.50
  1459.4 10.0 fusion.56
  1476.9 52.1 %conditional.19 = (f32[1280,8,64]{0,2,1:T(8,128)S(1)}, bf16[1,512,8,64]{1,3,2,0:T(8,128)(2,1)S(1)}, bf16[1,512,8,64]{1,3,2,0:T(8,128)(2,1)}) conditional(s32[]{:T(128)} %convert_element_type.237, f32[1280,8,64]{0,2,1:T(8,128)S(1)} %get-tuple-element.1777, (pred[1280,512]{0,1:T(8,128)(4,1)}, bf16[5,512,8,64]{1,3,2,0:T(8,128)(2,1)}, s32[]{:T(128)}, ...), branch_computations={%region_33.33_spmd, %region_34.34_spmd} | conditional | flops 3398041600 | bytes 160646816 | solution.py:238
  1476.9 14.6 fusion.52
  1491.5 14.4 fusion.50
  1589.4 165.9 %reduce-scatter.7.cloned.1.call-done = bf16[1280,512]{1,0:T(8,128)(2,1)} async-done(((bf16[2560,512]{1,0:T(8,128)(2,1)}), bf16[1280,512]{1,0:T(8,128)(2,1)}) %reduce-scatter.7.cloned.1.call-update) | async-done | bytes 1310736 | tf_op jit(solution)/shard_map/reduce_scatter | solution.py:247
  1755.3 40.0 %reduce-scatter.9.cloned.1.call-done = bf16[1280,512]{1,0:T(8,128)(2,1)} async-done(((bf16[2560,512]{1,0:T(8,128)(2,1)}), bf16[1280,512]{1,0:T(8,128)(2,1)}) %reduce-scatter.9.cloned.1.call-update) | async-done | bytes 1310736 | tf_op jit(solution)/shard_map/reduce_scatter | solution.py:253
  1795.3 13.4 convolution_bitcast_fusion.2
  1818.5 19.6 fusion.154
  1838.8 20.6 fusion.139
  1860.8 14.0 fusion.150
  1876.8 290.5 %all-reduce.12.cloned.1.call-done = f32[1280,2048]{1,0:T(8,128)} async-done(((f32[1280,2048]{1,0:T(8,128)}), f32[1280,2048]{1,0:T(8,128)}) %all-reduce.12.cloned.1.call-update) | async-done | bytes 10485776 | tf_op jit(solution)/shard_map/psum | solution.py:265
  2175.5 26.0 %all-reduce = (f32[2048]{0:T(1024)}, f32[2048]{0:T(1024)}, f32[2,512]{1,0:T(2,128)}, f32[2048]{0:T(1024)}, f32[2048]{0:T(1024)}, /*index=5*/f32[2048]{0:T(1024)}, f32[2048]{0:T(1024)}, f32[2048]{0:T(1024)}) all-reduce(f32[2048]{0:T(1024)S(1)} %get-tuple-element.1194, ...), channel_id=1, replica_groups=mesh['item'=4,'seq'=2,'mp'=4] {'item','seq'}, use_global_device_ids=true, to_apply=%region_42.43 | all-reduce | flops 15360 | bytes 122880 | tf_op jit(solution)/shard_map/psum | solution.py:279
  2201.5 14.4 fusion.126
  2222.0 120.4 %reduce-scatter.15.cloned.1.call-done = f32[256,2048]{1,0:T(8,128)} async-done(((f32[2048,2048]{1,0:T(8,128)}), f32[256,2048]{1,0:T(8,128)}) %reduce-scatter.15.cloned.1.call-update) | async-done | bytes 2097168 | tf_op jit(solution)/shard_map/reduce_scatter | solution.py:275
  2342.4 120.4 %reduce-scatter.17.cloned.1.call-done = f32[2048,256]{1,0:T(8,128)} async-done(((f32[2048,2048]{1,0:T(8,128)}), f32[2048,256]{1,0:T(8,128)}) %reduce-scatter.17.cloned.1.call-update) | async-done | bytes 2097168 | tf_op jit(solution)/shard_map/reduce_scatter | solution.py:277
  2462.8 96.8 %reduce-scatter.11.cloned.1.call-done = f32[256,3,512]{2,0,1:T(8,128)} async-done(((f32[2048,3,512]{2,0,1:T(8,128)}), f32[256,3,512]{2,0,1:T(8,128)}) %reduce-scatter.11.cloned.1.call-update) | async-done | bytes 1572880 | tf_op jit(solution)/shard_map/reduce_scatter | solution.py:274
  (350 shorter events, 271.1 us)
Async XLA Ops:
  7.2 52.7 %copy-start.24 = (f32[2048]{0:T(1024)S(1)}, f32[2048]{0:T(1024)}, u32[]{:S(2)}) copy-start(f32[2048]{0:T(1024)} %param.34) | copy-start | bytes 24580
  7.2 52.7 %copy-start.40 = (f32[2048]{0:T(1024)S(1)}, f32[2048]{0:T(1024)}, u32[]{:S(2)}) copy-start(f32[2048]{0:T(1024)} %param.35) | copy-start | bytes 24580
  7.2 52.7 %all-gather.8.cloned.1.call-start = ((), (), s32[]{:S(2)}) async-start(), calls=%async_computation.6 | async-start | bytes 7077888 | tf_op jit(solution)/shard_map/all_gather | solution.py:76
  9.6 106.3 %all-gather.18.cloned.1.call-start = ((), (), s32[]{:S(2)}) async-start(), calls=%async_computation.21 | async-start | bytes 3932160 | tf_op jit(solution)/shard_map/all_gather | solution.py:98
  12.9 59.4 %copy-start.12 = (f32[1280]{0:T(1024)}, f32[1280]{0:T(1024)S(1)}, u32[]{:S(2)}) copy-start(f32[1280]{0:T(1024)S(1)} %broadcast_multiply_fusion.5) | copy-start | bytes 15364
  16.9 55.4 %copy-start.16 = (f32[1280]{0:T(1024)}, f32[1280]{0:T(1024)S(1)}, u32[]{:S(2)}) copy-start(f32[1280]{0:T(1024)S(1)} %add_rsqrt_fusion.1) | copy-start | bytes 15364
  16.9 59.9 %copy-start.33 = (f32[2,512]{1,0:T(2,128)S(1)}, f32[2,512]{1,0:T(2,128)}, u32[]{:S(2)}) copy-start(f32[2,512]{1,0:T(2,128)} %param.37) | copy-start | bytes 12292
  76.7 86.6 %all-gather.10.cloned.1.call-start = ((), (), s32[]{:S(2)}) async-start(), calls=%async_computation.7 | async-start | bytes 3932160 | tf_op jit(solution)/shard_map/all_gather | solution.py:99
  79.8 141.9 %all-gather.12.cloned.1.call-start = ((), (), s32[]{:S(2)}) async-start(), calls=%async_computation.8 | async-start | bytes 2359296 | tf_op jit(solution)/shard_map/all_gather | solution.py:78
  80.4 543.7 %all-reduce.6.cloned.1.call-start = ((), (), s32[]{:S(2)}) async-start(), calls=%async_computation.9 | async-start | bytes 20971520 | tf_op jit(solution)/shard_map/psum | solution.py:160
  80.8 47.2 %copy-start.9 = (s32[1,2]{1,0:T(1,128)S(1)}, s32[1,2]{1,0:T(1,128)}, u32[]{:S(2)}) copy-start(s32[1,2]{1,0:T(1,128)} %param.33) | copy-start | bytes 28
  219.4 10.1 copy-start.2
  229.4 394.7 %copy-start.30 = (f32[2048]{0:T(1024)S(1)}, f32[2048]{0:T(1024)}, u32[]{:S(2)}) copy-start(f32[2048]{0:T(1024)} %param.39) | copy-start | bytes 24580
  229.5 449.8 %all-gather.14.cloned.1.call-start = ((), (), s32[]{:S(2)}) async-start(), calls=%async_computation.10 | async-start | bytes 9437184 | tf_op jit(solution)/shard_map/all_gather | solution.py:77
  230.1 507.1 %all-gather.16.cloned.1.call-start = ((), (), s32[]{:S(2)}) async-start(), calls=%async_computation.11 | async-start | bytes 9437184 | tf_op jit(solution)/shard_map/all_gather | solution.py:79
  230.8 905.2 %all-reduce.10.cloned.1.call-start = ((), (), s32[]{:S(2)}) async-start(), calls=%async_computation.13 | async-start | bytes 20971520 | tf_op jit(solution)/shard_map/psum | solution.py:177
  635.3 44.0 %copy-start.22 = (f32[2048]{0:T(1024)S(1)}, f32[2048]{0:T(1024)}, u32[]{:S(2)}) copy-start(f32[2048]{0:T(1024)} %param.40) | copy-start | bytes 24580
  635.3 44.0 %copy-start.36 = (f32[2048]{0:T(1024)S(1)}, f32[2048]{0:T(1024)}, u32[]{:S(2)}) copy-start(f32[2048]{0:T(1024)} %param.41) | copy-start | bytes 24580
  635.3 691.6 %copy-start.14 = (f32[1280]{0:T(1024)}, f32[1280]{0:T(1024)S(1)}, u32[]{:S(2)}) copy-start(f32[1280]{0:T(1024)S(1)} %broadcast_multiply_fusion.4) | copy-start | bytes 15364
  640.5 686.5 %copy-start.18 = (f32[1280]{0:T(1024)}, f32[1280]{0:T(1024)S(1)}, u32[]{:S(2)}) copy-start(f32[1280]{0:T(1024)S(1)} %add_rsqrt_fusion) | copy-start | bytes 15364
  640.5 96.6 %copy-start.38 = (f32[2048]{0:T(1024)S(1)}, f32[2048]{0:T(1024)}, u32[]{:S(2)}) copy-start(f32[2048]{0:T(1024)} %param.43) | copy-start | bytes 24580
  737.1 25.5 copy-start.34
  777.4 549.5 %all-reduce.8.cloned.1.call-start = ((), (), s32[]{:S(2)}) async-start(), calls=%async_computation.12 | async-start | bytes 10485760 | tf_op jit(solution)/shard_map/psum | solution.py:167
  796.3 959.0 %reduce-scatter.7.cloned.1.call-start = ((), (), s32[]{:S(2)}) async-start(), calls=%async_computation.14 | async-start | bytes 3932160 | tf_op jit(solution)/shard_map/reduce_scatter | solution.py:247
  796.4 530.6 %copy-start.31 = (f32[2048]{0:T(1024)S(1)}, f32[2048]{0:T(1024)}, u32[]{:S(2)}) copy-start(f32[2048]{0:T(1024)} %param.45) | copy-start | bytes 24580
  1326.9 16.3 copy-start.35
  1417.4 14.6 copy-start
  1446.4 8.4 slice-start.2
  1459.4 10.0 copy-start.1
  1476.9 14.6 copy-start
  1505.9 8.4 slice-start.1
  1505.9 8.4 slice-start.2
  1518.9 10.0 copy-start.1
  1571.6 223.7 %reduce-scatter.9.cloned.1.call-start = ((), (), s32[]{:S(2)}) async-start(), calls=%async_computation.15 | async-start | bytes 3932160 | tf_op jit(solution)/shard_map/reduce_scatter | solution.py:253
  1586.5 580.8 %all-reduce.12.cloned.1.call-start = ((), (), s32[]{:S(2)}) async-start(), calls=%async_computation.16 | async-start | bytes 20971520 | tf_op jit(solution)/shard_map/psum | solution.py:265
  1808.7 9.8 copy-start.15
  1808.7 9.8 copy-start.19
  1808.7 9.8 copy-start.23
  1808.8 9.8 copy-start.37
  1808.8 413.2 %reduce-scatter.13.cloned.1.call-start = ((), (), s32[]{:S(2)}) async-start(), calls=%async_computation.18 | async-start | bytes 4718592 | tf_op jit(solution)/shard_map/reduce_scatter | solution.py:276
  1818.4 524.0 %reduce-scatter.15.cloned.1.call-start = ((), (), s32[]{:S(2)}) async-start(), calls=%async_computation.19 | async-start | bytes 18874368 | tf_op jit(solution)/shard_map/reduce_scatter | solution.py:275
  1838.1 624.7 %reduce-scatter.17.cloned.1.call-start = ((), (), s32[]{:S(2)}) async-start(), calls=%async_computation.20 | async-start | bytes 18874368 | tf_op jit(solution)/shard_map/reduce_scatter | solution.py:277
  1859.5 700.1 %reduce-scatter.11.cloned.1.call-start = ((), (), s32[]{:S(2)}) async-start(), calls=%async_computation.17 | async-start | bytes 14155776 | tf_op jit(solution)/shard_map/reduce_scatter | solution.py:274
  1876.3 299.1 %copy-start.26 = (f32[2048]{0:T(1024)S(1)}, f32[2048]{0:T(1024)}, u32[]{:S(2)}) copy-start(f32[2048]{0:T(1024)} %get-tuple-element.1192) | copy-start | bytes 24580
  1876.4 299.1 %copy-start.27 = (f32[2048]{0:T(1024)S(1)}, f32[2048]{0:T(1024)}, u32[]{:S(2)}) copy-start(f32[2048]{0:T(1024)} %get-tuple-element.1198) | copy-start | bytes 24580
  1876.4 299.1 %copy-start.28 = (f32[2048]{0:T(1024)S(1)}, f32[2048]{0:T(1024)}, u32[]{:S(2)}) copy-start(f32[2048]{0:T(1024)} %get-tuple-element.1296) | copy-start | bytes 24580
  1876.4 299.1 %copy-start.29 = (f32[2048]{0:T(1024)S(1)}, f32[2048]{0:T(1024)}, u32[]{:S(2)}) copy-start(f32[2048]{0:T(1024)} %get-tuple-element.1327) | copy-start | bytes 24580
  1876.4 299.1 %copy-start.32 = (f32[2048]{0:T(1024)S(1)}, f32[2048]{0:T(1024)}, u32[]{:S(2)}) copy-start(f32[2048]{0:T(1024)} %get-tuple-element.1330) | copy-start | bytes 24580
  (18 other events, 64.2 us)
Sparse Core Ops, SparseCore 0:
  10.5 49.3 all-gather.7
  76.8 39.0 all-gather.17
  118.0 39.0 all-gather.9
  158.8 28.2 all-gather.11
  229.6 394.4 all-reduce.5
  625.9 53.3 all-gather.13
  681.1 55.9 all-gather.15
  777.5 358.4 all-reduce.9
  1139.0 187.9 all-reduce.7
  1571.7 183.5 reduce-scatter.6
  1757.6 37.5 reduce-scatter.8
  1808.8 358.4 all-reduce.11
  2171.2 50.6 reduce-scatter.12
  2226.4 115.9 reduce-scatter.14
  2346.8 115.9 reduce-scatter.16
  2467.2 92.3 reduce-scatter.10
where the time goes:
time: 2570 us
  waiting for transfers between devices  1910 us (74%)
  matrix products  358 us (14%)
  other arithmetic  132 us (5%)
  local copies, waits for them, and re-layouts  98.3 us (4%)
  loops' own time  28 us (1%)
  blocking collectives  26 us (1%)
    psum x1, waiting for transfers between devices, body(): lax.psum(jnp.dot(attended, out_full, preferred_element_type=jnp.float32),...  393 us
    psum x1, waiting for transfers between devices, body(): lax.psum(jnp.einsum('tf,df->td', grad_pre, up_full, preferred_element_typ...  340 us
    psum x1, waiting for transfers between devices, body(): lax.psum(jnp.einsum('tjc,djc->td', grad_projected, qkv_full, preferred_el...  290 us
    psum x1, waiting for transfers between devices, body(): lax.psum(jnp.dot(act_low, down_full, preferred_element_type=jnp.float32)....  180 us
    reduce_scatter x1, waiting for transfers between devices, body(): lax.psum_scatter(key_parts.reshape(TOKENS, width).astype(jnp.bfloat16), '...  166 us
    reduce_scatter x1, waiting for transfers between devices, body(): lax.psum_scatter(up_grad, ('item', 'seq'), scatter_dimension=0, tiled=True)  120 us
    reduce_scatter x1, waiting for transfers between devices, body(): lax.psum_scatter(down_grad, ('item', 'seq'), scatter_dimension=1, tiled=T...  120 us
    reduce_scatter x1, waiting for transfers between devices, body(): lax.psum_scatter(qkv_grad, ('item', 'seq'), scatter_dimension=0, tiled=True)  96.8 us
  transfers between devices with their start and end apart: 16, of which 14 were waited for; matrix products, arithmetic and copies ran while one was open for 11% of the time, Pallas kernels for 0%

commit v1 on v0

v1 whole, which is shorter than its diff:
```python
import functools
import math

import jax
import jax.numpy as jnp
from jax import lax
from jax.experimental import pallas as pl
from jax.experimental.pallas import tpu as pltpu
from jax.sharding import PartitionSpec as P

HDIM = 64
SLOT = 1280
SEGS = 2
SUMM = 50
SUMM_ROWS = 64
TOKENS = 2560
PAIR = 2 * HDIM
PIECE = 32
MIB = 1 << 20
MESH = pl.DeviceIdType.MESH
MASKED = -1e30


eps = 1e-05

NN = (((1,), (0,)), ((), ()))
NT = (((1,), (1,)), ((), ()))


def mm(left, right, dims=NN):
    return lax.dot_general(left, right, dims, preferred_element_type=jnp.float32)


def norm_stats(values):
    center = jnp.mean(values, axis=-1, keepdims=True)
    centered = values - center
    inverse = lax.rsqrt(jnp.mean(centered * centered, axis=-1, keepdims=True) + eps)
    return centered * inverse, inverse


def norm_back(grad_out, normed, inverse, gain):
    scaled = grad_out * gain
    centered = scaled - jnp.mean(scaled, axis=-1, keepdims=True)
    return inverse * (centered - normed * jnp.mean(scaled * normed, axis=-1, keepdims=True))


def gelu_parts(values):
    c = math.sqrt(2 / math.pi)
    squared = values * values
    t = jnp.tanh(c * values * (1 + 0.044715 * squared))
    half = 0.5 * (1 + t)
    slope = half + 0.5 * values * (1 - t * t) * (c * (1 + 3 * 0.044715 * squared))
    return values * half, slope


def key_masks(facts_ref, block, rows, bq, nk):
    first = facts_ref[0] + block * bq
    limit = jnp.minimum(
        first + 1 + lax.broadcasted_iota(jnp.int32, (1, bq), 1), facts_ref[1]
    )
    own = lax.broadcasted_iota(jnp.int32, (nk, bq), 0) < limit
    earlier = lax.broadcasted_iota(jnp.int32, (SUMM_ROWS, bq), 0) < facts_ref[2]
    return own, earlier


def head_lanes(head):
    lane = lax.broadcasted_iota(jnp.int32, (1, PAIR), 1)
    return (lane >= head * HDIM) & (lane < (head + 1) * HDIM)


def attend_kernel(bq, causal, facts_ref, q_ref, k_ref, v_ref, ks_ref, vs_ref, o_ref, lse_ref):
    rows, seg = q_ref.shape[0], k_ref.shape[0]
    v_t = v_ref[...].T
    vs_t = vs_ref[...].T
    ks = ks_ref[...]
    low_half = lax.broadcasted_iota(jnp.int32, (PAIR, 1), 0) < HDIM
    for block in range(rows // bq):
        nk = (block + 1) * bq if causal else seg
        own, earlier = key_masks(facts_ref, block, rows, bq, nk)
        q = q_ref[block * bq : (block + 1) * bq, :] * jnp.bfloat16(HDIM**-0.5)
        mixed = []
        for head in range(2):
            qh = jnp.where(head_lanes(head), q, jnp.zeros_like(q))
            s = jnp.where(own, mm(k_ref[:nk, :], qh, NT), MASKED)
            s2 = jnp.where(earlier, mm(ks, qh, NT), MASKED)
            top = jnp.maximum(jnp.max(s, axis=0, keepdims=True), jnp.max(s2, axis=0, keepdims=True))
            p = jnp.exp(s - top)
            p2 = jnp.exp(s2 - top)
            total = jnp.sum(p, axis=0, keepdims=True) + jnp.sum(p2, axis=0, keepdims=True)
            out = mm(v_t[:, :nk], p.astype(jnp.bfloat16)) + mm(vs_t, p2.astype(jnp.bfloat16))
            mixed.append(out / total)
            lse_ref[0, head : head + 1, block * bq : (block + 1) * bq] = top + jnp.log(total)
        joined = jnp.where(low_half, mixed[0], mixed[1])
        o_ref[block * bq : (block + 1) * bq, :] = joined.T.astype(jnp.bfloat16)


def attend_back_kernel(
    bq,
    causal,
    facts_ref,
    q_ref,
    k_ref,
    v_ref,
    ks_ref,
    vs_ref,
    do_ref,
    lse_ref,
    dq_ref,
    dk_ref,
    dv_ref,
    dks_ref,
    dvs_ref,
    dk_acc,
    dv_acc,
):
    rows, seg = q_ref.shape[0], k_ref.shape[0]
    scale = jnp.bfloat16(HDIM**-0.5)
    k_t = (k_ref[...] * scale).T
    ks_t = (ks_ref[...] * scale).T
    ks = ks_ref[...]
    vs = vs_ref[...]
    low_half = lax.broadcasted_iota(jnp.int32, (PAIR, 1), 0) < HDIM
    dk_acc[...] = jnp.zeros_like(dk_acc)
    dv_acc[...] = jnp.zeros_like(dv_acc)
    dks = jnp.zeros((SUMM_ROWS, PAIR), jnp.float32)
    dvs = jnp.zeros((SUMM_ROWS, PAIR), jnp.float32)
    for block in range(rows // bq):
        nk = (block + 1) * bq if causal else seg
        own, earlier = key_masks(facts_ref, block, rows, bq, nk)
        q = q_ref[block * bq : (block + 1) * bq, :] * scale
        do = do_ref[block * bq : (block + 1) * bq, :]
        grads = []
        for head in range(2):
            qh = jnp.where(head_lanes(head), q, jnp.zeros_like(q))
            doh = jnp.where(head_lanes(head), do, jnp.zeros_like(do))
            lse = lse_ref[0, head : head + 1, block * bq : (block + 1) * bq]
            p = jnp.exp(jnp.where(own, mm(k_ref[:nk, :], qh, NT), MASKED) - lse)
            p2 = jnp.exp(jnp.where(earlier, mm(ks, qh, NT), MASKED) - lse)
            dp = mm(v_ref[:nk, :], doh, NT)
            dp2 = mm(vs, doh, NT)
            delta = jnp.sum(p * dp, axis=0, keepdims=True) + jnp.sum(p2 * dp2, axis=0, keepdims=True)
            ds = (p * (dp - delta)).astype(jnp.bfloat16)
            ds2 = (p2 * (dp2 - delta)).astype(jnp.bfloat16)
            dv_acc[:nk, :] += mm(p.astype(jnp.bfloat16), doh)
            dk_acc[:nk, :] += mm(ds, qh)
            dvs = dvs + mm(p2.astype(jnp.bfloat16), doh)
            dks = dks + mm(ds2, qh)
            grads.append(mm(k_t[:, :nk], ds) + mm(ks_t, ds2))
        joined = jnp.where(low_half, grads[0], grads[1])
        dq_ref[block * bq : (block + 1) * bq, :] = joined.T.astype(jnp.bfloat16)
    dk_ref[...] = dk_acc[...].astype(jnp.bfloat16)
    dv_ref[...] = dv_acc[...].astype(jnp.bfloat16)
    dks_ref[...] = dks
    dvs_ref[...] = dvs


def query_block(rows):
    return 256 if rows % 256 == 0 else math.gcd(rows, 160)


def attend(facts, q, k, v, ks, vs):
    rows, width = q.shape
    seg = k.shape[0]
    pairs = width // PAIR
    column = lambda n: pl.BlockSpec((n, PAIR), lambda i: (0, i))
    return pl.pallas_call(
        functools.partial(attend_kernel, query_block(rows), rows == seg),
        grid=(pairs,),
        in_specs=[pl.BlockSpec(memory_space=pltpu.SMEM)]
        + [column(n) for n in (rows, seg, seg, SUMM_ROWS, SUMM_ROWS)],
        out_specs=[column(rows), pl.BlockSpec((1, 2, rows), lambda i: (i, 0, 0))],
        out_shape=[
            jax.ShapeDtypeStruct((rows, width), jnp.bfloat16),
            jax.ShapeDtypeStruct((pairs, 2, rows), jnp.float32),
        ],
        compiler_params=pltpu.CompilerParams(vmem_limit_bytes=48 * MIB),
        cost_estimate=pl.CostEstimate(
            flops=4 * rows * seg * width, bytes_accessed=8 * rows * width, transcendentals=0
        ),
        name="attend",
    )(facts, q, k, v, ks, vs)


def attend_back(facts, q, k, v, ks, vs, do, lse):
    rows, width = q.shape
    seg = k.shape[0]
    pairs = width // PAIR
    column = lambda n: pl.BlockSpec((n, PAIR), lambda i: (0, i))
    low = lambda n: jax.ShapeDtypeStruct((n, width), jnp.bfloat16)
    wide = lambda n: jax.ShapeDtypeStruct((n, width), jnp.float32)
    return pl.pallas_call(
        functools.partial(attend_back_kernel, query_block(rows), rows == seg),
        grid=(pairs,),
        in_specs=[pl.BlockSpec(memory_space=pltpu.SMEM)]
        + [column(n) for n in (rows, seg, seg, SUMM_ROWS, SUMM_ROWS, rows)]
        + [pl.BlockSpec((1, 2, rows), lambda i: (i, 0, 0))],
        out_specs=[column(n) for n in (rows, seg, seg, SUMM_ROWS, SUMM_ROWS)],
        out_shape=[low(rows), low(seg), low(seg), wide(SUMM_ROWS), wide(SUMM_ROWS)],
        scratch_shapes=[pltpu.VMEM((seg, PAIR), jnp.float32)] * 2,
        compiler_params=pltpu.CompilerParams(vmem_limit_bytes=48 * MIB),
        cost_estimate=pl.CostEstimate(
            flops=10 * rows * seg * width, bytes_accessed=16 * rows * width, transcendentals=0
        ),
        name="attend_back",
    )(facts, q, k, v, ks, vs, do, lse)


def keys_for(local, lengths, seq_count):
    rows, width = local.shape[-2:]
    pad = ((0, 0), (0, SUMM_ROWS - SUMM), (0, 0))
    if rows == SLOT:
        here = lengths[lax.axis_index("seq")]
        summary = jnp.pad(lax.dynamic_slice(local, (0, here, 0), (2, SUMM, width)), pad)
        moves = [(i, i + 1) for i in range(seq_count - 1)]
        return local, lax.ppermute(summary, "seq", moves)
    everything = lax.all_gather(local, "seq", axis=1, tiled=True)
    segment = lax.axis_index("seq") * rows // SLOT
    own = lax.dynamic_slice(everything, (0, segment * SLOT, 0), (2, SLOT, width))
    summary = lax.dynamic_slice(everything, (0, lengths[0], 0), (2, SUMM, width))
    return own, jnp.pad(summary, pad)


def keys_back(own, summary, rows, lengths, seq_count):
    width = own.shape[-1]
    summary = summary[:, :SUMM]
    if rows == SLOT:
        moves = [(i + 1, i) for i in range(seq_count - 1)]
        arrived = lax.ppermute(summary, "seq", moves)
        here = lengths[lax.axis_index("seq")]
        old = lax.dynamic_slice(own, (0, here, 0), (2, SUMM, width))
        new = (old.astype(jnp.float32) + arrived).astype(jnp.bfloat16)
        return lax.dynamic_update_slice(own, new, (0, here, 0))
    segment = lax.axis_index("seq") * rows // SLOT
    everything = jnp.zeros((2, TOKENS, width), jnp.float32)
    everything = lax.dynamic_update_slice(
        everything, own.astype(jnp.float32), (0, segment * SLOT, 0)
    )
    old = lax.dynamic_slice(everything, (0, lengths[0], 0), (2, SUMM, width))
    added = jnp.where(segment > 0, summary, 0.0)
    everything = lax.dynamic_update_slice(everything, old + added, (0, lengths[0], 0))
    return lax.psum_scatter(
        everything.astype(jnp.bfloat16), "seq", scatter_dimension=1, tiled=True
    )


def body(
    seq_count,
    mp_count,
    hidden_in,
    cotangent,
    seg_lengths,
    pre_gain,
    pre_shift,
    qkv_weight,
    qv_bias,
    out_weight,
    out_bias,
    mid_gain,
    mid_shift,
    up_weight,
    up_bias,
    down_weight,
    down_bias,
):
    group = ("item", "seq")
    width = qkv_weight.shape[2]
    gathered = lambda weight, axis: lax.all_gather(weight, group, axis=axis, tiled=True)
    qkv_full = gathered(qkv_weight.reshape(-1, 3 * width), 0)
    out_full = gathered(out_weight, 1)
    up_full = gathered(up_weight, 0)
    down_full = gathered(down_weight, 1)
    hidden = hidden_in[0].astype(jnp.float32)
    lengths = seg_lengths[0]
    rows = hidden.shape[0]
    first_row = lax.axis_index("seq") * rows
    segment = first_row // SLOT
    facts = jnp.stack(
        [
            first_row % SLOT,
            lengths[segment] + SUMM,
            jnp.where(segment > 0, SUMM, 0),
        ]
    ).astype(jnp.int32)

    pre_normed, pre_inverse = norm_stats(hidden)
    normed = (pre_normed * pre_gain + pre_shift).astype(jnp.bfloat16)
    q = (mm(normed, qkv_full[:, :width]) + qv_bias[0]).astype(jnp.bfloat16)
    k = mm(normed, qkv_full[:, width : 2 * width]).astype(jnp.bfloat16)
    v = (mm(normed, qkv_full[:, 2 * width :]) + qv_bias[1]).astype(jnp.bfloat16)
    own, summary = keys_for(jnp.stack([k, v]), lengths, seq_count)
    tables = (own[0], own[1], summary[0], summary[1])
    attended, log_total = attend(facts, q, *tables)

    branch = lax.psum(mm(attended, out_full).astype(jnp.bfloat16), "mp").astype(jnp.float32)
    residual = hidden + branch + out_bias
    mid_normed, mid_inverse = norm_stats(residual)
    mid_low = (mid_normed * mid_gain + mid_shift).astype(jnp.bfloat16)
    activated, slope = gelu_parts(mm(mid_low, up_full) + up_bias)
    act_low = activated.astype(jnp.bfloat16)
    feed = lax.psum(mm(act_low, down_full).astype(jnp.bfloat16), "mp").astype(jnp.float32)
    hidden_out = (residual + feed + down_bias).astype(jnp.bfloat16)

    grad_down = cotangent[0]
    grad_out = grad_down.astype(jnp.float32)
    grad_pre = (slope * mm(grad_down, down_full, NT)).astype(jnp.bfloat16)
    over_rows = lambda left, right: mm(left, right, (((0,), (0,)), ((), ())))
    spread = lambda grad, axis: lax.psum_scatter(
        grad.astype(jnp.bfloat16), group, scatter_dimension=axis, tiled=True
    ).astype(jnp.float32)
    down_grad = spread(over_rows(act_low, grad_down), 1)
    up_grad = spread(over_rows(mid_low, grad_pre), 0)
    grad_mid = lax.psum(mm(grad_pre, up_full, NT).astype(jnp.bfloat16), "mp").astype(jnp.float32)
    grad_residual = grad_out + norm_back(grad_mid, mid_normed, mid_inverse, mid_gain)
    grad_branch = grad_residual.astype(jnp.bfloat16)
    out_grad = spread(over_rows(attended, grad_branch), 1)
    grad_attended = mm(grad_branch, out_full, NT).astype(jnp.bfloat16)

    dq, dk, dv, dks, dvs = attend_back(facts, q, *tables, grad_attended, log_total)
    dk, dv = keys_back(jnp.stack([dk, dv]), jnp.stack([dks, dvs]), rows, lengths, seq_count)
    grad_projected = jnp.concatenate([dq, dk, dv], axis=1)
    qkv_grad = spread(over_rows(normed, grad_projected), 0)
    grad_normed = lax.psum(mm(grad_projected, qkv_full, NT).astype(jnp.bfloat16), "mp").astype(
        jnp.float32
    )
    grad_input = grad_residual + norm_back(grad_normed, pre_normed, pre_inverse, pre_gain)
    total = lambda value: jnp.sum(value.astype(jnp.float32), axis=0)
    small = lax.psum(
        (
            total(grad_normed * pre_normed),
            total(grad_normed),
            jnp.stack([total(dq), total(dv)]),
            total(grad_residual),
            total(grad_mid * mid_normed),
            total(grad_mid),
            total(grad_pre),
            total(grad_out),
        ),
        group,
    )
    return (
        hidden_out[None],
        grad_input[None],
        small[0],
        small[1],
        qkv_grad.reshape(-1, 3, width),
        small[2],
        out_grad,
        small[3],
        small[4],
        small[5],
        up_grad,
        small[6],
        down_grad,
        small[7],
    )


def solution(mesh):
    rows = P("item", "seq", None)
    qkv = P(("item", "seq"), None, "mp")
    first = P(("item", "seq"), "mp")
    second = P("mp", ("item", "seq"))
    bias = P(None, "mp")
    return jax.shard_map(
        functools.partial(body, mesh.shape["seq"], mesh.shape["mp"]),
        mesh=mesh,
        in_specs=(
            rows,
            rows,
            P("item", None),
            P(),
            P(),
            qkv,
            bias,
            second,
            P(),
            P(),
            P(),
            first,
            P("mp"),
            second,
            P(),
        ),
        out_specs=(
            rows,
            rows,
            P(),
            P(),
            qkv,
            bias,
            second,
            P(),
            P(),
            P(),
            first,
            P("mp"),
            second,
            P(),
        ),
        check_vma=False,
    )
```

time: 2570 us -> 1360 us (0.53)
  waiting for transfers between devices: 1910 us -> 966 us
  matrix products: 358 us -> 183 us
  local copies, waits for them, and re-layouts: 98.3 us -> 17.9 us
  Pallas kernels: 0 us -> 59 us
  other arithmetic: 132 us -> 78.5 us
  loops' own time: 28 us -> 0 us
    psum x4 -> x3, waiting for transfers between devices: 1200 us -> 738 us  [the longest x1 359 us: body(): lax.psum(mm(act_low, down_full).astype(jnp.bfloat16), 'mp')]
    reduce_scatter x6 -> x4, waiting for transfers between devices: 550 us -> 104 us  [body(): lax.psum_scatter(grad.astype(jnp.bfloat16), group, scatter_dimension=axis...]
    dot_general x30 -> x14, matrix products: 358 us -> 183 us  [mm(): lax.dot_general(left, right, dims, preferred_element_type=jnp.float32)]
    pallas_call x0 -> x2, Pallas kernels: none -> 59 us  [the longest x1 33.5 us: attend_back(): pl.pallas_call(functools.partial(attend_back_kernel, query_block(rows), r...]
    all_gather x6 -> x4, waiting for transfers between devices: 154 us -> 109 us  [body(): lax.all_gather(weight, group, axis=axis, tiled=True)]
    reduce_or x20 -> x0, other arithmetic: 41.6 us -> none  [the longest x5 13.1 us: grad_step(): jnp.any(permitted)]
    convert_element_type x4 -> x0, local copies, waits for them, and re-layouts: 29.7 us -> none  [the longest x2 14.9 us: body(): key_parts.reshape(TOKENS, width).astype(jnp.bfloat16)]
    another operation x24 -> x0, loops' own time: 28 us -> none  [the longest x1 7.14 us: body(): lax.scan(mix_step, jnp.zeros((local_rows, local_heads, HDIM), jnp.float32...]
  transfers between devices with their start and end apart: 16 -> 13, of which waited for: 14 -> 10; matrix products, arithmetic and copies ran while one was open for 11% -> 13% of each run, Pallas kernels for 0% -> 4%
where the time goes in v1:
time: 1360 us; the launch traced here: 1350 us
  waiting for transfers between devices  966 us (71%)
  matrix products  183 us (13%)
  other arithmetic  78.5 us (6%)
  Pallas kernels  59 us (4%)
  blocking collectives  25.9 us (2%)
  local copies, waits for them, and re-layouts  17.9 us (1%)
  between operations  17.4 us (1%)
    psum x1, waiting for transfers between devices, body(): lax.psum(mm(act_low, down_full).astype(jnp.bfloat16), 'mp')  359 us
    psum x1, waiting for transfers between devices, body(): lax.psum(mm(attended, out_full).astype(jnp.bfloat16), 'mp')  190 us
    psum x1, waiting for transfers between devices, body(): lax.psum(mm(grad_pre, up_full, NT).astype(jnp.bfloat16), 'mp')  189 us
    dot_general x14, matrix products, mm(): lax.dot_general(left, right, dims, preferred_element_type=jnp.float32)  183 us
    all_gather x4, waiting for transfers between devices, body(): lax.all_gather(weight, group, axis=axis, tiled=True)  109 us
    reduce_scatter x4, waiting for transfers between devices, body(): lax.psum_scatter(grad.astype(jnp.bfloat16), group, scatter_dimension=axis...  104 us
    pallas_call x1, Pallas kernels, attend_back(): pl.pallas_call(functools.partial(attend_back_kernel, query_block(rows), r...  33.5 us
    reduce_sum x5, other arithmetic, body(): total = lambda value: jnp.sum(value.astype(jnp.float32), axis=0)  29.6 us
  transfers between devices with their start and end apart: 13, of which 10 were waited for; matrix products, arithmetic and copies ran while one was open for 13% of the time, Pallas kernels for 4%

profile of v1, /device:TPU:0, one launch (start us, length us, event | category | flops | bytes accessed | tf_op | source)
XLA Modules:
  0.0 1352.5 jit_solution(4557464086473488817)
XLA Ops:
  7.2 2.3 copy.30
  10.4 3.4 convert_reduce_fusion.3
  14.4 1.5 fusion.18
  15.9 4.3 fusion.13
  23.6 36.3 %all-gather.5.cloned.1.call-done = bf16[2048,1536]{0,1:T(8,128)(2,1)} async-done(((bf16[256,1536]{0,1:T(8,128)(2,1)}), bf16[2048,1536]{0,1:T(8,128)(2,1)}) %all-gather.5.cloned.1.call-update) | async-done | bytes 6291472 | tf_op jit(solution)/shard_map/all_gather | solution.py:267
  59.9 6.2 convolution_convert_fusion.9.k_ref
  66.4 2.9 fusion.31.v_ref
  69.4 2.6 collective-permute-start
  72.0 2.9 fusion.30.q_ref
  75.5 25.5 %attend.1 = (bf16[1280,512]{1,0:T(8,128)(2,1)S(1)}, f32[4,2,1280]{2,1,0:T(2,128)S(1)}) custom-call(s32[3]{0:T(128)S(1)} %pad_add_fusion.facts_ref, bf16[1280,512]{1,0:T(8,128)(2,1)S(1)} %fusion.30.q_ref, bf16[1280,512]{1,0:T(8,128)(2,1)S(1)} %convolution_convert_fusion.9.k_ref, bf16[1280,512]{1,0:T(8,128)(2,1)S(1)} %fusion.31.v_ref, ...), custom_call_target="tpu_custom_call" | custom-call | flops 3355443200 | bytes 5242880 | tf_op jit(solution)/shard_map/attend/pallas_call | solution.py:166
  103.3 6.2 convolution_convert_fusion
  110.7 190.0 %all-reduce.7.cloned.1.call-done = bf16[1280,2048]{1,0:T(8,128)(2,1)} async-done(((bf16[1280,2048]{1,0:T(8,128)(2,1)}), bf16[1280,2048]{1,0:T(8,128)(2,1)}) %all-reduce.7.cloned.1.call-update) | async-done | bytes 5242896 | tf_op jit(solution)/shard_map/psum | solution.py:294
  300.7 6.0 fusion.29
  306.8 5.5 multiply_reduce_fusion
  312.3 43.6 %all-gather.9.cloned.1.call-done = bf16[2048,2048]{1,0:T(8,128)(2,1)} async-done(((bf16[256,2048]{1,0:T(8,128)(2,1)}), bf16[2048,2048]{1,0:T(8,128)(2,1)}) %all-gather.9.cloned.1.call-update) | async-done | bytes 8388624 | tf_op jit(solution)/shard_map/all_gather | solution.py:267
  355.9 28.2 %fusion.41 = f32[1280,2048]{1,0:T(8,128)} fusion(bf16[2048,2048]{1,0:T(8,128)(2,1)} %all-gather.9.cloned.1.call-done, f32[2048]{0:T(1024)S(1)} %copy-done.34, f32[2048]{0:T(1024)S(1)} %copy-done.26, f32[1280]{0:T(1024)S(1)} %add_rsqrt_fusion, f32[1280]{0:T(1024)S(1)} %broadcast_multiply_fusion.4, f32[2048]{0:T(1024)S(1)} %copy-done.19, ...), kind=kOutput, calls=%fused_computation.98 | convolution fusion | flops 10761011200 | bytes 29394944 | tf_op jit(solution)/shard_map/dot_general | solution.py:31
  384.1 29.5 %all-gather.11.cloned.1.call-done = bf16[2048,2048]{1,0:T(8,128)(2,1)} async-done(((bf16[2048,256]{1,0:T(8,128)(2,1)}), bf16[2048,2048]{1,0:T(8,128)(2,1)}) %all-gather.11.cloned.1.call-update) | async-done | bytes 8388624 | tf_op jit(solution)/shard_map/all_gather | solution.py:267
  413.6 24.4 %convert_reduce_fusion.4 = (f32[2048]{0:T(1024)}, bf16[1280,2048]{1,0:T(8,128)(2,1)}) fusion(bf16[2048,2048]{1,0:T(8,128)(2,1)} %all-gather.11.cloned.1.call-done, bf16[1,1280,2048]{2,1,0:T(8,128)(2,1)} %param.16, f32[1280,2048]{1,0:T(8,128)} %fusion.41, f32[2048]{0:T(1024)S(1)} %copy-done.35), kind=kOutput, calls=%fused_computation.36 | convolution fusion | flops 10792466432 | bytes 29376512 | tf_op jit(solution)/shard_map/dot_general | solution.py:31
  438.1 14.7 %convolution_convert_fusion.5 = bf16[1280,2048]{1,0:T(8,128)(2,1)} fusion(bf16[1280,2048]{1,0:T(8,128)(2,1)} %get-tuple-element.88, bf16[2048,2048]{1,0:T(8,128)(2,1)S(1)} %copy-done.32), kind=kOutput, calls=%fused_computation.50 | convolution fusion | flops 10740039680 | bytes 18874368 | tf_op jit(solution)/shard_map/dot_general | solution.py:31
  452.8 189.0 %all-reduce.9.cloned.1.call-done = bf16[1280,2048]{1,0:T(8,128)(2,1)} async-done(((bf16[1280,2048]{1,0:T(8,128)(2,1)}), bf16[1280,2048]{1,0:T(8,128)(2,1)}) %all-reduce.9.cloned.1.call-update) | async-done | bytes 5242896 | tf_op jit(solution)/shard_map/psum | solution.py:312
  641.9 10.2 fusion.24
  652.0 10.3 fusion.42
  662.3 4.0 copy-done.12
  666.3 4.1 convolution_convert_fusion.7
  670.4 19.7 %convolution_convert_fusion.1 = bf16[2048,2048]{1,0:T(8,128)(2,1)} fusion(bf16[1,1280,2048]{2,1,0:T(8,128)(2,1)} %param.16, f32[1280,2048]{1,0:T(8,128)} %fusion.41, f32[2048]{0:T(1024)S(1)} %copy-done.35), kind=kOutput, calls=%fused_computation.46 | convolution fusion | flops 10767826944 | bytes 24125440 | tf_op jit(solution)/shard_map/dot_general | solution.py:31
  690.2 18.8 %convolution_convert_fusion.2 = bf16[2048,2048]{1,0:T(8,128)(2,1)} fusion(bf16[1280,2048]{1,0:T(8,128)(2,1)} %get-tuple-element.88, f32[2048]{0:T(1024)S(1)} %copy-done.34, f32[2048]{0:T(1024)S(1)} %copy-done.26, f32[1280]{0:T(1024)S(1)} %add_rsqrt_fusion, f32[1280]{0:T(1024)S(1)} %broadcast_multiply_fusion.4, f32[2048]{0:T(1024)S(1)} %copy-done.19, ...), kind=kOutput, calls=%fused_computation.47 | convolution fusion | flops 10765205504 | bytes 24152064 | tf_op jit(solution)/shard_map/dot_general | solution.py:31
  709.2 8.7 convolution_convert_fusion.8.do_ref
  717.9 33.5 %attend_back.1 = (bf16[1280,512]{1,0:T(8,128)(2,1)S(1)}, bf16[1280,512]{1,0:T(8,128)(2,1)S(1)}, bf16[1280,512]{1,0:T(8,128)(2,1)S(1)}, f32[64,512]{1,0:T(8,128)S(1)}, f32[64,512]{1,0:T(8,128)S(1)}) custom-call(s32[3]{0:T(128)S(1)} %copy-done.7, bf16[1280,512]{1,0:T(8,128)(2,1)S(1)} %copy-done.9, bf16[1280,512]{1,0:T(8,128)(2,1)} %copy-done, ...), custom_call_target="tpu_custom_call" | custom-call | flops 8388608000 | bytes 10485760 | tf_op jit(solution)/shard_map/attend_back/pallas_call | solution.py:191
  751.4 1.3 collective-permute-start.1
  752.7 1.7 pad_maximum_fusion.1
  754.4 12.0 collective-permute-done.1
  766.4 1.8 dynamic_update_slice.3
  768.2 1.9 slice_bitcast_fusion.1
  771.1 13.1 convolution_convert_fusion.3
  784.4 19.3 %convolution_convert_fusion.6 = bf16[1280,2048]{1,0:T(8,128)(2,1)} fusion(bf16[2048,2048]{1,0:T(8,128)(2,1)} %all-gather.11.cloned.1.call-done, f32[1280,2048]{1,0:T(8,128)} %fusion.41, f32[2048]{0:T(1024)S(1)} %copy-done.35), kind=kOutput, calls=%fused_computation.51 | convolution fusion | flops 10766254080 | bytes 24125440 | tf_op jit(solution)/shard_map/dot_general | solution.py:31
  803.6 13.9 %convolution_convert_fusion.4 = bf16[1280,2048]{1,0:T(8,128)(2,1)} fusion(bf16[2048,1536]{0,1:T(8,128)(2,1)} %all-gather.5.cloned.1.call-done, bf16[1280,512]{1,0:T(8,128)(2,1)S(1)} %copy-done.16, bf16[1280,512]{1,0:T(8,128)(2,1)S(1)} %get-tuple-element.79, bf16[1280,512]{1,0:T(8,128)(2,1)S(1)} %get-tuple-element.23), kind=kOutput, calls=%fused_computation.49 | convolution fusion | flops 8067481600 | bytes 15466496 | tf_op jit(solution)/shard_map/dot_general | solution.py:31
  817.9 1.6 convert_reduce_fusion.5
  819.5 1.8 convert_element_type.129
  821.3 2.7 convert_element_type.134
  824.0 41.5 %reduce-scatter.9.cloned.1.call-done = bf16[256,2048]{1,0:T(8,128)(2,1)} async-done(((bf16[2048,2048]{1,0:T(8,128)(2,1)}), bf16[256,2048]{1,0:T(8,128)(2,1)}) %reduce-scatter.9.cloned.1.call-update) | async-done | bytes 1048592 | tf_op jit(solution)/shard_map/reduce_scatter | solution.py:307
  865.5 2.8 convert_element_type.131
  868.3 62.6 %reduce-scatter.5.cloned.1.call-done = bf16[256,1536]{1,0:T(8,128)(2,1)} async-done(((bf16[2048,1536]{1,0:T(8,128)(2,1)}), bf16[256,1536]{1,0:T(8,128)(2,1)}) %reduce-scatter.5.cloned.1.call-update) | async-done | bytes 786448 | tf_op jit(solution)/shard_map/reduce_scatter | solution.py:307
  930.8 1.4 copy.31
  932.2 1.6 copy.32
  933.9 359.4 %all-reduce.11.cloned.1.call-done = (bf16[1280,2048]{1,0:T(8,128)(2,1)}, bf16[1280,2048]{1,0:T(8,128)(2,1)}) async-done(((bf16[1280,2048]{1,0:T(8,128)(2,1)}, bf16[1280,2048]{1,0:T(8,128)(2,1)}), (bf16[1280,2048]{1,0:T(8,128)(2,1)}, bf16[1280,2048]{1,0:T(8,128)(2,1)})) %all-reduce.11.cloned.1.call-update) | async-done | bytes 10485776 | tf_op jit(solution)/shard_map/psum | solution.py:300
  1293.2 7.3 fusion.25
  1300.6 25.9 %all-reduce.1 = (f32[2048]{0:T(1024)}, f32[2048]{0:T(1024)}, f32[2,512]{1,0:T(2,128)}, f32[2048]{0:T(1024)}, f32[2048]{0:T(1024)}, /*index=5*/f32[2048]{0:T(1024)}, f32[2048]{0:T(1024)}, f32[2048]{0:T(1024)}) all-reduce(f32[2048]{0:T(1024)S(1)} %get-tuple-element.58, ...), channel_id=1, replica_groups=mesh['item'=4,'seq'=2,'mp'=4] {'item','seq'}, use_global_device_ids=true, to_apply=%region_13.14 | all-reduce | flops 15360 | bytes 122880 | tf_op jit(solution)/shard_map/psum | solution.py:327
  1326.5 19.0 %fusion.17 = (f32[1,1280,2048]{2,1,0:T(8,128)}, bf16[1,1280,2048]{2,1,0:T(8,128)(2,1)}) fusion(f32[1280,2048]{1,0:T(8,128)} %copy-done.12, bf16[1,1280,2048]{2,1,0:T(8,128)(2,1)} %param.15, bf16[1280,2048]{1,0:T(8,128)(2,1)} %get-tuple-element.73, f32[1280]{0:T(1024)S(1)} %broadcast_multiply_fusion, f32[1280]{0:T(1024)S(1)} %broadcast_multiply_fusion.1, ...), kind=kLoop, calls=%fused_computation.27 | loop fusion | flops 44564480 | bytes 47230976 | tf_op jit(solution)/shard_map/broadcast_in_dim | solution.py:342
  (114 shorter events, 8.4 us)
Async XLA Ops:
  7.2 8.7 copy-start.22
  7.2 8.7 copy-start.27
  7.2 52.7 %all-gather.5.cloned.1.call-start = ((), (), s32[]{:S(2)}) async-start(), calls=%async_computation.4 | async-start | bytes 7077888 | tf_op jit(solution)/shard_map/all_gather | solution.py:267
  9.6 93.8 %all-gather.7.cloned.1.call-start = ((), (), s32[]{:S(2)}) async-start(), calls=%async_computation.5 | async-start | bytes 2359296 | tf_op jit(solution)/shard_map/all_gather | solution.py:267
  10.3 290.4 %all-reduce.7.cloned.1.call-start = ((), (), s32[]{:S(2)}) async-start(), calls=%async_computation.6 | async-start | bytes 10485760 | tf_op jit(solution)/shard_map/psum | solution.py:294
  10.4 4.0 copy-start.10
  13.8 6.5 copy-start.31
  13.8 9.8 copy-start.30
  14.4 5.9 copy-start.17
  15.9 4.3 copy-start.20
  23.6 51.9 %copy-start.6 = (s32[3]{0:T(128)}, s32[3]{0:T(128)S(1)}, u32[]{:S(2)}) copy-start(s32[3]{0:T(128)S(1)} %pad_add_fusion.facts_ref) | copy-start | bytes 40
  59.9 6.2 copy-start.14
  59.9 6.5 copy-start.33
  66.1 9.4 copy-start
  69.3 6.2 copy-start.1
  69.4 6.1 collective-permute-start
  101.6 0.6 copy-start.4
  102.3 1.1 copy-start.8
  103.3 197.4 %copy-start.19 = (f32[2048]{0:T(1024)S(1)}, f32[2048]{0:T(1024)}, u32[]{:S(2)}) copy-start(f32[2048]{0:T(1024)} %param.23) | copy-start | bytes 24580
  109.5 246.4 %all-gather.9.cloned.1.call-start = ((), (), s32[]{:S(2)}) async-start(), calls=%async_computation.7 | async-start | bytes 9437184 | tf_op jit(solution)/shard_map/all_gather | solution.py:267
  110.1 303.5 %all-gather.11.cloned.1.call-start = ((), (), s32[]{:S(2)}) async-start(), calls=%async_computation.8 | async-start | bytes 9437184 | tf_op jit(solution)/shard_map/all_gather | solution.py:267
  110.7 245.2 %copy-start.26 = (f32[2048]{0:T(1024)S(1)}, f32[2048]{0:T(1024)}, u32[]{:S(2)}) copy-start(f32[2048]{0:T(1024)} %param.24) | copy-start | bytes 24580
  110.7 245.2 %copy-start.34 = (f32[2048]{0:T(1024)S(1)}, f32[2048]{0:T(1024)}, u32[]{:S(2)}) copy-start(f32[2048]{0:T(1024)} %param.25) | copy-start | bytes 24580
  110.7 531.1 %all-reduce.9.cloned.1.call-start = ((), (), s32[]{:S(2)}) async-start(), calls=%async_computation.9 | async-start | bytes 10485760 | tf_op jit(solution)/shard_map/psum | solution.py:312
  300.7 6.0 copy-start.11
  312.3 101.3 %copy-start.35 = (f32[2048]{0:T(1024)S(1)}, f32[2048]{0:T(1024)}, u32[]{:S(2)}) copy-start(f32[2048]{0:T(1024)} %param.27) | copy-start | bytes 24580
  413.6 24.4 %copy-start.32 = (bf16[2048,2048]{1,0:T(8,128)(2,1)S(1)}, bf16[2048,2048]{1,0:T(8,128)(2,1)}, u32[]{:S(2)}) copy-start(bf16[2048,2048]{1,0:T(8,128)(2,1)} %all-gather.9.cloned.1.call-done) | copy-start | bytes 25165828
  452.8 366.7 %reduce-scatter.7.cloned.1.call-start = ((), (), s32[]{:S(2)}) async-start(), calls=%async_computation.11 | async-start | bytes 2359296 | tf_op jit(solution)/shard_map/reduce_scatter | solution.py:307
  641.9 10.2 copy-start.13
  662.3 4.0 copy-start.12
  670.4 150.9 %reduce-scatter.11.cloned.1.call-start = ((), (), s32[]{:S(2)}) async-start(), calls=%async_computation.13 | async-start | bytes 9437184 | tf_op jit(solution)/shard_map/reduce_scatter | solution.py:307
  690.2 175.3 %reduce-scatter.9.cloned.1.call-start = ((), (), s32[]{:S(2)}) async-start(), calls=%async_computation.12 | async-start | bytes 9437184 | tf_op jit(solution)/shard_map/reduce_scatter | solution.py:307
  709.1 8.8 copy-start.3
  709.1 8.8 copy-start.5
  709.1 8.8 copy-start.7
  709.1 8.8 copy-start.9
  709.1 221.7 %reduce-scatter.5.cloned.1.call-start = ((), (), s32[]{:S(2)}) async-start(), calls=%async_computation.10 | async-start | bytes 7077888 | tf_op jit(solution)/shard_map/reduce_scatter | solution.py:307
  751.4 14.9 %collective-permute-start.1 = (f32[2,50,512]{2,1,0:T(8,128)S(1)}, f32[2,50,512]{2,1,0:T(8,128)S(1)}, u32[]{:S(2)}, u32[]{:S(2)}) collective-permute-start(f32[2,50,512]{2,1,0:T(8,128)S(1)} %pad_maximum_fusion.4), channel_id=1, source_target_pairs={{4,0},{5,1},{6,2},{7,3},{12,8},{13,9},{14,10},{15,11},{20,16},{21,... | collective-permute-start | bytes 614408 | tf_op jit(solution)/shard_map/ppermute | solution.py:228
  770.1 1.1 copy-start.15
  784.3 508.9 %all-reduce.11.cloned.1.call-start = ((), (), s32[]{:S(2)}) async-start(), calls=%async_computation.14 | async-start | bytes 20971520 | tf_op jit(solution)/shard_map/psum | solution.py:300
  784.4 19.3 %copy-start.16 = (bf16[1280,512]{1,0:T(8,128)(2,1)S(1)}, bf16[1280,512]{1,0:T(8,128)(2,1)}, u32[]{:S(2)}) copy-start(bf16[1280,512]{1,0:T(8,128)(2,1)} %copy-done.15) | copy-start | bytes 3932164
  817.6 475.6 %copy-start.18 = (f32[1280]{0:T(1024)S(1)}, f32[1280]{0:T(1024)}, u32[]{:S(2)}) copy-start(f32[1280]{0:T(1024)} %copy-done.17) | copy-start | bytes 15364
  817.6 475.6 %copy-start.21 = (f32[1280]{0:T(1024)S(1)}, f32[1280]{0:T(1024)}, u32[]{:S(2)}) copy-start(f32[1280]{0:T(1024)} %copy-done.20) | copy-start | bytes 15364
  817.6 475.6 %copy-start.23 = (f32[2048]{0:T(1024)S(1)}, f32[2048]{0:T(1024)}, u32[]{:S(2)}) copy-start(f32[2048]{0:T(1024)} %param.18) | copy-start | bytes 24580
  868.3 432.3 %copy-start.24 = (f32[2048]{0:T(1024)S(1)}, f32[2048]{0:T(1024)}, u32[]{:S(2)}) copy-start(f32[2048]{0:T(1024)} %get-tuple-element.56) | copy-start | bytes 24580
  868.3 432.3 %copy-start.25 = (f32[2048]{0:T(1024)S(1)}, f32[2048]{0:T(1024)}, u32[]{:S(2)}) copy-start(f32[2048]{0:T(1024)} %get-tuple-element.62) | copy-start | bytes 24580
  868.3 432.4 %copy-start.28 = (f32[2048]{0:T(1024)S(1)}, f32[2048]{0:T(1024)}, u32[]{:S(2)}) copy-start(f32[2048]{0:T(1024)} %get-tuple-element.87) | copy-start | bytes 24580
  868.3 458.2 %copy-start.29 = (f32[2048]{0:T(1024)S(1)}, f32[2048]{0:T(1024)}, u32[]{:S(2)}) copy-start(f32[2048]{0:T(1024)} %param.29) | copy-start | bytes 24580
  (1 other events, 0.6 us)
Sparse Core Ops, SparseCore 0:
  10.5 49.3 all-gather.4
  61.8 28.8 all-gather.6
  109.6 191.0 all-reduce.6
  302.5 53.3 all-gather.8
  357.6 55.9 all-gather.10
  452.9 188.8 all-reduce.8
  670.5 40.1 reduce-scatter.6
  714.6 76.0 reduce-scatter.10
  794.2 71.2 reduce-scatter.8
  869.1 61.7 reduce-scatter.4
  934.0 359.1 all-reduce.10

commit v2 on v1

--- a/solution.py
+++ b/solution.py
@@ -16,6 +16,7 @@
 TOKENS = 2560
 PAIR = 2 * HDIM
 PIECE = 32
+SKEW = 2
 MIB = 1 << 20
 MESH = pl.DeviceIdType.MESH
 MASKED = -1e30
@@ -243,7 +244,310 @@
     )
 
 
+def line_kernel(count, half, group, dims, n_left, n_extra, n_owned, n_acc, finish, *refs):
+    refs = list(refs)
+    take = lambda n: [refs.pop(0) for _ in range(n)]
+    lefts, (right,), extras = take(n_left), take(1), take(n_extra)
+    (out,), owned, accs = take(1), take(n_owned), take(1 if n_acc else 0)
+    part, arrived, staged, up_sent, up_got, down_sent, down_got, local = refs
+    me = lax.axis_index("mp")
+    pieces = half // PIECE
+    per_group = group // PIECE
+    barrier = pltpu.get_barrier_semaphore()
+
+    @pl.when(me > 0)
+    def _():
+        pl.semaphore_signal(barrier, inc=1, device_id={"mp": me - 1}, device_id_type=MESH)
+
+    @pl.when(me < count - 1)
+    def _():
+        pl.semaphore_signal(barrier, inc=1, device_id={"mp": me + 1}, device_id_type=MESH)
+
+    if n_acc:
+        accs[0][...] = jnp.zeros_like(accs[0])
+
+    def multiply(flow, g):
+        rows = pl.ds(pl.multiple_of(flow * half + g * group, 16), group)
+        at = 0
+        for number, left in enumerate(lefts):
+            depth = left.shape[1]
+            cut = right.at[:, at : at + depth] if dims == NT else right.at[at : at + depth, :]
+            product = mm(left[rows, :], cut[...], dims)
+            if number == 0:
+                part[flow, g % 2] = product
+            else:
+                part[flow, g % 2] += product
+            at += depth
+
+    for flow in range(2):
+        multiply(flow, 0)
+
+    ends = (me == 0) | (me == count - 1)
+
+    @pl.when(ends)
+    def _():
+        pl.semaphore_wait(barrier, 1)
+
+    @pl.when(jnp.logical_not(ends))
+    def _():
+        pl.semaphore_wait(barrier, 2)
+
+    def onward(flow, k, place):
+        to = me - 1 if flow == 0 else me + 1
+        return pltpu.make_async_remote_copy(
+            src_ref=staged.at[flow, pl.ds(k * PIECE, PIECE)],
+            dst_ref=arrived.at[flow, pl.ds(k * PIECE, PIECE)],
+            send_sem=up_sent.at[flow, k],
+            recv_sem=up_got.at[flow, k],
+            device_id={"mp": to},
+            device_id_type=MESH,
+        )
+
+    def back(flow, k, owner):
+        to = me + 1 if flow == 0 else me - 1
+        rows = pl.ds(flow * half + k * PIECE, PIECE)
+        return pltpu.make_async_remote_copy(
+            src_ref=staged.at[flow, pl.ds(k * PIECE, PIECE)] if owner else out.at[rows],
+            dst_ref=out.at[rows],
+            send_sem=down_sent.at[flow, k],
+            recv_sem=down_got.at[flow, k],
+            device_id={"mp": to},
+            device_id_type=MESH,
+        )
+
+    def keep(flow, k):
+        return pltpu.make_async_copy(
+            staged.at[flow, pl.ds(k * PIECE, PIECE)],
+            out.at[pl.ds(flow * half + k * PIECE, PIECE)],
+            local.at[k],
+        )
+
+    def step(t, carry):
+        for flow in range(2):
+            place = count - 1 - me if flow == 0 else me
+            k = t - SKEW * place
+            here = pl.ds(pl.multiple_of(k * PIECE, PIECE), PIECE)
+            busy = (k >= 0) & (k < pieces)
+
+            def mine():
+                slot = (k // per_group) % 2
+                inner = pl.ds(pl.multiple_of((k % per_group) * PIECE, PIECE), PIECE)
+                return part[flow, slot, inner, :]
+
+            @pl.when(busy & (place == 0))
+            def _():
+                staged[flow, here, :] = mine().astype(jnp.bfloat16)
+                onward(flow, k, place).start()
+
+            @pl.when(busy & (place > 0) & (place < count - 1))
+            def _():
+                onward(flow, k, place).wait_recv()
+                total = mine() + arrived[flow, here, :].astype(jnp.float32)
+                staged[flow, here, :] = total.astype(jnp.bfloat16)
+                onward(flow, k, place).start()
+
+            @pl.when(busy & (place == count - 1))
+            def _():
+                onward(flow, k, place).wait_recv()
+                total = mine() + arrived[flow, here, :].astype(jnp.float32)
+                staged[flow, here, :] = finish(flow, k, total, extras, owned, accs).astype(
+                    jnp.bfloat16
+                )
+                back(flow, k, True).start()
+                keep(flow, k).start()
+
+        for flow in range(2):
+            place = count - 1 - me if flow == 0 else me
+            j = t - SKEW * (2 * (count - 1) - place)
+
+            @pl.when((j >= 0) & (j < pieces) & (place < count - 1))
+            def _():
+                back(flow, j, False).wait_recv()
+
+                @pl.when(place > 0)
+                def _():
+                    back(flow, j, False).start()
+
+        for flow in range(2):
+            place = count - 1 - me if flow == 0 else me
+            k = t - SKEW * place
+            g = k // per_group + 1
+
+            @pl.when((k >= 0) & (k % per_group == 0) & (g < pieces // per_group))
+            def _():
+                multiply(flow, g)
+
+        return carry
+
+    lax.fori_loop(0, pieces + 2 * SKEW * (count - 1), step, 0)
+
+    def settle(k, carry):
+        for flow in range(2):
+            place = count - 1 - me if flow == 0 else me
+
+            @pl.when(place < count - 1)
+            def _():
+                onward(flow, k, place).wait_send()
+
+                @pl.when(place > 0)
+                def _():
+                    back(flow, k, False).wait_send()
+
+            @pl.when(place == count - 1)
+            def _():
+                back(flow, k, True).wait_send()
+                keep(flow, k).wait()
+
+        return carry
+
+    lax.fori_loop(0, pieces, settle, 0)
+
+
+def line_sum(number, count, lefts, right, dims, extras, n_owned, n_acc, finish, name):
+    rows = lefts[0].shape[0]
+    features = right.shape[1 if dims == NN else 0]
+    half = rows // 2
+    pieces = half // PIECE
+    group = 5 * PIECE if pieces % 5 == 0 else PIECE
+    vmem = pl.BlockSpec(memory_space=pltpu.VMEM)
+    anywhere = pl.BlockSpec(memory_space=pl.ANY)
+    acc = [jax.ShapeDtypeStruct((n_acc, 8, features), jnp.float32)] if n_acc else []
+    dma = lambda *shape: pltpu.SemaphoreType.DMA(shape)
+    return pl.pallas_call(
+        functools.partial(
+            line_kernel, count, half, group, dims, len(lefts), len(extras), n_owned, n_acc, finish
+        ),
+        in_specs=[vmem] * (len(lefts) + 1 + len(extras)),
+        out_specs=[anywhere] + [vmem] * (n_owned + len(acc)),
+        out_shape=[jax.ShapeDtypeStruct((rows, features), jnp.bfloat16)]
+        + [jax.ShapeDtypeStruct((half, features), jnp.float32)] * n_owned
+        + acc,
+        scratch_shapes=[
+            pltpu.VMEM((2, 2, group, features), jnp.float32),
+            pltpu.VMEM((2, half, features), jnp.bfloat16),
+            pltpu.VMEM((2, half, features), jnp.bfloat16),
+            dma(2, pieces),
+            dma(2, pieces),
+            dma(2, pieces),
+            dma(2, pieces),
+            dma(pieces),
+        ],
+        compiler_params=pltpu.CompilerParams(
+            collective_id=number, has_side_effects=True, vmem_limit_bytes=60 * MIB
+        ),
+        cost_estimate=pl.CostEstimate(
+            flops=2 * rows * features * sum(left.shape[1] for left in lefts),
+            bytes_accessed=4 * rows * features,
+            transcendentals=0,
+        ),
+        name=name,
+    )(*lefts, right, *extras)
+
+
+def piece_rows(flow, k, half):
+    return pl.ds(pl.multiple_of(flow * half + k * PIECE, PIECE), PIECE)
+
+
+def fold(values):
+    return jnp.sum(values.reshape(-1, 8, values.shape[-1]), axis=0)
+
+
+def finish_mid(flow, k, total, extras, owned, accs):
+    hidden, bias, gain, shift = extras
+    (residual_ref,) = owned
+    half = residual_ref.shape[0]
+    residual = hidden[piece_rows(flow, k, half), :].astype(jnp.float32) + total + bias[...]
+    residual_ref[piece_rows(0, k, half), :] = residual
+    return norm_stats(residual)[0] * gain[...] + shift[...]
+
+
+def finish_branch(flow, k, total, extras, owned, accs):
+    residual, cotangent, gain = extras
+    (grad_ref,) = owned
+    (acc,) = accs
+    half = grad_ref.shape[0]
+    normed, inverse = norm_stats(residual[piece_rows(0, k, half), :])
+    grad = cotangent[piece_rows(flow, k, half), :].astype(jnp.float32)
+    grad = grad + norm_back(total, normed, inverse, gain[...])
+    grad_ref[piece_rows(0, k, half), :] = grad
+    acc[0] += fold(total * normed)
+    acc[1] += fold(total)
+    acc[2] += fold(grad)
+    return grad
+
+
+def finish_input(flow, k, total, extras, owned, accs):
+    hidden, grad, gain = extras
+    (acc,) = accs
+    half = grad.shape[0]
+    normed, inverse = norm_stats(hidden[piece_rows(flow, k, half), :].astype(jnp.float32))
+    acc[0] += fold(total * normed)
+    acc[1] += fold(total)
+    return grad[piece_rows(0, k, half), :] + norm_back(total, normed, inverse, gain[...])
+
+
+def finish_out(flow, k, total, extras, owned, accs):
+    residual, bias = extras
+    half = residual.shape[0]
+    return residual[piece_rows(0, k, half), :] + total + bias[...]
+
+
+def small_kernel(stages, shared, own_ref, out_ref, sent, got, send_sem, recv_sem):
+    barrier = pltpu.get_barrier_semaphore()
+
+    def partner(axis, bit):
+        index = lax.axis_index(axis)
+        return {axis: index + bit - 2 * bit * ((index // bit) % 2)}
+
+    for axis, bit in stages:
+        pl.semaphore_signal(barrier, inc=1, device_id=partner(axis, bit), device_id_type=MESH)
+    pl.semaphore_wait(barrier, len(stages))
+    sent[0] = own_ref[...]
+    row = lax.broadcasted_iota(jnp.int32, own_ref.shape, 0)
+    for number, (axis, bit) in enumerate(stages):
+        copy = pltpu.make_async_remote_copy(
+            src_ref=sent.at[number],
+            dst_ref=got.at[number],
+            send_sem=send_sem.at[number],
+            recv_sem=recv_sem.at[number],
+            device_id=partner(axis, bit),
+            device_id_type=MESH,
+        )
+        copy.start()
+        copy.wait()
+        total = sent[number] + got[number]
+        if axis == "mp":
+            total = jnp.where(row < shared, total, sent[number])
+        if number + 1 < len(stages):
+            sent[number + 1] = total
+        else:
+            out_ref[...] = total
+
+
+def small_sum(number, sizes, shared, values):
+    stages = tuple(
+        (axis, 1 << bit) for axis, size in sizes for bit in range(size.bit_length() - 1)
+    )
+    steps = len(stages)
+    vmem = pl.BlockSpec(memory_space=pltpu.VMEM)
+    return pl.pallas_call(
+        functools.partial(small_kernel, stages, shared),
+        in_specs=[vmem],
+        out_specs=vmem,
+        out_shape=jax.ShapeDtypeStruct(values.shape, jnp.float32),
+        scratch_shapes=[
+            pltpu.VMEM((steps, *values.shape), jnp.float32),
+            pltpu.VMEM((steps, *values.shape), jnp.float32),
+            pltpu.SemaphoreType.DMA((steps,)),
+            pltpu.SemaphoreType.DMA((steps,)),
+        ],
+        compiler_params=pltpu.CompilerParams(collective_id=number, has_side_effects=True),
+        name="small_sum",
+    )(values)
+
+
 def body(
+    item_count,
     seq_count,
     mp_count,
     hidden_in,
@@ -282,8 +586,7 @@
         ]
     ).astype(jnp.int32)
 
-    pre_normed, pre_inverse = norm_stats(hidden)
-    normed = (pre_normed * pre_gain + pre_shift).astype(jnp.bfloat16)
+    normed = (norm_stats(hidden)[0] * pre_gain + pre_shift).astype(jnp.bfloat16)
     q = (mm(normed, qkv_full[:, :width]) + qv_bias[0]).astype(jnp.bfloat16)
     k = mm(normed, qkv_full[:, width : 2 * width]).astype(jnp.bfloat16)
     v = (mm(normed, qkv_full[:, 2 * width :]) + qv_bias[1]).astype(jnp.bfloat16)
@@ -291,67 +594,106 @@
     tables = (own[0], own[1], summary[0], summary[1])
     attended, log_total = attend(facts, q, *tables)
 
-    branch = lax.psum(mm(attended, out_full).astype(jnp.bfloat16), "mp").astype(jnp.float32)
-    residual = hidden + branch + out_bias
-    mid_normed, mid_inverse = norm_stats(residual)
-    mid_low = (mid_normed * mid_gain + mid_shift).astype(jnp.bfloat16)
+    row = lambda vector: vector[None, :]
+    mid_low, residual = line_sum(
+        1,
+        mp_count,
+        [attended],
+        out_full,
+        NN,
+        [hidden_in[0], row(out_bias), row(mid_gain), row(mid_shift)],
+        1,
+        0,
+        finish_mid,
+        "out_sum",
+    )
     activated, slope = gelu_parts(mm(mid_low, up_full) + up_bias)
     act_low = activated.astype(jnp.bfloat16)
-    feed = lax.psum(mm(act_low, down_full).astype(jnp.bfloat16), "mp").astype(jnp.float32)
-    hidden_out = (residual + feed + down_bias).astype(jnp.bfloat16)
-
     grad_down = cotangent[0]
-    grad_out = grad_down.astype(jnp.float32)
     grad_pre = (slope * mm(grad_down, down_full, NT)).astype(jnp.bfloat16)
+    grad_branch, grad_residual, mid_sums = line_sum(
+        2,
+        mp_count,
+        [grad_pre],
+        up_full,
+        NT,
+        [residual, grad_down, row(mid_gain)],
+        1,
+        3,
+        finish_branch,
+        "mid_sum",
+    )
     over_rows = lambda left, right: mm(left, right, (((0,), (0,)), ((), ())))
     spread = lambda grad, axis: lax.psum_scatter(
         grad.astype(jnp.bfloat16), group, scatter_dimension=axis, tiled=True
     ).astype(jnp.float32)
     down_grad = spread(over_rows(act_low, grad_down), 1)
     up_grad = spread(over_rows(mid_low, grad_pre), 0)
-    grad_mid = lax.psum(mm(grad_pre, up_full, NT).astype(jnp.bfloat16), "mp").astype(jnp.float32)
-    grad_residual = grad_out + norm_back(grad_mid, mid_normed, mid_inverse, mid_gain)
-    grad_branch = grad_residual.astype(jnp.bfloat16)
     out_grad = spread(over_rows(attended, grad_branch), 1)
     grad_attended = mm(grad_branch, out_full, NT).astype(jnp.bfloat16)
+    (hidden_out,) = line_sum(
+        3,
+        mp_count,
+        [act_low],
+        down_full,
+        NN,
+        [residual, row(down_bias)],
+        0,
+        0,
+        finish_out,
+        "down_sum",
+    )
 
     dq, dk, dv, dks, dvs = attend_back(facts, q, *tables, grad_attended, log_total)
     dk, dv = keys_back(jnp.stack([dk, dv]), jnp.stack([dks, dvs]), rows, lengths, seq_count)
-    grad_projected = jnp.concatenate([dq, dk, dv], axis=1)
-    qkv_grad = spread(over_rows(normed, grad_projected), 0)
-    grad_normed = lax.psum(mm(grad_projected, qkv_full, NT).astype(jnp.bfloat16), "mp").astype(
-        jnp.float32
-    )
-    grad_input = grad_residual + norm_back(grad_normed, pre_normed, pre_inverse, pre_gain)
+    grad_input, pre_sums = line_sum(
+        4,
+        mp_count,
+        [dq, dk, dv],
+        qkv_full,
+        NT,
+        [hidden_in[0], grad_residual, row(pre_gain)],
+        0,
+        2,
+        finish_input,
+        "input_sum",
+    )
+    qkv_grad = spread(over_rows(normed, jnp.concatenate([dq, dk, dv], axis=1)), 0)
     total = lambda value: jnp.sum(value.astype(jnp.float32), axis=0)
-    small = lax.psum(
-        (
-            total(grad_normed * pre_normed),
-            total(grad_normed),
-            jnp.stack([total(dq), total(dv)]),
-            total(grad_residual),
-            total(grad_mid * mid_normed),
-            total(grad_mid),
-            total(grad_pre),
-            total(grad_out),
+    features = hidden.shape[1]
+    qv_sums = jnp.concatenate([total(dq), total(dv)])
+    sums = small_sum(
+        5,
+        [("item", item_count), ("seq", seq_count), ("mp", mp_count)],
+        6,
+        jnp.concatenate(
+            [
+                jnp.sum(mid_sums, axis=1),
+                jnp.sum(pre_sums, axis=1),
+                row(jnp.where(lax.axis_index("mp") == 0, total(grad_down), 0.0)),
+                total(grad_pre).reshape(-1, features),
+                jnp.pad(qv_sums, (0, -qv_sums.shape[0] % features)).reshape(-1, features),
+            ]
         ),
-        group,
-    )
+    )
+    ff_rows = up_weight.shape[1] // features
+    up_bias_grad = sums[6 : 6 + ff_rows].reshape(-1)
+    qv_bias_grad = sums[6 + ff_rows :].reshape(-1)[: 2 * width].reshape(2, width)
     return (
         hidden_out[None],
-        grad_input[None],
-        small[0],
-        small[1],
+        grad_input.astype(jnp.float32)[None],
+        sums[3],
+        sums[4],
         qkv_grad.reshape(-1, 3, width),
-        small[2],
+        qv_bias_grad,
         out_grad,
-        small[3],
-        small[4],
-        small[5],
+        sums[2],
+        sums[0],
+        sums[1],
         up_grad,
-        small[6],
+        up_bias_grad,
         down_grad,
-        small[7],
+        sums[5],
     )
 
 
@@ -362,7 +704,7 @@
     second = P("mp", ("item", "seq"))
     bias = P(None, "mp")
     return jax.shard_map(
-        functools.partial(body, mesh.shape["seq"], mesh.shape["mp"]),
+        functools.partial(body, mesh.shape["item"], mesh.shape["seq"], mesh.shape["mp"]),
         mesh=mesh,
         in_specs=(
             rows,

time: 1360 us -> 888 us (0.65)
  waiting for transfers between devices: 966 us -> 40.6 us
  Pallas kernels: 59 us -> 645 us
  matrix products: 183 us -> 117 us
  other arithmetic: 78.5 us -> 31.3 us
  blocking collectives: 25.9 us -> 0 us
    psum x3 -> x0, waiting for transfers between devices: 738 us -> none  [the longest x1 359 us: body(): lax.psum(mm(act_low, down_full).astype(jnp.bfloat16), 'mp')]
    pallas_call x0 -> x5, Pallas kernels: none -> 586 us  [the longest x4 566 us: line_sum(): pl.pallas_call(functools.partial(line_kernel, count, half, group, dims, l...]
    reduce_scatter x4, waiting for transfers between devices: 104 us -> 0.01 us  [body(): lax.psum_scatter(grad.astype(jnp.bfloat16), group, scatter_dimension=axis...]
    all_gather x4, waiting for transfers between devices: 109 us -> 33.7 us  [body(): lax.all_gather(weight, group, axis=axis, tiled=True)]
    dot_general x14 -> x10, matrix products: 183 us -> 117 us  [mm(): lax.dot_general(left, right, dims, preferred_element_type=jnp.float32)]
    psum x1 -> x0, blocking collectives: 25.9 us -> none  [body(): lax.psum((total(grad_normed * pre_normed), total(grad_normed), jnp.stack(...]
    reduce_sum x5 -> x3, other arithmetic: 29.6 us -> 3.91 us  [body(): total = lambda value: jnp.sum(value.astype(jnp.float32), axis=0)]
  transfers between devices with their start and end apart: 13 -> 10, of which waited for: 10 -> 2; matrix products, arithmetic and copies ran while one was open for 13% -> 14% of each run, Pallas kernels for 4% -> 57%
where the time goes in v2:
time: 888 us; the launch traced here: 881 us
  Pallas kernels  645 us (73%)
  matrix products  117 us (13%)
  waiting for transfers between devices  40.6 us (5%)
  other arithmetic  31.3 us (4%)
  local copies, waits for them, and re-layouts  24.1 us (3%)
  between operations  17.4 us (2%)
    pallas_call x4, Pallas kernels, line_sum(): pl.pallas_call(functools.partial(line_kernel, count, half, group, dims, l...  566 us
    dot_general x10, matrix products, mm(): lax.dot_general(left, right, dims, preferred_element_type=jnp.float32)  117 us
    pallas_call x1, Pallas kernels, attend_back(): pl.pallas_call(functools.partial(attend_back_kernel, query_block(rows), r...  33.7 us
    all_gather x4, waiting for transfers between devices, body(): lax.all_gather(weight, group, axis=axis, tiled=True)  33.7 us
    pallas_call x1, Pallas kernels, attend(): pl.pallas_call(functools.partial(attend_kernel, query_block(rows), rows =...  25.5 us
    pallas_call x1, Pallas kernels, small_sum(): pl.pallas_call(functools.partial(small_kernel, stages, shared), in_specs=...  19.9 us
  transfers between devices with their start and end apart: 10, of which 2 were waited for; matrix products, arithmetic and copies ran while one was open for 14% of the time, Pallas kernels for 57%

profile of v2, /device:TPU:0, one launch (start us, length us, event | category | flops | bytes accessed | tf_op | source)
XLA Modules:
  0.0 880.5 jit_solution(17857833879803638883)
XLA Ops:
  7.2 1.4 copy.31
  8.7 1.2 copy.32
  9.9 0.7 all-gather.7.cloned.1.call-update
  10.6 0.7 all-gather.9.cloned.1.call-update
  12.0 0.6 constant_dynamic-slice_fusion
  15.3 3.4 convert_reduce_fusion
  19.2 1.5 fusion.2
  20.8 4.3 fusion.5
  25.1 33.7 %all-gather.5.cloned.1.call-done.refs_3_ = bf16[2048,1536]{1,0:T(8,128)(2,1)} async-done(((bf16[256,1536]{1,0:T(8,128)(2,1)}), bf16[2048,1536]{1,0:T(8,128)(2,1)}) %all-gather.5.cloned.1.call-update) | async-done | bytes 6291472 | tf_op jit(solution)/shard_map/all_gather | solution.py:571
  58.7 6.2 convolution_convert_fusion.5.k_ref
  65.3 2.9 fusion.12.v_ref
  68.2 3.4 collective-permute-start
  71.7 2.9 fusion.11.q_ref
  74.6 25.5 %attend.1 = (bf16[1280,512]{1,0:T(8,128)(2,1)S(1)}, f32[4,2,1280]{2,1,0:T(2,128)S(1)}) custom-call(s32[3]{0:T(128)S(1)} %pad_add_fusion.facts_ref, bf16[1280,512]{1,0:T(8,128)(2,1)S(1)} %fusion.11.q_ref, bf16[1280,512]{1,0:T(8,128)(2,1)S(1)} %convolution_convert_fusion.5.k_ref, bf16[1280,512]{1,0:T(8,128)(2,1)S(1)} %fusion.12.v_ref, ...), custom_call_target="tpu_custom_call" | custom-call | flops 3355443200 | bytes 5242880 | tf_op jit(solution)/shard_map/attend/pallas_call | solution.py:167
  100.2 1.0 copy-done.3
  101.2 1.1 copy-done.5
  102.3 139.3 %out_sum.1 = (bf16[1280,2048]{1,0:T(8,128)(2,1)}, f32[640,2048]{1,0:T(8,128)}) custom-call(bf16[1280,512]{1,0:T(8,128)(2,1)} %copy-done.3, bf16[512,2048]{1,0:T(8,128)(2,1)} %all-gather.7.cloned.1.call-done.refs_1_, bf16[1280,2048]{1,0:T(8,128)(2,1)} %bitcast.77, f32[1,2048]{1,0:T(1,128)} %bitcast.96, f32[1,2048]{1,0:T(1,128)} %bitcast.98, f32[1,2048]{1,0:T(1,128)} %bitcast.97), custom_call_target="tpu_custom_call" | custom-call | flops 2684354560 | bytes 10485760 | tf_op jit(solution)/shard_map/out_sum/pallas_call | solution.py:416
  241.6 20.4 %multiply_convert_fusion.1 = (bf16[1280,2048]{1,0:T(8,128)(2,1)}, f32[1280,2048]{1,0:T(8,128)}) fusion(f32[2048]{0:T(1024)S(1)} %copy-done.18, bf16[1280,2048]{1,0:T(8,128)(2,1)} %get-tuple-element.29, bf16[2048,2048]{1,0:T(8,128)(2,1)} %all-gather.9.cloned.1.call-done.refs_1_), kind=kOutput, calls=%fused_computation.11 | convolution fusion | flops 10763632640 | bytes 29368320 | tf_op jit(solution)/shard_map/dot_general | solution.py:32
  262.0 23.8 %convert_reduce_fusion.1 = (f32[2048]{0:T(1024)S(1)}, bf16[1280,2048]{1,0:T(8,128)(2,1)}) fusion(bf16[2048,2048]{1,0:T(8,128)(2,1)} %all-gather.11.cloned.1.call-done.refs_1_, bf16[1,1280,2048]{2,1,0:T(8,128)(2,1)} %param.16, f32[1280,2048]{1,0:T(8,128)} %get-tuple-element.88, f32[2048]{0:T(1024)S(1)} %copy-done.18), kind=kOutput, calls=%fused_computation.8 | convolution fusion | flops 10792466432 | bytes 29376512 | tf_op jit(solution)/shard_map/dot_general | solution.py:32
  285.9 147.6 %mid_sum.1 = (bf16[1280,2048]{1,0:T(8,128)(2,1)}, f32[640,2048]{1,0:T(8,128)}, f32[3,8,2048]{2,1,0:T(8,128)}) custom-call(bf16[1280,2048]{1,0:T(8,128)(2,1)} %get-tuple-element.86.refs_0_, bf16[2048,2048]{1,0:T(8,128)(2,1)} %all-gather.9.cloned.1.call-done.refs_1_, f32[640,2048]{1,0:T(8,128)} %get-tuple-element.30.refs_2_, bf16[1280,2048]{1,0:T(8,128)(2,1)} %bitcast.80, ...), custom_call_target="tpu_custom_call" | custom-call | flops 10737418240 | bytes 10485760 | tf_op jit(solution)/shard_map/mid_sum/pallas_call | solution.py:416
  433.5 6.6 convolution_convert_fusion.3
  440.2 7.2 convolution_convert_fusion.4.do_ref
  447.4 33.7 %attend_back.1 = (bf16[1280,512]{1,0:T(8,128)(2,1)S(1)}, bf16[1280,512]{1,0:T(8,128)(2,1)S(1)}, bf16[1280,512]{1,0:T(8,128)(2,1)S(1)}, f32[64,512]{1,0:T(8,128)S(1)}, f32[64,512]{1,0:T(8,128)S(1)}) custom-call(s32[3]{0:T(128)S(1)} %pad_add_fusion.facts_ref, bf16[1280,512]{1,0:T(8,128)(2,1)S(1)} %copy-done.6, bf16[1280,512]{1,0:T(8,128)(2,1)} %copy-done.1, ...), custom_call_target="tpu_custom_call" | custom-call | flops 8388608000 | bytes 10485760 | tf_op jit(solution)/shard_map/attend_back/pallas_call | solution.py:192
  481.1 1.3 collective-permute-start.1
  482.4 1.7 pad_maximum_fusion
  484.2 4.9 collective-permute-done.1
  489.1 1.8 dynamic_update_slice.3
  490.9 1.9 slice_bitcast_fusion
  492.8 1.0 copy-done.10
  494.3 13.0 %convolution_convert_fusion.2 = bf16[2048,1536]{1,0:T(8,128)(2,1)} fusion(bf16[1280,2048]{1,0:T(8,128)(2,1)} %fusion.5, bf16[1280,512]{1,0:T(8,128)(2,1)S(1)} %get-tuple-element.70.refs_2_, bf16[1280,512]{1,0:T(8,128)(2,1)S(1)} %get-tuple-element.71.refs_1_, bf16[1280,512]{1,0:T(8,128)(2,1)S(1)} %get-tuple-element.33.refs_0_), kind=kOutput, calls=%fused_computation.16 | convolution fusion | flops 8068005888 | bytes 15466496 | tf_op jit(solution)/shard_map/dot_general | solution.py:32
  507.4 16.9 %convolution_convert_fusion.1 = bf16[2048,2048]{1,0:T(8,128)(2,1)} fusion(bf16[1280,2048]{1,0:T(8,128)(2,1)} %get-tuple-element.29, bf16[1280,2048]{1,0:T(8,128)(2,1)} %get-tuple-element.86.refs_0_), kind=kOutput, calls=%fused_computation.15 | convolution fusion | flops 10741612544 | bytes 18874368 | tf_op jit(solution)/shard_map/dot_general | solution.py:32
  524.3 16.7 %convolution_convert_fusion = bf16[2048,2048]{1,0:T(8,128)(2,1)} fusion(bf16[1280,2048]{1,0:T(8,128)(2,1)} %get-tuple-element.87.refs_0_, bf16[1,1280,2048]{2,1,0:T(8,128)(2,1)} %param.16), kind=kOutput, calls=%fused_computation.14 | convolution fusion | flops 10741612544 | bytes 18874368 | tf_op jit(solution)/shard_map/dot_general | solution.py:32
  541.1 3.4 convert_reduce_fusion.2
  544.5 138.1 %down_sum.1 = bf16[1280,2048]{1,0:T(8,128)(2,1)} custom-call(bf16[1280,2048]{1,0:T(8,128)(2,1)} %get-tuple-element.87.refs_0_, bf16[2048,2048]{1,0:T(8,128)(2,1)} %all-gather.11.cloned.1.call-done.refs_1_, f32[640,2048]{1,0:T(8,128)} %get-tuple-element.30.refs_2_, f32[1,2048]{1,0:T(1,128)} %bitcast.100), custom_call_target="tpu_custom_call" | custom-call | flops 10737418240 | bytes 10485760 | tf_op jit(solution)/shard_map/down_sum/pallas_call | solution.py:416
  682.9 141.2 %input_sum.1 = (bf16[1280,2048]{1,0:T(8,128)(2,1)}, f32[2,8,2048]{2,1,0:T(8,128)}) custom-call(bf16[1280,512]{1,0:T(8,128)(2,1)} %copy-done, bf16[1280,512]{1,0:T(8,128)(2,1)} %copy-done.11, bf16[1280,512]{1,0:T(8,128)(2,1)} %copy-done.10, bf16[2048,1536]{1,0:T(8,128)(2,1)} %all-gather.5.cloned.1.call-done.refs_3_, bf16[1280,2048]{1,0:T(8,128)(2,1)} %bitcast.78, ...), custom_call_target="tpu_custom_call" | custom-call | flops 8053063680 | bytes 10485760 | tf_op jit(solution)/shard_map/input_sum/pallas_call | solution.py:416
  824.1 1.0 reduce_sum.75
  825.3 0.7 concatenate.10.own_ref
  826.0 19.9 %small_sum.1 = f32[8,2048]{1,0:T(8,128)} custom-call(f32[8,2048]{1,0:T(8,128)} %concatenate.10.own_ref), custom_call_target="tpu_custom_call" | custom-call | tf_op jit(solution)/shard_map/small_sum/pallas_call | solution.py:533
  846.0 0.8 slice_reduce_fusion
  846.7 0.6 reshape.89
  847.3 2.0 fusion.21
  849.4 8.0 bitcast_convert_fusion
  857.4 1.8 convert_element_type.85
  859.2 1.4 copy.33
  860.6 1.6 copy.34
  862.2 2.8 convert_element_type.87
  865.0 2.7 convert_element_type.89
  867.7 5.7 copy.37
  (71 shorter events, 3.1 us)
Async XLA Ops:
  7.2 4.8 copy-start.16
  7.2 8.1 copy-start.15
  7.2 51.5 %all-gather.5.cloned.1.call-start = ((), (), s32[]{:S(2)}) async-start(), calls=%async_computation.4 | async-start | bytes 7077888 | tf_op jit(solution)/shard_map/all_gather | solution.py:571
  9.8 92.4 %all-gather.7.cloned.1.call-start = ((), (), s32[]{:S(2)}) async-start(), calls=%async_computation.5 | async-start | bytes 2359296 | tf_op jit(solution)/shard_map/all_gather | solution.py:571
  10.6 231.0 %all-gather.9.cloned.1.call-start = ((), (), s32[]{:S(2)}) async-start(), calls=%async_computation.6 | async-start | bytes 9437184 | tf_op jit(solution)/shard_map/all_gather | solution.py:571
  11.3 250.7 %all-gather.11.cloned.1.call-start = ((), (), s32[]{:S(2)}) async-start(), calls=%async_computation.7 | async-start | bytes 9437184 | tf_op jit(solution)/shard_map/all_gather | solution.py:571
  11.9 845.5 %reduce-scatter.7.cloned.1.call-start = ((), (), s32[]{:S(2)}) async-start(), calls=%async_computation.9 | async-start | bytes 2359296 | tf_op jit(solution)/shard_map/reduce_scatter | solution.py:627
  15.2 4.0 copy-start.7
  15.3 5.5 copy-start.13
  15.3 5.5 copy-start.14
  58.7 6.2 copy-start.9
  58.7 6.5 copy-start.17
  64.9 9.7 %copy-start.1 = (bf16[1280,512]{1,0:T(8,128)(2,1)}, bf16[1280,512]{1,0:T(8,128)(2,1)S(1)}, u32[]{:S(2)}) copy-start(bf16[1280,512]{1,0:T(8,128)(2,1)S(1)} %convolution_convert_fusion.5.k_ref) | copy-start | bytes 3932164
  68.2 6.5 copy-start.2
  68.2 6.3 collective-permute-start
  100.2 1.1 copy-start.3
  101.2 1.1 copy-start.5
  102.3 139.4 %copy-start.18 = (f32[2048]{0:T(1024)S(1)}, f32[2048]{0:T(1024)}, u32[]{:S(2)}) copy-start(f32[2048]{0:T(1024)} %param.27) | copy-start | bytes 24580
  285.9 147.6 %copy-start.4 = (bf16[1280,512]{1,0:T(8,128)(2,1)S(1)}, bf16[1280,512]{1,0:T(8,128)(2,1)}, u32[]{:S(2)}) copy-start(bf16[1280,512]{1,0:T(8,128)(2,1)} %copy-done.3) | copy-start | bytes 3932164
  440.1 7.3 copy-start.6
  440.1 419.1 %reduce-scatter.5.cloned.1.call-start = ((), (), s32[]{:S(2)}) async-start(), calls=%async_computation.8 | async-start | bytes 7077888 | tf_op jit(solution)/shard_map/reduce_scatter | solution.py:627
  481.1 201.6 %copy-start = (bf16[1280,512]{1,0:T(8,128)(2,1)}, bf16[1280,512]{1,0:T(8,128)(2,1)S(1)}, u32[]{:S(2)}) copy-start(bf16[1280,512]{1,0:T(8,128)(2,1)S(1)} %get-tuple-element.33.refs_0_) | copy-start | bytes 3932164
  481.1 7.9 collective-permute-start.1
  492.8 1.1 copy-start.10
  492.8 1.5 copy-start.11
  507.3 354.9 %reduce-scatter.9.cloned.1.call-start = ((), (), s32[]{:S(2)}) async-start(), calls=%async_computation.10 | async-start | bytes 9437184 | tf_op jit(solution)/shard_map/reduce_scatter | solution.py:627
  524.3 340.7 %reduce-scatter.11.cloned.1.call-start = ((), (), s32[]{:S(2)}) async-start(), calls=%async_computation.11 | async-start | bytes 9437184 | tf_op jit(solution)/shard_map/reduce_scatter | solution.py:627
  544.5 138.1 %copy-start.12 = (f32[3,8,2048]{2,1,0:T(8,128)S(1)}, f32[3,8,2048]{2,1,0:T(8,128)}, u32[]{:S(2)}) copy-start(f32[3,8,2048]{2,1,0:T(8,128)} %get-tuple-element.40) | copy-start | bytes 589828
  682.9 142.2 %copy-start.8 = (bf16[2,1280,512]{2,1,0:T(8,128)(2,1)S(1)}, bf16[2,1280,512]{2,1,0:T(8,128)(2,1)}, u32[]{:S(2)}) copy-start(bf16[2,1280,512]{2,1,0:T(8,128)(2,1)} %dynamic_update_slice.3) | copy-start | bytes 7864324
Sparse Core Ops, SparseCore 0:
  10.5 48.2 all-gather.4
  60.6 28.8 all-gather.6
  91.4 54.3 all-gather.8
  147.6 55.9 all-gather.10
  440.2 42.5 reduce-scatter.6
  507.5 60.9 reduce-scatter.4
  571.9 71.2 reduce-scatter.8
  647.1 71.2 reduce-scatter.10

commit v3 on v2

--- a/solution.py
+++ b/solution.py
@@ -95,66 +95,6 @@
         o_ref[block * bq : (block + 1) * bq, :] = joined.T.astype(jnp.bfloat16)
 
 
-def attend_back_kernel(
-    bq,
-    causal,
-    facts_ref,
-    q_ref,
-    k_ref,
-    v_ref,
-    ks_ref,
-    vs_ref,
-    do_ref,
-    lse_ref,
-    dq_ref,
-    dk_ref,
-    dv_ref,
-    dks_ref,
-    dvs_ref,
-    dk_acc,
-    dv_acc,
-):
-    rows, seg = q_ref.shape[0], k_ref.shape[0]
-    scale = jnp.bfloat16(HDIM**-0.5)
-    k_t = (k_ref[...] * scale).T
-    ks_t = (ks_ref[...] * scale).T
-    ks = ks_ref[...]
-    vs = vs_ref[...]
-    low_half = lax.broadcasted_iota(jnp.int32, (PAIR, 1), 0) < HDIM
-    dk_acc[...] = jnp.zeros_like(dk_acc)
-    dv_acc[...] = jnp.zeros_like(dv_acc)
-    dks = jnp.zeros((SUMM_ROWS, PAIR), jnp.float32)
-    dvs = jnp.zeros((SUMM_ROWS, PAIR), jnp.float32)
-    for block in range(rows // bq):
-        nk = (block + 1) * bq if causal else seg
-        own, earlier = key_masks(facts_ref, block, rows, bq, nk)
-        q = q_ref[block * bq : (block + 1) * bq, :] * scale
-        do = do_ref[block * bq : (block + 1) * bq, :]
-        grads = []
-        for head in range(2):
-            qh = jnp.where(head_lanes(head), q, jnp.zeros_like(q))
-            doh = jnp.where(head_lanes(head), do, jnp.zeros_like(do))
-            lse = lse_ref[0, head : head + 1, block * bq : (block + 1) * bq]
-            p = jnp.exp(jnp.where(own, mm(k_ref[:nk, :], qh, NT), MASKED) - lse)
-            p2 = jnp.exp(jnp.where(earlier, mm(ks, qh, NT), MASKED) - lse)
-            dp = mm(v_ref[:nk, :], doh, NT)
-            dp2 = mm(vs, doh, NT)
-            delta = jnp.sum(p * dp, axis=0, keepdims=True) + jnp.sum(p2 * dp2, axis=0, keepdims=True)
-            ds = (p * (dp - delta)).astype(jnp.bfloat16)
-            ds2 = (p2 * (dp2 - delta)).astype(jnp.bfloat16)
-            dv_acc[:nk, :] += mm(p.astype(jnp.bfloat16), doh)
-            dk_acc[:nk, :] += mm(ds, qh)
-            dvs = dvs + mm(p2.astype(jnp.bfloat16), doh)
-            dks = dks + mm(ds2, qh)
-            grads.append(mm(k_t[:, :nk], ds) + mm(ks_t, ds2))
-        joined = jnp.where(low_half, grads[0], grads[1])
-        dq_ref[block * bq : (block + 1) * bq, :] = joined.T.astype(jnp.bfloat16)
-    dk_ref[...] = dk_acc[...].astype(jnp.bfloat16)
-    dv_ref[...] = dv_acc[...].astype(jnp.bfloat16)
-    dks_ref[...] = dks
-    dvs_ref[...] = dvs
-
-
 def query_block(rows):
     return 256 if rows % 256 == 0 else math.gcd(rows, 160)
 
@@ -182,30 +122,6 @@
     )(facts, q, k, v, ks, vs)
 
 
-def attend_back(facts, q, k, v, ks, vs, do, lse):
-    rows, width = q.shape
-    seg = k.shape[0]
-    pairs = width // PAIR
-    column = lambda n: pl.BlockSpec((n, PAIR), lambda i: (0, i))
-    low = lambda n: jax.ShapeDtypeStruct((n, width), jnp.bfloat16)
-    wide = lambda n: jax.ShapeDtypeStruct((n, width), jnp.float32)
-    return pl.pallas_call(
-        functools.partial(attend_back_kernel, query_block(rows), rows == seg),
-        grid=(pairs,),
-        in_specs=[pl.BlockSpec(memory_space=pltpu.SMEM)]
-        + [column(n) for n in (rows, seg, seg, SUMM_ROWS, SUMM_ROWS, rows)]
-        + [pl.BlockSpec((1, 2, rows), lambda i: (i, 0, 0))],
-        out_specs=[column(n) for n in (rows, seg, seg, SUMM_ROWS, SUMM_ROWS)],
-        out_shape=[low(rows), low(seg), low(seg), wide(SUMM_ROWS), wide(SUMM_ROWS)],
-        scratch_shapes=[pltpu.VMEM((seg, PAIR), jnp.float32)] * 2,
-        compiler_params=pltpu.CompilerParams(vmem_limit_bytes=48 * MIB),
-        cost_estimate=pl.CostEstimate(
-            flops=10 * rows * seg * width, bytes_accessed=16 * rows * width, transcendentals=0
-        ),
-        name="attend_back",
-    )(facts, q, k, v, ks, vs, do, lse)
-
-
 def keys_for(local, lengths, seq_count):
     rows, width = local.shape[-2:]
     pad = ((0, 0), (0, SUMM_ROWS - SUMM), (0, 0))
@@ -244,196 +160,262 @@
     )
 
 
-def line_kernel(count, half, group, dims, n_left, n_extra, n_owned, n_acc, finish, *refs):
-    refs = list(refs)
-    take = lambda n: [refs.pop(0) for _ in range(n)]
-    lefts, (right,), extras = take(n_left), take(1), take(n_extra)
-    (out,), owned, accs = take(1), take(n_owned), take(1 if n_acc else 0)
-    part, arrived, staged, up_sent, up_got, down_sent, down_got, local = refs
-    me = lax.axis_index("mp")
-    pieces = half // PIECE
-    per_group = group // PIECE
-    barrier = pltpu.get_barrier_semaphore()
-
-    @pl.when(me > 0)
-    def _():
-        pl.semaphore_signal(barrier, inc=1, device_id={"mp": me - 1}, device_id_type=MESH)
-
-    @pl.when(me < count - 1)
-    def _():
-        pl.semaphore_signal(barrier, inc=1, device_id={"mp": me + 1}, device_id_type=MESH)
-
-    if n_acc:
-        accs[0][...] = jnp.zeros_like(accs[0])
-
-    def multiply(flow, g):
-        rows = pl.ds(pl.multiple_of(flow * half + g * group, 16), group)
-        at = 0
-        for number, left in enumerate(lefts):
-            depth = left.shape[1]
-            cut = right.at[:, at : at + depth] if dims == NT else right.at[at : at + depth, :]
-            product = mm(left[rows, :], cut[...], dims)
-            if number == 0:
-                part[flow, g % 2] = product
-            else:
-                part[flow, g % 2] += product
-            at += depth
-
-    for flow in range(2):
-        multiply(flow, 0)
-
-    ends = (me == 0) | (me == count - 1)
-
-    @pl.when(ends)
-    def _():
-        pl.semaphore_wait(barrier, 1)
-
-    @pl.when(jnp.logical_not(ends))
-    def _():
-        pl.semaphore_wait(barrier, 2)
-
-    def onward(flow, k, place):
-        to = me - 1 if flow == 0 else me + 1
-        return pltpu.make_async_remote_copy(
-            src_ref=staged.at[flow, pl.ds(k * PIECE, PIECE)],
-            dst_ref=arrived.at[flow, pl.ds(k * PIECE, PIECE)],
-            send_sem=up_sent.at[flow, k],
-            recv_sem=up_got.at[flow, k],
-            device_id={"mp": to},
-            device_id_type=MESH,
-        )
-
-    def back(flow, k, owner):
-        to = me + 1 if flow == 0 else me - 1
-        rows = pl.ds(flow * half + k * PIECE, PIECE)
-        return pltpu.make_async_remote_copy(
-            src_ref=staged.at[flow, pl.ds(k * PIECE, PIECE)] if owner else out.at[rows],
-            dst_ref=out.at[rows],
-            send_sem=down_sent.at[flow, k],
-            recv_sem=down_got.at[flow, k],
-            device_id={"mp": to},
-            device_id_type=MESH,
-        )
-
-    def keep(flow, k):
-        return pltpu.make_async_copy(
-            staged.at[flow, pl.ds(k * PIECE, PIECE)],
-            out.at[pl.ds(flow * half + k * PIECE, PIECE)],
-            local.at[k],
-        )
-
-    def step(t, carry):
-        for flow in range(2):
-            place = count - 1 - me if flow == 0 else me
-            k = t - SKEW * place
-            here = pl.ds(pl.multiple_of(k * PIECE, PIECE), PIECE)
-            busy = (k >= 0) & (k < pieces)
-
-            def mine():
-                slot = (k // per_group) % 2
-                inner = pl.ds(pl.multiple_of((k % per_group) * PIECE, PIECE), PIECE)
-                return part[flow, slot, inner, :]
-
-            @pl.when(busy & (place == 0))
-            def _():
-                staged[flow, here, :] = mine().astype(jnp.bfloat16)
-                onward(flow, k, place).start()
-
-            @pl.when(busy & (place > 0) & (place < count - 1))
-            def _():
-                onward(flow, k, place).wait_recv()
-                total = mine() + arrived[flow, here, :].astype(jnp.float32)
-                staged[flow, here, :] = total.astype(jnp.bfloat16)
-                onward(flow, k, place).start()
-
-            @pl.when(busy & (place == count - 1))
-            def _():
-                onward(flow, k, place).wait_recv()
-                total = mine() + arrived[flow, here, :].astype(jnp.float32)
-                staged[flow, here, :] = finish(flow, k, total, extras, owned, accs).astype(
-                    jnp.bfloat16
-                )
-                back(flow, k, True).start()
-                keep(flow, k).start()
-
-        for flow in range(2):
-            place = count - 1 - me if flow == 0 else me
-            j = t - SKEW * (2 * (count - 1) - place)
-
-            @pl.when((j >= 0) & (j < pieces) & (place < count - 1))
-            def _():
-                back(flow, j, False).wait_recv()
-
-                @pl.when(place > 0)
-                def _():
-                    back(flow, j, False).start()
-
-        for flow in range(2):
-            place = count - 1 - me if flow == 0 else me
-            k = t - SKEW * place
-            g = k // per_group + 1
-
-            @pl.when((k >= 0) & (k % per_group == 0) & (g < pieces // per_group))
-            def _():
-                multiply(flow, g)
-
-        return carry
-
-    lax.fori_loop(0, pieces + 2 * SKEW * (count - 1), step, 0)
-
-    def settle(k, carry):
-        for flow in range(2):
-            place = count - 1 - me if flow == 0 else me
-
-            @pl.when(place < count - 1)
-            def _():
-                onward(flow, k, place).wait_send()
-
-                @pl.when(place > 0)
-                def _():
-                    back(flow, k, False).wait_send()
-
-            @pl.when(place == count - 1)
-            def _():
-                back(flow, k, True).wait_send()
-                keep(flow, k).wait()
-
-        return carry
-
-    lax.fori_loop(0, pieces, settle, 0)
-
-
-def line_sum(number, count, lefts, right, dims, extras, n_owned, n_acc, finish, name):
-    rows = lefts[0].shape[0]
-    features = right.shape[1 if dims == NN else 0]
-    half = rows // 2
-    pieces = half // PIECE
-    group = 5 * PIECE if pieces % 5 == 0 else PIECE
-    vmem = pl.BlockSpec(memory_space=pltpu.VMEM)
-    anywhere = pl.BlockSpec(memory_space=pl.ANY)
-    acc = [jax.ShapeDtypeStruct((n_acc, 8, features), jnp.float32)] if n_acc else []
-    dma = lambda *shape: pltpu.SemaphoreType.DMA(shape)
-    return pl.pallas_call(
-        functools.partial(
-            line_kernel, count, half, group, dims, len(lefts), len(extras), n_owned, n_acc, finish
-        ),
-        in_specs=[vmem] * (len(lefts) + 1 + len(extras)),
-        out_specs=[anywhere] + [vmem] * (n_owned + len(acc)),
-        out_shape=[jax.ShapeDtypeStruct((rows, features), jnp.bfloat16)]
-        + [jax.ShapeDtypeStruct((half, features), jnp.float32)] * n_owned
-        + acc,
-        scratch_shapes=[
+class Line:
+    def __init__(self, count, half, multiply, finish, out, part, moving, sems):
+        self.count, self.half, self.multiply, self.finish = count, half, multiply, finish
+        self.out, self.part, self.moving = out, part, moving
+        self.up_sent, self.up_got, self.down_sent, self.down_got, self.local = sems
+        self.me = lax.axis_index("mp")
+        self.pieces = half // PIECE
+        self.per_group = part.shape[2] // PIECE
+        self.steps = self.pieces + 2 * SKEW * (count - 1)
+
+    @staticmethod
+    def scratch(half, features):
+        pieces = half // PIECE
+        group = 5 * PIECE if pieces % 5 == 0 else PIECE
+        dma = lambda *shape: pltpu.SemaphoreType.DMA(shape)
+        return [
             pltpu.VMEM((2, 2, group, features), jnp.float32),
-            pltpu.VMEM((2, half, features), jnp.bfloat16),
             pltpu.VMEM((2, half, features), jnp.bfloat16),
             dma(2, pieces),
             dma(2, pieces),
             dma(2, pieces),
             dma(2, pieces),
             dma(pieces),
-        ],
+        ]
+
+    def place(self, flow):
+        return self.count - 1 - self.me if flow == 0 else self.me
+
+    def greet(self, barrier):
+        me = self.me
+
+        @pl.when(me > 0)
+        def _():
+            pl.semaphore_signal(barrier, inc=1, device_id={"mp": me - 1}, device_id_type=MESH)
+
+        @pl.when(me < self.count - 1)
+        def _():
+            pl.semaphore_signal(barrier, inc=1, device_id={"mp": me + 1}, device_id_type=MESH)
+
+    def meet(self, barrier, others=0):
+        ends = (self.me == 0) | (self.me == self.count - 1)
+
+        @pl.when(ends)
+        def _():
+            pl.semaphore_wait(barrier, 1 + others)
+
+        @pl.when(jnp.logical_not(ends))
+        def _():
+            pl.semaphore_wait(barrier, 2 + others)
+
+    def first(self):
+        for flow in range(2):
+            self.part[flow, 0] = self.multiply(flow, 0)
+
+    def onward(self, flow, k):
+        here = self.moving.at[flow, pl.ds(k * PIECE, PIECE)]
+        return pltpu.make_async_remote_copy(
+            src_ref=here,
+            dst_ref=here,
+            send_sem=self.up_sent.at[flow, k],
+            recv_sem=self.up_got.at[flow, k],
+            device_id={"mp": self.me - 1 if flow == 0 else self.me + 1},
+            device_id_type=MESH,
+        )
+
+    def back(self, flow, k, owner):
+        rows = self.out.at[pl.ds(flow * self.half + k * PIECE, PIECE)]
+        return pltpu.make_async_remote_copy(
+            src_ref=self.moving.at[flow, pl.ds(k * PIECE, PIECE)] if owner else rows,
+            dst_ref=rows,
+            send_sem=self.down_sent.at[flow, k],
+            recv_sem=self.down_got.at[flow, k],
+            device_id={"mp": self.me + 1 if flow == 0 else self.me - 1},
+            device_id_type=MESH,
+        )
+
+    def keep(self, flow, k):
+        return pltpu.make_async_copy(
+            self.moving.at[flow, pl.ds(k * PIECE, PIECE)],
+            self.out.at[pl.ds(flow * self.half + k * PIECE, PIECE)],
+            self.local.at[k],
+        )
+
+    def step(self, t):
+        last = self.count - 1
+        for flow in range(2):
+            place = self.place(flow)
+            k = t - SKEW * place
+            here = pl.ds(pl.multiple_of(k * PIECE, PIECE), PIECE)
+            busy = (k >= 0) & (k < self.pieces)
+
+            def mine():
+                slot = (k // self.per_group) % 2
+                inner = pl.ds(pl.multiple_of((k % self.per_group) * PIECE, PIECE), PIECE)
+                return self.part[flow, slot, inner, :]
+
+            @pl.when(busy & (place == 0))
+            def _():
+                self.moving[flow, here, :] = mine().astype(jnp.bfloat16)
+                self.onward(flow, k).start()
+
+            @pl.when(busy & (place > 0) & (place < last))
+            def _():
+                self.onward(flow, k).wait_recv()
+                total = mine() + self.moving[flow, here, :].astype(jnp.float32)
+                self.moving[flow, here, :] = total.astype(jnp.bfloat16)
+                self.onward(flow, k).start()
+
+            @pl.when(busy & (place == last))
+            def _():
+                self.onward(flow, k).wait_recv()
+                total = mine() + self.moving[flow, here, :].astype(jnp.float32)
+                self.moving[flow, here, :] = self.finish(flow, k, total).astype(jnp.bfloat16)
+                self.back(flow, k, True).start()
+                self.keep(flow, k).start()
+
+        for flow in range(2):
+            place = self.place(flow)
+            j = t - SKEW * (2 * last - place)
+
+            @pl.when((j >= 0) & (j < self.pieces) & (place < last))
+            def _():
+                self.back(flow, j, False).wait_recv()
+
+                @pl.when(place > 0)
+                def _():
+                    self.back(flow, j, False).start()
+
+        for flow in range(2):
+            k = t - SKEW * self.place(flow)
+            g = k // self.per_group + 1
+
+            @pl.when((k >= 0) & (k % self.per_group == 0) & (g < self.pieces // self.per_group))
+            def _():
+                self.part[flow, g % 2] = self.multiply(flow, g)
+
+    def settle(self):
+        def one(k, carry):
+            for flow in range(2):
+                place = self.place(flow)
+
+                @pl.when(place < self.count - 1)
+                def _():
+                    self.onward(flow, k).wait_send()
+
+                    @pl.when(place > 0)
+                    def _():
+                        self.back(flow, k, False).wait_send()
+
+                @pl.when(place == self.count - 1)
+                def _():
+                    self.back(flow, k, True).wait_send()
+                    self.keep(flow, k).wait()
+
+            return carry
+
+        lax.fori_loop(0, self.pieces, one, 0)
+
+
+def group_product(lefts, right, dims, half, group):
+    def multiply(flow, g):
+        rows = pl.ds(pl.multiple_of(flow * half + g * group, 16), group)
+        at, total = 0, None
+        for left in lefts:
+            depth = left.shape[1]
+            cut = right[:, at : at + depth] if dims == NT else right[at : at + depth, :]
+            product = mm(left[rows, :], cut, dims)
+            total = product if total is None else total + product
+            at += depth
+        return total
+
+    return multiply
+
+
+def line_kernel(count, half, dims, n_left, n_extra, n_owned, n_acc, finish, side, *refs):
+    refs = list(refs)
+    take = lambda n: [refs.pop(0) for _ in range(n)]
+    lefts, (right,), extras, side_in = take(n_left), take(1), take(n_extra), take(side.n_in)
+    (out,), owned, accs = take(1), take(n_owned), take(1 if n_acc else 0)
+    side_out = take(side.n_out)
+    part, moving, sems, side_scratch = *take(2), take(5), refs
+    multiply = group_product(lefts, right, dims, half, part.shape[2])
+    ending = lambda flow, k, total: finish(flow, k, total, extras, owned, accs)
+    line = Line(count, half, multiply, ending, out, part, moving, sems)
+    job = side(side_in, side_out, side_scratch)
+    barrier = pltpu.get_barrier_semaphore()
+    line.greet(barrier)
+    job.greet(barrier)
+    if n_acc:
+        accs[0][...] = jnp.zeros_like(accs[0])
+    job.first()
+    line.first()
+    line.meet(barrier, job.others)
+
+    def step(t, carry):
+        line.step(t)
+        job.step(t)
+        return carry
+
+    lax.fori_loop(0, max(line.steps, job.steps), step, 0)
+    line.settle()
+    job.settle()
+
+
+class Nothing:
+    n_in = n_out = others = steps = 0
+    operands, in_specs, out_shape, out_specs, scratch_shapes = (), (), (), (), ()
+
+    def __call__(self, ins, outs, scratch):
+        return self
+
+    def greet(self, barrier):
+        pass
+
+    def first(self):
+        pass
+
+    def step(self, t):
+        pass
+
+    def settle(self):
+        pass
+
+
+VMEM = pl.BlockSpec(memory_space=pltpu.VMEM)
+ANY = pl.BlockSpec(memory_space=pl.ANY)
+SMEM = pl.BlockSpec(memory_space=pltpu.SMEM)
+
+
+def line_sum(number, count, lefts, right, dims, extras, n_owned, n_acc, finish, name, side=Nothing()):
+    rows = lefts[0].shape[0]
+    features = right.shape[1 if dims == NN else 0]
+    half = rows // 2
+    acc = [jax.ShapeDtypeStruct((n_acc, 8, features), jnp.float32)] if n_acc else []
+    return pl.pallas_call(
+        functools.partial(
+            line_kernel,
+            count,
+            half,
+            dims,
+            len(lefts),
+            len(extras),
+            n_owned,
+            n_acc,
+            finish,
+            side,
+        ),
+        in_specs=[VMEM] * (len(lefts) + 1 + len(extras)) + list(side.in_specs),
+        out_specs=[ANY] + [VMEM] * (n_owned + len(acc)) + list(side.out_specs),
+        out_shape=[jax.ShapeDtypeStruct((rows, features), jnp.bfloat16)]
+        + [jax.ShapeDtypeStruct((half, features), jnp.float32)] * n_owned
+        + acc
+        + list(side.out_shape),
+        scratch_shapes=Line.scratch(half, features) + list(side.scratch_shapes),
         compiler_params=pltpu.CompilerParams(
-            collective_id=number, has_side_effects=True, vmem_limit_bytes=60 * MIB
+            collective_id=number, has_side_effects=True, vmem_limit_bytes=62 * MIB
         ),
         cost_estimate=pl.CostEstimate(
             flops=2 * rows * features * sum(left.shape[1] for left in lefts),
@@ -441,7 +423,7 @@
             transcendentals=0,
         ),
         name=name,
-    )(*lefts, right, *extras)
+    )(*lefts, right, *extras, *side.operands)
 
 
 def piece_rows(flow, k, half):
@@ -490,6 +472,397 @@
     residual, bias = extras
     half = residual.shape[0]
     return residual[piece_rows(0, k, half), :] + total + bias[...]
+
+
+class AttendBack(Nothing):
+    n_in, n_out = 8, 5
+
+    def __init__(self, facts, q, k, v, ks, vs, do, lse):
+        rows, width = q.shape
+        seg = k.shape[0]
+        self.operands = (facts, q, k, v, ks, vs, do, lse)
+        self.in_specs = (SMEM,) + (VMEM,) * 7
+        low = lambda n: jax.ShapeDtypeStruct((n, width), jnp.bfloat16)
+        wide = lambda n: jax.ShapeDtypeStruct((n, width), jnp.float32)
+        self.out_shape = (low(rows), low(seg), low(seg), wide(SUMM_ROWS), wide(SUMM_ROWS))
+        self.out_specs = (VMEM,) * 5
+        self.scratch_shapes = (
+            pltpu.VMEM((seg, PAIR), jnp.float32),
+            pltpu.VMEM((seg, PAIR), jnp.float32),
+            pltpu.VMEM((PAIR, seg), jnp.bfloat16),
+        )
+        self.bq = query_block(rows)
+        self.blocks = rows // self.bq
+        self.pairs = width // PAIR
+        self.steps = self.pairs * self.blocks
+        self.causal = rows == seg
+
+    def __call__(self, ins, outs, scratch):
+        self.ins, self.outs, self.scratch = ins, outs, scratch
+        return self
+
+    def step(self, t):
+        pair = t // self.blocks
+        for block in range(self.blocks):
+
+            @pl.when((t < self.steps) & (t % self.blocks == block))
+            def _():
+                self.unit(pair, block)
+
+    def unit(self, pair, block):
+        facts, q_ref, k_ref, v_ref, ks_ref, vs_ref, do_ref, lse_ref = self.ins
+        dq_ref, dk_ref, dv_ref, dks_ref, dvs_ref = self.outs
+        dk_acc, dv_acc, k_t = self.scratch
+        seg, bq = k_ref.shape[0], self.bq
+        cols = pl.ds(pl.multiple_of(pair * PAIR, PAIR), PAIR)
+        scale = jnp.bfloat16(HDIM**-0.5)
+        low_half = lax.broadcasted_iota(jnp.int32, (PAIR, 1), 0) < HDIM
+        if block == 0:
+            k_t[...] = (k_ref[:, cols] * scale).T
+            dk_acc[...] = jnp.zeros_like(dk_acc)
+            dv_acc[...] = jnp.zeros_like(dv_acc)
+            dks_ref[:, cols] = jnp.zeros((SUMM_ROWS, PAIR), jnp.float32)
+            dvs_ref[:, cols] = jnp.zeros((SUMM_ROWS, PAIR), jnp.float32)
+        ks, vs = ks_ref[:, cols], vs_ref[:, cols]
+        ks_t = (ks * scale).T
+        nk = (block + 1) * bq if self.causal else seg
+        here = slice(block * bq, (block + 1) * bq)
+        own, earlier = key_masks(facts, block, self.blocks * bq, bq, nk)
+        q = q_ref[here, cols] * scale
+        do = do_ref[here, cols]
+        k, v = k_ref[:nk, cols], v_ref[:nk, cols]
+        grads = []
+        for head in range(2):
+            qh = jnp.where(head_lanes(head), q, jnp.zeros_like(q))
+            doh = jnp.where(head_lanes(head), do, jnp.zeros_like(do))
+            lse = lse_ref[pair, head : head + 1, here]
+            p = jnp.exp(jnp.where(own, mm(k, qh, NT), MASKED) - lse)
+            p2 = jnp.exp(jnp.where(earlier, mm(ks, qh, NT), MASKED) - lse)
+            dp = mm(v, doh, NT)
+            dp2 = mm(vs, doh, NT)
+            delta = jnp.sum(p * dp, axis=0, keepdims=True) + jnp.sum(p2 * dp2, axis=0, keepdims=True)
+            ds = (p * (dp - delta)).astype(jnp.bfloat16)
+            ds2 = (p2 * (dp2 - delta)).astype(jnp.bfloat16)
+            dv_acc[:nk, :] += mm(p.astype(jnp.bfloat16), doh)
+            dk_acc[:nk, :] += mm(ds, qh)
+            dvs_ref[:, cols] += mm(p2.astype(jnp.bfloat16), doh)
+            dks_ref[:, cols] += mm(ds2, qh)
+            grads.append(mm(k_t[:, :nk], ds) + mm(ks_t, ds2))
+        joined = jnp.where(low_half, grads[0], grads[1])
+        dq_ref[here, cols] = joined.T.astype(jnp.bfloat16)
+        if block == self.blocks - 1:
+            dk_ref[:, cols] = dk_acc[...].astype(jnp.bfloat16)
+            dv_ref[:, cols] = dv_acc[...].astype(jnp.bfloat16)
+
+
+class Spread(Nothing):
+    others = 3
+    n_in, n_out = 10, 4
+    block = 256
+    lag = (2, 5, 8)
+
+    def __init__(self, factors, columns):
+        rows, features = factors[0].shape
+        block, half = self.block, self.block // 2
+        assert features == 8 * block
+        self.rows = rows
+        self.operands = tuple(factors) + tuple(right for _, right, _, _ in columns)
+        self.in_specs = (ANY,) * self.n_in
+        self.table, self.phases = [], {}
+        at, widths = 0, [0] * 4
+        for number, (left, right, result, place) in enumerate(columns):
+            self.phases.setdefault(left, at)
+            self.table.append((number, at, at + right.shape[1] // block, result, place))
+            at += right.shape[1] // block
+            widths[result] += right.shape[1]
+        self.chunks = at
+        self.steps = at + self.lag[2]
+        self.across = (True, False, False, True)
+        self.out_shape = tuple(
+            jax.ShapeDtypeStruct((block, n) if across else (n, block), jnp.float32)
+            for n, across in zip(widths, self.across)
+        )
+        self.out_specs = (ANY,) * 4
+        low = lambda *shape: pltpu.VMEM(shape, jnp.bfloat16)
+        wide = lambda *shape: pltpu.VMEM(shape, jnp.float32)
+        dma = lambda n: pltpu.SemaphoreType.DMA((n,))
+        self.scratch_shapes = (
+            low(2, rows, features),
+            low(2, rows, block),
+            low(3, 2, block, 2 * block),
+            wide(3, 2, block, 2 * block),
+            low(4, 2, block, 2 * block),
+            low(3, half, 2 * block),
+            low(3, 2, half, block),
+            wide(3, half, 2 * block),
+            wide(3, 2, half, block),
+            low(6, half, 2 * block),
+            low(6, 2, half, block),
+            low(3, 2, half, block),
+            wide(3, 2, half, block),
+            low(6, 2, half, block),
+            wide(3, block, block),
+            dma(2),
+            dma(2),
+            dma(3),
+            dma(4),
+            dma(3),
+            dma(6),
+            dma(3),
+            dma(6),
+            dma(3),
+            dma(6),
+            dma(3),
+            dma(6),
+            dma(3),
+        )
+
+    def __call__(self, ins, outs, scratch):
+        self.lefts, self.rights, self.outs = ins[:4], ins[4:], outs
+        (
+            self.x_buf,
+            self.y_buf,
+            self.s1,
+            self.own,
+            self.r1,
+            self.s2x,
+            self.s2y,
+            self.top,
+            self.low,
+            self.r2x,
+            self.r2y,
+            self.s3,
+            self.kept,
+            self.r3,
+            self.tile,
+            self.x_sem,
+            self.y_sem,
+            self.s1_sem,
+            self.r1_sem,
+            self.s2x_sem,
+            self.r2x_sem,
+            self.s2y_sem,
+            self.r2y_sem,
+            self.s3y_sem,
+            self.r3y_sem,
+            self.s3x_sem,
+            self.r3x_sem,
+            self.out_sem,
+        ) = scratch
+        item, seq = lax.axis_index("item"), lax.axis_index("seq")
+        self.core, self.x, self.y = item % 2, item // 2, seq
+        self.to_core = {"item": item + 1 - 2 * self.core}
+        self.to_x = {"item": item + 2 - 4 * self.x}
+        self.to_y = {"seq": 1 - seq}
+        return self
+
+    def greet(self, barrier):
+        for to in (self.to_core, self.to_x, self.to_y):
+            pl.semaphore_signal(barrier, inc=1, device_id=to, device_id_type=MESH)
+
+
+    def left_copy(self, left):
+        slot = list(self.phases).index(left) % 2
+        return pltpu.make_async_copy(self.lefts[left], self.x_buf.at[slot], self.x_sem.at[slot])
+
+    def right_copy(self, m, act):
+        for number, start, stop, _, _ in self.table:
+
+            @pl.when((m >= start) & (m < stop))
+            def _():
+                cols = pl.ds(pl.multiple_of((m - start) * self.block, self.block), self.block)
+                act(
+                    pltpu.make_async_copy(
+                        self.rights[number].at[:, cols], self.y_buf.at[m % 2], self.y_sem.at[m % 2]
+                    )
+                )
+
+    def out_copy(self, m, act):
+        for _, start, stop, result, place in self.table:
+
+            @pl.when((m >= start) & (m < stop))
+            def _():
+                cols = pl.ds(
+                    pl.multiple_of(place + (m - start) * self.block, self.block), self.block
+                )
+                out = self.outs[result]
+                out = out.at[:, cols] if self.across[result] else out.at[cols, :]
+                act(pltpu.make_async_copy(self.tile.at[m % 3], out, self.out_sem.at[m % 3]))
+
+    def remote(self, src, dst, send, recv, to):
+        return pltpu.make_async_remote_copy(
+            src_ref=src, dst_ref=dst, send_sem=send, recv_sem=recv, device_id=to, device_id_type=MESH
+        )
+
+    def first_copy(self, m):
+        return self.remote(
+            self.s1.at[m % 3],
+            self.r1.at[m % 4],
+            self.s1_sem.at[m % 3],
+            self.r1_sem.at[m % 4],
+            self.to_core,
+        )
+
+    def second_copies(self, m):
+        return (
+            self.remote(
+                self.s2x.at[m % 3],
+                self.r2x.at[m % 6],
+                self.s2x_sem.at[m % 3],
+                self.r2x_sem.at[m % 6],
+                self.to_x,
+            ),
+            self.remote(
+                self.s2y.at[m % 3],
+                self.r2y.at[m % 6],
+                self.s2y_sem.at[m % 3],
+                self.r2y_sem.at[m % 6],
+                self.to_y,
+            ),
+        )
+
+    def third_copies(self, m):
+        return (
+            self.remote(
+                self.s3.at[m % 3, 0],
+                self.r3.at[m % 6, 0],
+                self.s3y_sem.at[m % 3],
+                self.r3y_sem.at[m % 6],
+                self.to_y,
+            ),
+            self.remote(
+                self.s3.at[m % 3, 1],
+                self.r3.at[m % 6, 1],
+                self.s3x_sem.at[m % 3],
+                self.r3x_sem.at[m % 6],
+                self.to_x,
+            ),
+        )
+
+    def first(self):
+        for left in list(self.phases)[:2]:
+            self.left_copy(left).start()
+        self.right_copy(0, lambda copy: copy.start())
+
+    def step(self, t):
+        for stage, lag in ((self.fourth, 8), (self.third, 5), (self.second, 2), (self.multiply, 0)):
+            m = t - lag
+
+            @pl.when((m >= 0) & (m < self.chunks))
+            def _():
+                stage(m)
+
+    def multiply(self, m):
+        order = list(self.phases)
+        for number, left in enumerate(order):
+
+            @pl.when(m == self.phases[left])
+            def _():
+                self.left_copy(left).wait()
+                if 1 <= number < len(order) - 1:
+                    self.left_copy(order[number + 1]).start()
+
+        @pl.when(m + 1 < self.chunks)
+        def _():
+            self.right_copy(m + 1, lambda copy: copy.start())
+
+        self.right_copy(m, lambda copy: copy.wait())
+
+        @pl.when(m >= 3)
+        def _():
+            self.first_copy(m - 3).wait_send()
+
+        phase = sum((m >= start).astype(jnp.int32) for start in self.phases.values()) - 1
+        turned = self.y_buf[m % 2].T
+        wide = 2 * self.block
+
+        def product(x, core):
+            cols = pl.ds(pl.multiple_of(x * 2 * wide + core * wide, wide), wide)
+            return mm(turned, self.x_buf[phase % 2, :, cols])
+
+        for x in range(2):
+            self.s1[m % 3, x] = product(x, 1 - self.core).astype(jnp.bfloat16)
+        self.first_copy(m).start()
+        for x in range(2):
+            self.own[m % 3, x] = product(x, self.core)
+
+    def second(self, m):
+        half = self.block // 2
+
+        @pl.when(m >= 3)
+        def _():
+            for copy in self.second_copies(m - 3):
+                copy.wait_send()
+
+        self.first_copy(m).wait_recv()
+        slot = m % 3
+        here, there = self.x, 1 - self.x
+        mine = pl.ds(pl.multiple_of(self.y * self.block, self.block), self.block)
+        others = pl.ds(pl.multiple_of((1 - self.y) * self.block, self.block), self.block)
+        added = lambda x, rows, cols: (
+            self.own[slot, x, rows, cols] + self.r1[m % 4, x, rows, cols].astype(jnp.float32)
+        )
+        upper, lower, every = pl.ds(0, half), pl.ds(half, half), pl.ds(0, 2 * self.block)
+        self.s2x[slot] = added(there, upper, every).astype(jnp.bfloat16)
+        for x in range(2):
+            self.s2y[slot, x] = added(x, lower, others).astype(jnp.bfloat16)
+        for copy in self.second_copies(m):
+            copy.start()
+        self.top[slot] = added(here, upper, every)
+        for x in range(2):
+            self.low[slot, x] = added(x, lower, mine)
+
+    def third(self, m):
+        @pl.when(m >= 3)
+        def _():
+            for copy in self.third_copies(m - 3):
+                copy.wait_send()
+
+        for copy in self.second_copies(m):
+            copy.wait_recv()
+        slot, got = m % 3, m % 6
+        mine = pl.ds(pl.multiple_of(self.y * self.block, self.block), self.block)
+        others = pl.ds(pl.multiple_of((1 - self.y) * self.block, self.block), self.block)
+        top = lambda cols: self.top[slot, :, cols] + self.r2x[got, :, cols].astype(jnp.float32)
+        low = lambda x: self.low[slot, x] + self.r2y[got, x].astype(jnp.float32)
+        self.s3[slot, 0] = top(others).astype(jnp.bfloat16)
+        self.s3[slot, 1] = low(1 - self.x).astype(jnp.bfloat16)
+        for copy in self.third_copies(m):
+            copy.start()
+        self.kept[slot, 0] = top(mine)
+        self.kept[slot, 1] = low(self.x)
+
+    def fourth(self, m):
+        @pl.when(m >= 3)
+        def _():
+            self.out_copy(m - 3, lambda copy: copy.wait())
+
+        for copy in self.third_copies(m):
+            copy.wait_recv()
+        slot, half = m % 3, self.block // 2
+        total = self.kept[slot] + self.r3[m % 6].astype(jnp.float32)
+        total = total.reshape(self.block, self.block)
+        across = jnp.zeros((), jnp.bool_)
+        for _, start, stop, result, _ in self.table:
+            if self.across[result]:
+                across = across | ((m >= start) & (m < stop))
+
+        @pl.when(across)
+        def _():
+            self.tile[slot] = total.T
+
+        @pl.when(jnp.logical_not(across))
+        def _():
+            self.tile[slot] = total
+
+        self.out_copy(m, lambda copy: copy.start())
+
+    def settle(self):
+        for m in range(self.chunks - 3, self.chunks):
+            self.first_copy(m).wait_send()
+            for copy in self.second_copies(m) + self.third_copies(m):
+                copy.wait_send()
+            self.out_copy(jnp.int32(m), lambda copy: copy.wait())
 
 
 def small_kernel(stages, shared, own_ref, out_ref, sent, got, send_sem, recv_sem):
@@ -544,6 +917,24 @@
         compiler_params=pltpu.CompilerParams(collective_id=number, has_side_effects=True),
         name="small_sum",
     )(values)
+
+
+def gradients_over(group, lefts, columns):
+    over_rows = lambda left, right: mm(left, right, (((0,), (0,)), ((), ()))).astype(jnp.bfloat16)
+    parts = [[] for _ in range(4)]
+    for left, right, result, _ in columns:
+        across = result in (0, 3)
+        product = over_rows(lefts[left], right) if across else over_rows(right, lefts[left])
+        parts[result].append(product)
+    return [
+        lax.psum_scatter(
+            jnp.concatenate(part, axis=1),
+            group,
+            scatter_dimension=0 if result in (0, 3) else 1,
+            tiled=True,
+        ).astype(jnp.float32)
+        for result, part in enumerate(parts)
+    ]
 
 
 def body(
@@ -623,15 +1014,8 @@
         finish_branch,
         "mid_sum",
     )
-    over_rows = lambda left, right: mm(left, right, (((0,), (0,)), ((), ())))
-    spread = lambda grad, axis: lax.psum_scatter(
-        grad.astype(jnp.bfloat16), group, scatter_dimension=axis, tiled=True
-    ).astype(jnp.float32)
-    down_grad = spread(over_rows(act_low, grad_down), 1)
-    up_grad = spread(over_rows(mid_low, grad_pre), 0)
-    out_grad = spread(over_rows(attended, grad_branch), 1)
     grad_attended = mm(grad_branch, out_full, NT).astype(jnp.bfloat16)
-    (hidden_out,) = line_sum(
+    hidden_out, dq, dk, dv, dks, dvs = line_sum(
         3,
         mp_count,
         [act_low],
@@ -642,11 +1026,22 @@
         0,
         finish_out,
         "down_sum",
+        AttendBack(facts, q, *tables, grad_attended, log_total),
     )
-
-    dq, dk, dv, dks, dvs = attend_back(facts, q, *tables, grad_attended, log_total)
     dk, dv = keys_back(jnp.stack([dk, dv]), jnp.stack([dks, dvs]), rows, lengths, seq_count)
-    grad_input, pre_sums = line_sum(
+    lefts = (mid_low, grad_down, grad_branch, normed)
+    columns = (
+        (0, grad_pre, 0, 0),
+        (1, act_low, 1, 0),
+        (2, attended, 2, 0),
+        (3, dq, 3, 0),
+        (3, dk, 3, width),
+        (3, dv, 3, 2 * width),
+    )
+    spread = Nothing()
+    if (item_count, seq_count) == (4, 2):
+        spread = Spread(lefts, columns)
+    grad_input, pre_sums, *weight_grads = line_sum(
         4,
         mp_count,
         [dq, dk, dv],
@@ -657,8 +1052,11 @@
         2,
         finish_input,
         "input_sum",
+        spread,
     )
-    qkv_grad = spread(over_rows(normed, jnp.concatenate([dq, dk, dv], axis=1)), 0)
+    if not weight_grads:
+        weight_grads = gradients_over(group, lefts, columns)
+    up_grad, down_grad, out_grad, qkv_grad = weight_grads
     total = lambda value: jnp.sum(value.astype(jnp.float32), axis=0)
     features = hidden.shape[1]
     qv_sums = jnp.concatenate([total(dq), total(dv)])

time: 888 us -> 803 us (0.904)
  matrix products: 117 us -> 63.6 us
  Pallas kernels: 645 us -> 622 us
    dot_general x10 -> x6, matrix products: 117 us -> 63.6 us  [mm(): lax.dot_general(left, right, dims, preferred_element_type=jnp.float32)]
    pallas_call x5 -> x4, Pallas kernels: 600 us -> 577 us  [line_sum(): pl.pallas_call(functools.partial(line_kernel, count, half, dims, len(left...]
  transfers between devices with their start and end apart: 10 -> 6, of which waited for: 2 -> 3; matrix products, arithmetic and copies ran while one was open for 14% -> 6% of each run, Pallas kernels for 57% -> 21%
where the time goes in v3:
time: 803 us; the launch traced here: 795 us
  Pallas kernels  622 us (77%)
  matrix products  63.6 us (8%)
  waiting for transfers between devices  37.4 us (5%)
  other arithmetic  25 us (3%)
  local copies, waits for them, and re-layouts  24.9 us (3%)
  between operations  17.2 us (2%)
    pallas_call x4, Pallas kernels, line_sum(): pl.pallas_call(functools.partial(line_kernel, count, half, dims, len(left...  577 us
    dot_general x6, matrix products, mm(): lax.dot_general(left, right, dims, preferred_element_type=jnp.float32)  63.6 us
    all_gather x4, waiting for transfers between devices, body(): lax.all_gather(weight, group, axis=axis, tiled=True)  32.4 us
    pallas_call x1, Pallas kernels, attend(): pl.pallas_call(functools.partial(attend_kernel, query_block(rows), rows =...  25.5 us
    pallas_call x1, Pallas kernels, small_sum(): pl.pallas_call(functools.partial(small_kernel, stages, shared), in_specs=...  19.4 us
    unnamed x50, local copies, waits for them, and re-layouts  16.4 us
  transfers between devices with their start and end apart: 6, of which 3 were waited for; matrix products, arithmetic and copies ran while one was open for 6% of the time, Pallas kernels for 21%

profile of v3, /device:TPU:0, one launch (start us, length us, event | category | flops | bytes accessed | tf_op | source)
XLA Modules:
  0.0 794.8 jit_solution(967214027689135217)
XLA Ops:
  7.2 1.4 copy.31
  8.7 1.2 copy.32
  9.9 0.7 all-gather.7.cloned.1.call-update
  10.6 0.7 all-gather.9.cloned.1.call-update
  11.4 0.5 all-gather.11.cloned.1.call-update
  11.9 0.6 constant_dynamic-slice_fusion
  15.3 3.4 convert_reduce_fusion
  18.7 0.5 copy-done.8
  19.2 1.5 fusion.2
  21.1 0.9 convert_reduce_fusion.2
  22.0 4.3 fusion.5.refs_10_
  26.3 32.4 %all-gather.5.cloned.1.call-done.refs_3_ = bf16[2048,1536]{1,0:T(8,128)(2,1)} async-done(((bf16[256,1536]{1,0:T(8,128)(2,1)}), bf16[2048,1536]{1,0:T(8,128)(2,1)}) %all-gather.5.cloned.1.call-update) | async-done | bytes 6291472 | tf_op jit(solution)/shard_map/all_gather | solution.py:962
  58.7 6.2 convolution_convert_fusion.1.k_ref.refs_6_
  65.3 2.9 fusion.7.v_ref.refs_7_
  68.2 3.3 collective-permute-start
  71.6 2.9 fusion.6.q_ref.refs_5_
  74.6 25.5 %attend.1 = (bf16[1280,512]{1,0:T(8,128)(2,1)S(1)}, f32[4,2,1280]{2,1,0:T(2,128)S(1)}) custom-call(s32[3]{0:T(128)S(1)} %pad_add_fusion.facts_ref.refs_4_, bf16[1280,512]{1,0:T(8,128)(2,1)S(1)} %fusion.6.q_ref.refs_5_, bf16[1280,512]{1,0:T(8,128)(2,1)S(1)} %convolution_convert_fusion.1.k_ref.refs_6_, bf16[1280,512]{1,0:T(8,128)(2,1)S(1)} %fusion.7.v_ref.refs_7_, ...), custom_call_target="tpu_custom_call" | custom-call | flops 3355443200 | bytes 5242880 | tf_op jit(solution)/shard_map/attend/pallas_call | solution.py:107
  100.1 1.0 copy-done.2
  101.2 1.1 copy-done.6
  102.3 0.6 copy-done.7
  102.9 138.8 %out_sum.1 = (bf16[1280,2048]{1,0:T(8,128)(2,1)}, f32[640,2048]{1,0:T(8,128)}) custom-call(bf16[1280,512]{1,0:T(8,128)(2,1)} %copy-done.2, bf16[512,2048]{1,0:T(8,128)(2,1)} %all-gather.7.cloned.1.call-done.refs_1_, bf16[1280,2048]{1,0:T(8,128)(2,1)} %bitcast.63, f32[1,2048]{1,0:T(1,128)} %bitcast.89, f32[1,2048]{1,0:T(1,128)} %bitcast.91, f32[1,2048]{1,0:T(1,128)} %bitcast.90), custom_call_target="tpu_custom_call" | custom-call | flops 2684354560 | bytes 10485760 | tf_op jit(solution)/shard_map/out_sum/pallas_call | solution.py:397
  241.8 20.4 %multiply_convert_fusion.1 = (bf16[1280,2048]{1,0:T(8,128)(2,1)}, f32[1280,2048]{1,0:T(8,128)}) fusion(f32[2048]{0:T(1024)S(1)} %copy-done.21, bf16[1280,2048]{1,0:T(8,128)(2,1)} %get-tuple-element.34.refs_7_, bf16[2048,2048]{1,0:T(8,128)(2,1)} %all-gather.9.cloned.1.call-done.refs_1_), kind=kOutput, calls=%fused_computation.11 | convolution fusion | flops 10763632640 | bytes 29368320 | tf_op jit(solution)/shard_map/dot_general | solution.py:32
  262.2 24.1 %convert_reduce_fusion.1 = (f32[2048]{0:T(1024)S(1)}, bf16[1280,2048]{1,0:T(8,128)(2,1)}) fusion(bf16[2048,2048]{1,0:T(8,128)(2,1)} %all-gather.11.cloned.1.call-done.refs_1_, bf16[1,1280,2048]{2,1,0:T(8,128)(2,1)} %param.16, f32[1280,2048]{1,0:T(8,128)} %get-tuple-element.96, f32[2048]{0:T(1024)S(1)} %copy-done.21), kind=kOutput, calls=%fused_computation.8 | convolution fusion | flops 10792466432 | bytes 29376512 | tf_op jit(solution)/shard_map/dot_general | solution.py:32
  286.2 147.5 %mid_sum.1 = (bf16[1280,2048]{1,0:T(8,128)(2,1)}, f32[640,2048]{1,0:T(8,128)}, f32[3,8,2048]{2,1,0:T(8,128)}) custom-call(bf16[1280,2048]{1,0:T(8,128)(2,1)} %get-tuple-element.98.refs_0_.refs_11_, bf16[2048,2048]{1,0:T(8,128)(2,1)} %all-gather.9.cloned.1.call-done.refs_1_, f32[640,2048]{1,0:T(8,128)} %get-tuple-element.35.refs_2_, ...), custom_call_target="tpu_custom_call" | custom-call | flops 10737418240 | bytes 10485760 | tf_op jit(solution)/shard_map/mid_sum/pallas_call | solution.py:397
  433.7 7.1 convolution_convert_fusion.refs_10_
  440.8 144.8 %down_sum.1 = (bf16[1280,2048]{1,0:T(8,128)(2,1)}, bf16[1280,512]{1,0:T(8,128)(2,1)}, bf16[1280,512]{1,0:T(8,128)(2,1)}, bf16[1280,512]{1,0:T(8,128)(2,1)}, f32[64,512]{1,0:T(8,128)}, /*index=5*/f32[64,512]{1,0:T(8,128)}) custom-call(bf16[1280,2048]{1,0:T(8,128)(2,1)} %get-tuple-element.95.refs_0_.refs_12_, ...), custom_call_target="tpu_custom_call" | custom-call | flops 10737418240 | bytes 10485760 | tf_op jit(solution)/shard_map/down_sum/pallas_call | solution.py:397
  585.7 1.0 pad_maximum_fusion.1
  586.7 1.3 collective-permute-start.1
  588.0 2.0 pad_maximum_fusion
  590.0 1.6 convert_reduce_fusion.4
  591.6 3.0 collective-permute-done.1
  594.6 0.9 add_convert_fusion
  595.5 0.7 dynamic_update_slice.3
  596.5 1.7 slice_bitcast_fusion
  598.1 145.9 %input_sum.1 = (bf16[1280,2048]{1,0:T(8,128)(2,1)}, f32[2,8,2048]{2,1,0:T(8,128)}, f32[256,2048]{1,0:T(8,128)}, f32[2048,256]{1,0:T(8,128)}, f32[512,256]{1,0:T(8,128)}, /*index=5*/f32[256,1536]{1,0:T(8,128)}) custom-call(bf16[1280,512]{1,0:T(8,128)(2,1)} %get-tuple-element.39.refs_0_.refs_14_, bf16[1280,512]{1,0:T(8,128)(2,1)} %get-tuple-element.81.refs_1_.refs_15_, ...), custom_call_target="tpu_custom_call" | custom-call | flops 8053063680 | bytes 10485760 | tf_op jit(solution)/shard_map/input_sum/pallas_call | solution.py:397
  744.0 1.0 reduce_sum.75
  745.0 0.7 concatenate.7.own_ref
  745.7 19.4 %small_sum.1 = f32[8,2048]{1,0:T(8,128)} custom-call(f32[8,2048]{1,0:T(8,128)} %concatenate.7.own_ref), custom_call_target="tpu_custom_call" | custom-call | tf_op jit(solution)/shard_map/small_sum/pallas_call | solution.py:906
  765.1 1.8 fusion.14
  766.9 0.8 slice_reduce_fusion
  767.7 0.6 reshape.85
  768.3 8.1 %bitcast_convert_fusion = f32[1,1280,2048]{2,1,0:T(8,128)} fusion(bf16[1280,2048]{1,0:T(8,128)(2,1)} %get-tuple-element.45), kind=kLoop, calls=%fused_computation.14 | loop fusion | flops 2621440 | bytes 15728640 | tf_op jit(solution)/shard_map/broadcast_in_dim | solution.py:1082
  776.4 0.5 copy.33
  776.9 1.6 copy.34
  778.5 5.8 copy.40
  784.3 0.8 copy.41
  785.1 1.3 copy.42
  786.5 1.3 copy.43
  (60 shorter events, 1.6 us)
Async XLA Ops:
  7.2 4.8 copy-start.20
  7.2 8.0 %copy-start.19 = (f32[2,512]{1,0:T(2,128)S(1)}, f32[2,512]{1,0:T(2,128)}, u32[]{:S(2)}) copy-start(f32[2,512]{1,0:T(2,128)} %param.21) | copy-start | bytes 12292
  7.2 51.5 %all-gather.5.cloned.1.call-start = ((), (), s32[]{:S(2)}) async-start(), calls=%async_computation | async-start | bytes 7077888 | tf_op jit(solution)/shard_map/all_gather | solution.py:962
  9.8 93.0 %all-gather.7.cloned.1.call-start = ((), (), s32[]{:S(2)}) async-start(), calls=%async_computation.1 | async-start | bytes 2359296 | tf_op jit(solution)/shard_map/all_gather | solution.py:962
  10.6 231.2 %all-gather.9.cloned.1.call-start = ((), (), s32[]{:S(2)}) async-start(), calls=%async_computation.2 | async-start | bytes 9437184 | tf_op jit(solution)/shard_map/all_gather | solution.py:962
  11.3 250.9 %all-gather.11.cloned.1.call-start = ((), (), s32[]{:S(2)}) async-start(), calls=%async_computation.3 | async-start | bytes 9437184 | tf_op jit(solution)/shard_map/all_gather | solution.py:962
  15.1 4.0 copy-start.8
  15.2 59.3 %copy-start.5 = (s32[3]{0:T(128)}, s32[3]{0:T(128)S(1)}, u32[]{:S(2)}) copy-start(s32[3]{0:T(128)S(1)} %pad_add_fusion.facts_ref.refs_4_) | copy-start | bytes 40
  15.2 5.9 copy-start.9
  19.2 2.8 copy-start.17
  19.2 2.8 copy-start.18
  58.7 6.2 copy-start.10
  58.7 6.5 copy-start.11
  64.9 9.7 %copy-start = (bf16[1280,512]{1,0:T(8,128)(2,1)}, bf16[1280,512]{1,0:T(8,128)(2,1)S(1)}, u32[]{:S(2)}) copy-start(bf16[1280,512]{1,0:T(8,128)(2,1)S(1)} %convolution_convert_fusion.1.k_ref.refs_6_) | copy-start | bytes 3932164
  68.2 6.4 copy-start.1
  68.2 6.3 collective-permute-start
  74.5 25.6 %copy-start.3 = (bf16[64,512]{1,0:T(8,128)(2,1)}, bf16[64,512]{1,0:T(8,128)(2,1)S(1)}, u32[]{:S(2)}) copy-start(bf16[64,512]{1,0:T(8,128)(2,1)S(1)} %get-tuple-element.82.vs_ref.refs_9_) | copy-start | bytes 196612
  74.6 25.6 %copy-start.4 = (bf16[64,512]{1,0:T(8,128)(2,1)}, bf16[64,512]{1,0:T(8,128)(2,1)S(1)}, u32[]{:S(2)}) copy-start(bf16[64,512]{1,0:T(8,128)(2,1)S(1)} %get-tuple-element.83.ks_ref.refs_8_) | copy-start | bytes 196612
  100.1 1.1 copy-start.2
  101.2 1.1 copy-start.6
  102.3 0.6 copy-start.7
  102.9 138.9 %copy-start.21 = (f32[2048]{0:T(1024)S(1)}, f32[2048]{0:T(1024)}, u32[]{:S(2)}) copy-start(f32[2048]{0:T(1024)} %param.27) | copy-start | bytes 24580
  585.7 4.3 copy-start.16
  586.7 7.9 collective-permute-start.1
  768.3 8.1 %copy-start.14 = (f32[256,1536]{1,0:T(8,128)S(1)}, f32[256,1536]{1,0:T(8,128)}, u32[]{:S(2)}) copy-start(f32[256,1536]{1,0:T(8,128)} %get-tuple-element.48) | copy-start | bytes 4718596
  778.5 5.9 copy-start.15
  778.5 6.7 copy-start.13
  784.3 2.1 copy-start.12
Sparse Core Ops, SparseCore 0:
  10.5 48.2 all-gather.4
  60.6 28.8 all-gather.6
  91.4 54.3 all-gather.8
  147.6 55.9 all-gather.10

commit v4 on v3

--- a/solution.py
+++ b/solution.py
@@ -17,6 +17,8 @@
 PAIR = 2 * HDIM
 PIECE = 32
 SKEW = 2
+SECOND_STREAM = 19
+WEIGHTS_READY = 16
 MIB = 1 << 20
 MESH = pl.DeviceIdType.MESH
 MASKED = -1e30
@@ -288,7 +290,7 @@
                 def _():
                     self.back(flow, j, False).start()
 
-        for flow in range(2):
+        for flow in range(2 if self.multiply else 0):
             k = t - SKEW * self.place(flow)
             g = k // self.per_group + 1
 
@@ -432,30 +434,6 @@
 
 def fold(values):
     return jnp.sum(values.reshape(-1, 8, values.shape[-1]), axis=0)
-
-
-def finish_mid(flow, k, total, extras, owned, accs):
-    hidden, bias, gain, shift = extras
-    (residual_ref,) = owned
-    half = residual_ref.shape[0]
-    residual = hidden[piece_rows(flow, k, half), :].astype(jnp.float32) + total + bias[...]
-    residual_ref[piece_rows(0, k, half), :] = residual
-    return norm_stats(residual)[0] * gain[...] + shift[...]
-
-
-def finish_branch(flow, k, total, extras, owned, accs):
-    residual, cotangent, gain = extras
-    (grad_ref,) = owned
-    (acc,) = accs
-    half = grad_ref.shape[0]
-    normed, inverse = norm_stats(residual[piece_rows(0, k, half), :])
-    grad = cotangent[piece_rows(flow, k, half), :].astype(jnp.float32)
-    grad = grad + norm_back(total, normed, inverse, gain[...])
-    grad_ref[piece_rows(0, k, half), :] = grad
-    acc[0] += fold(total * normed)
-    acc[1] += fold(total)
-    acc[2] += fold(grad)
-    return grad
 
 
 def finish_input(flow, k, total, extras, owned, accs):
@@ -865,6 +843,416 @@
             self.out_copy(jnp.int32(m), lambda copy: copy.wait())
 
 
+class Gather:
+    others = 3
+
+    def __init__(self, shards, fulls, sems):
+        self.shards, self.fulls = shards, fulls
+        self.sent, self.got, self.local = sems
+        item, seq = lax.axis_index("item"), lax.axis_index("seq")
+        self.core, self.x, self.y = item % 2, item // 2, seq
+        self.to_core = {"item": item + 1 - 2 * self.core}
+        self.to_x = {"item": item + 2 - 4 * self.x}
+        self.to_y = {"seq": 1 - seq}
+
+    @staticmethod
+    def sems():
+        dma = lambda *shape: pltpu.SemaphoreType.DMA(shape)
+        return [dma(2, 9), dma(2, 9), dma(2)]
+
+    def greet(self, barrier):
+        for to in (self.to_core, self.to_x, self.to_y):
+            pl.semaphore_signal(barrier, inc=1, device_id=to, device_id_type=MESH)
+
+    def spot(self, w, x, core, y, part=None):
+        size = self.shards[w].shape[w]
+        at = pl.ds(pl.multiple_of(((2 * x + core) * 2 + y) * size, size), size)
+        if w == 0:
+            if part is not None:
+                half = size // 2
+                start = ((2 * x + core) * 2 + y) * size + part * half
+                at = pl.ds(pl.multiple_of(start, half), half)
+            return self.fulls[0].at[at, :]
+        rows = self.fulls[1].shape[0]
+        if part is not None:
+            return self.fulls[1].at[pl.ds(part * (rows // 2), rows // 2), at]
+        return self.fulls[1].at[:, at]
+
+    def message(self, w, number, src, dst, to):
+        return pltpu.make_async_remote_copy(
+            src_ref=src,
+            dst_ref=dst,
+            send_sem=self.sent.at[w, number],
+            recv_sem=self.got.at[w, number],
+            device_id=to,
+            device_id_type=MESH,
+        )
+
+    def messages(self, w):
+        c, x, y = self.core, self.x, self.y
+        own, spot = self.shards[w].at[...], functools.partial(self.spot, w)
+        plan = (
+            (own, spot(x, c, y), spot(x, 1 - c, y), self.to_core),
+            (own, spot(x, c, y), spot(1 - x, c, y), self.to_x),
+            (own, spot(x, c, y), spot(x, c, 1 - y), self.to_y),
+            (None, spot(1 - x, c, y, 0), spot(1 - x, c, 1 - y, 0), self.to_y),
+            (None, spot(x, c, 1 - y, 1), spot(1 - x, c, 1 - y, 1), self.to_x),
+            (None, spot(1 - x, c, y), spot(1 - x, 1 - c, y), self.to_core),
+            (None, spot(x, c, 1 - y), spot(x, 1 - c, 1 - y), self.to_core),
+            (None, spot(1 - x, c, 1 - y, 0), spot(1 - x, 1 - c, 1 - y, 0), self.to_core),
+            (None, spot(1 - x, c, 1 - y, 1), spot(1 - x, 1 - c, 1 - y, 1), self.to_core),
+        )
+        return [
+            (
+                self.message(w, number, out if src is None else src, out, to),
+                self.message(w, number, landing, landing, to),
+            )
+            for number, (src, out, landing, to) in enumerate(plan)
+        ]
+
+    def send(self, w, numbers):
+        messages = self.messages(w)
+        for number in numbers:
+            messages[number][0].start()
+
+    def receive(self, w, numbers):
+        messages = self.messages(w)
+        for number in numbers:
+            messages[number][1].wait_recv()
+
+    def mine(self, w):
+        return pltpu.make_async_copy(
+            self.shards[w], self.spot(w, self.x, self.core, self.y), self.local.at[w]
+        )
+
+    def first(self):
+        for w in range(2):
+            self.mine(w).start()
+
+    def begin(self):
+        for w in range(2):
+            self.send(w, (1, 2, 0))
+
+    def step(self, t):
+        for w, at in ((0, 5), (1, 9)):
+
+            @pl.when(t == at)
+            def _():
+                self.receive(w, (1, 2))
+                self.send(w, (3, 4, 5, 6))
+
+        for w, at in ((0, 12), (1, 15)):
+
+            @pl.when(t == at)
+            def _():
+                self.receive(w, (3, 4))
+                self.send(w, (7, 8))
+
+        @pl.when(t == WEIGHTS_READY)
+        def _():
+            for w in range(2):
+                self.receive(w, (0, 5, 6, 7, 8))
+                self.mine(w).wait()
+
+    def settle(self):
+        for w in range(2):
+            for out, _ in self.messages(w):
+                out.wait_send()
+
+
+class Load:
+    others = 0
+
+    def __init__(self, shards, fulls, sems):
+        self.copies = [
+            pltpu.make_async_copy(shard, full, sems[2].at[w])
+            for w, (shard, full) in enumerate(zip(shards, fulls))
+        ]
+
+    sems = Gather.sems
+
+    def greet(self, barrier):
+        pass
+
+    def first(self):
+        for copy in self.copies:
+            copy.start()
+
+    def begin(self):
+        pass
+
+    def step(self, t):
+        @pl.when(t == WEIGHTS_READY)
+        def _():
+            for copy in self.copies:
+                copy.wait()
+
+    def settle(self):
+        pass
+
+
+def ffn_kernel(
+    count,
+    half,
+    weights_job,
+    attended,
+    out_w,
+    out_bias,
+    mid_gain,
+    mid_shift,
+    up_bias,
+    hidden,
+    cotangent,
+    up_shard,
+    down_shard,
+    mid,
+    act,
+    grad_pre,
+    residual_out,
+    branch,
+    grad_out,
+    down_out,
+    acc,
+    acc_up,
+    part1,
+    moving1,
+    part2,
+    moving2,
+    rows_in,
+    residual,
+    up,
+    down,
+    mid_in,
+    cot_in,
+    act_out,
+    pre_out,
+    *sems,
+):
+    sems = list(sems)
+    take = lambda n: [sems.pop(0) for _ in range(n)]
+    sems1, sems2, weight_sems = take(5), take(5), take(3)
+    in_sem, residual_sem, grad_sem, mid_sem, cot_sem, act_sem, pre_sem, down_sem = sems
+    me = lax.axis_index("mp")
+    group = part2.shape[2]
+    per_group = group // PIECE
+    pieces = half // PIECE
+    last = count - 1
+    weights = weights_job((up_shard, down_shard), (up, down), weight_sems)
+    piece = lambda k: pl.ds(pl.multiple_of(k * PIECE, PIECE), PIECE)
+    owner = (me == 0) | (me == last)
+    my_flow = jnp.where(me == 0, 0, 1)
+
+    def piece_in(source, k, flow):
+        return pltpu.make_async_copy(
+            source.at[pl.ds(flow * half + k * PIECE, PIECE)], rows_in.at[piece(k)], in_sem.at[k]
+        )
+
+    def residual_copy(k):
+        return pltpu.make_async_copy(
+            residual.at[piece(k)], residual_out.at[piece(k)], residual_sem.at[k]
+        )
+
+    def grad_copy(k):
+        return pltpu.make_async_copy(residual.at[piece(k)], grad_out.at[piece(k)], grad_sem.at[k])
+
+    def finish_first(flow, k, total):
+        piece_in(hidden, k, flow).wait()
+        value = rows_in[piece(k), :].astype(jnp.float32) + total + out_bias[...]
+        residual[piece(k), :] = value
+        residual_copy(k).start()
+        piece_in(cotangent, k, flow).start()
+        return norm_stats(value)[0] * mid_gain[...] + mid_shift[...]
+
+    def finish_second(flow, k, total):
+        piece_in(cotangent, k, flow).wait()
+        residual_copy(k).wait()
+        normed, inverse = norm_stats(residual[piece(k), :])
+        grad = rows_in[piece(k), :].astype(jnp.float32)
+        grad = grad + norm_back(total, normed, inverse, mid_gain[...])
+        residual[piece(k), :] = grad
+        grad_copy(k).start()
+        acc[0] += fold(total * normed)
+        acc[1] += fold(total)
+        acc[2] += fold(grad)
+        return grad
+
+    multiply = group_product([attended], out_w, NN, half, part1.shape[2])
+    line1 = Line(count, half, multiply, finish_first, mid, part1, moving1, sems1)
+    line2 = Line(count, half, None, finish_second, branch, part2, moving2, sems2)
+
+    def group_rows(flow, g):
+        return pl.ds(pl.multiple_of(flow * half + g * group, 16), group)
+
+    def mid_fetch(flow, g, here):
+        rows = pl.ds(pl.multiple_of(g * group, 16), group)
+        source = moving1.at[flow, rows] if here else mid.at[group_rows(flow, g)]
+        return pltpu.make_async_copy(source, mid_in.at[flow], mid_sem.at[flow])
+
+    def cot_fetch(flow, g):
+        return pltpu.make_async_copy(
+            cotangent.at[group_rows(flow, g)], cot_in.at[flow], cot_sem.at[flow]
+        )
+
+    def act_copy(flow, g):
+        return pltpu.make_async_copy(
+            act_out.at[flow], act.at[group_rows(flow, g)], act_sem.at[flow]
+        )
+
+    def pre_copy(flow, g):
+        return pltpu.make_async_copy(
+            pre_out.at[flow], grad_pre.at[group_rows(flow, g)], pre_sem.at[flow]
+        )
+
+    def products(flow, g):
+        mid_fetch(flow, g, False).wait()
+        cot_fetch(flow, g).wait()
+
+        @pl.when(g > 0)
+        def _():
+            act_copy(flow, g - 1).wait()
+            pre_copy(flow, g - 1).wait()
+
+        block = 512
+        for number in range(up.shape[1] // block):
+            cols = slice(number * block, (number + 1) * block)
+            value, slope = gelu_parts(mm(mid_in[flow], up[:, cols]) + up_bias[:, cols])
+            act_out[flow, :, cols] = value.astype(jnp.bfloat16)
+            pre = (slope * mm(cot_in[flow], down[cols, :], NT)).astype(jnp.bfloat16)
+            pre_out[flow, :, cols] = pre
+            acc_up[:, cols] += fold(pre.astype(jnp.float32))
+            product = mm(pre, up[:, cols], NT)
+            if number == 0:
+                part2[flow, g % 2] = product
+            else:
+                part2[flow, g % 2] += product
+        act_copy(flow, g).start()
+        pre_copy(flow, g).start()
+
+    barrier = pltpu.get_barrier_semaphore()
+    line1.greet(barrier)
+    weights.greet(barrier)
+    acc[...] = jnp.zeros_like(acc)
+    acc_up[...] = jnp.zeros_like(acc_up)
+    weights.first()
+
+    @pl.when(owner)
+    def _():
+        def one(k, carry):
+            piece_in(hidden, k, my_flow).start()
+            return carry
+
+        lax.fori_loop(0, pieces, one, 0)
+
+    line1.first()
+    line1.meet(barrier, weights.others)
+    weights.begin()
+
+    def step(t, carry):
+        line1.step(t)
+        line2.step(t - SECOND_STREAM)
+        weights.step(t)
+
+        @pl.when(t == WEIGHTS_READY + 1)
+        def _():
+            pltpu.make_async_copy(down, down_out, down_sem.at[0]).start()
+
+        for flow in range(2):
+            place = line1.place(flow)
+            u = t - SECOND_STREAM - SKEW * place
+            fetch = u + 3
+            compute = u + 2
+
+            @pl.when((fetch >= 0) & (fetch % per_group == 0) & (fetch < pieces))
+            def _():
+                g = fetch // per_group
+                cot_fetch(flow, g).start()
+
+                @pl.when(place == last)
+                def _():
+                    mid_fetch(flow, g, True).start()
+
+                @pl.when(place < last)
+                def _():
+                    mid_fetch(flow, g, False).start()
+
+            @pl.when((compute >= 0) & (compute % per_group == 0) & (compute < pieces))
+            def _():
+                products(flow, compute // per_group)
+
+        return carry
+
+    lax.fori_loop(0, SECOND_STREAM + line2.steps, step, 0)
+    line1.settle()
+    line2.settle()
+    weights.settle()
+    pltpu.make_async_copy(down, down_out, down_sem.at[0]).wait()
+    for flow in range(2):
+        act_copy(flow, pieces // per_group - 1).wait()
+        pre_copy(flow, pieces // per_group - 1).wait()
+
+    @pl.when(owner)
+    def _():
+        def one(k, carry):
+            grad_copy(k).wait()
+            return carry
+
+        lax.fori_loop(0, pieces, one, 0)
+
+
+def ffn_sums(number, count, weights_job, attended, out_w, vectors, hidden, cotangent, up_w, down_w):
+    rows, features = hidden.shape
+    ff = up_w.shape[1]
+    half = rows // 2
+    pieces = half // PIECE
+    low = lambda *shape: jax.ShapeDtypeStruct(shape, jnp.bfloat16)
+    wide = lambda *shape: jax.ShapeDtypeStruct(shape, jnp.float32)
+    first = Line.scratch(half, features)
+    small = 2 * PIECE if pieces % 2 == 0 else PIECE
+    first[0] = pltpu.VMEM((2, 2, small, features), jnp.float32)
+    second = Line.scratch(half, features)
+    group = second[0].shape[2]
+    dma = lambda n: pltpu.SemaphoreType.DMA((n,))
+    return pl.pallas_call(
+        functools.partial(ffn_kernel, count, half, weights_job),
+        in_specs=[VMEM] * 6 + [ANY] * 4,
+        out_specs=[ANY] * 7 + [VMEM] * 2,
+        out_shape=[
+            low(rows, features),
+            low(rows, ff),
+            low(rows, ff),
+            wide(half, features),
+            low(rows, features),
+            wide(half, features),
+            low(ff, features),
+            wide(3, 8, features),
+            wide(8, ff),
+        ],
+        scratch_shapes=first[:2]
+        + second[:2]
+        + [
+            pltpu.VMEM((half, features), jnp.bfloat16),
+            pltpu.VMEM((half, features), jnp.float32),
+            pltpu.VMEM((features, ff), jnp.bfloat16),
+            pltpu.VMEM((ff, features), jnp.bfloat16),
+            pltpu.VMEM((2, group, features), jnp.bfloat16),
+            pltpu.VMEM((2, group, features), jnp.bfloat16),
+            pltpu.VMEM((2, group, ff), jnp.bfloat16),
+            pltpu.VMEM((2, group, ff), jnp.bfloat16),
+        ]
+        + first[2:]
+        + second[2:]
+        + Gather.sems()
+        + [dma(pieces), dma(pieces), dma(pieces), dma(2), dma(2), dma(2), dma(2), dma(1)],
+        compiler_params=pltpu.CompilerParams(
+            collective_id=number, has_side_effects=True, vmem_limit_bytes=62 * MIB
+        ),
+        cost_estimate=pl.CostEstimate(
+            flops=6 * rows * features * ff, bytes_accessed=30 * rows * features, transcendentals=0
+        ),
+        name="ffn_sums",
+    )(attended, out_w, *vectors, hidden, cotangent, up_w, down_w)
+
+
 def small_kernel(stages, shared, own_ref, out_ref, sent, got, send_sem, recv_sem):
     barrier = pltpu.get_barrier_semaphore()
 
@@ -962,8 +1350,6 @@
     gathered = lambda weight, axis: lax.all_gather(weight, group, axis=axis, tiled=True)
     qkv_full = gathered(qkv_weight.reshape(-1, 3 * width), 0)
     out_full = gathered(out_weight, 1)
-    up_full = gathered(up_weight, 0)
-    down_full = gathered(down_weight, 1)
     hidden = hidden_in[0].astype(jnp.float32)
     lengths = seg_lengths[0]
     rows = hidden.shape[0]
@@ -986,33 +1372,29 @@
     attended, log_total = attend(facts, q, *tables)
 
     row = lambda vector: vector[None, :]
-    mid_low, residual = line_sum(
+    ours = (item_count, seq_count) == (4, 2)
+    grad_down = cotangent[0]
+    (
+        mid_low,
+        act_low,
+        grad_pre,
+        residual,
+        grad_branch,
+        grad_residual,
+        down_full,
+        mid_sums,
+        up_sums,
+    ) = ffn_sums(
         1,
         mp_count,
-        [attended],
+        Gather if ours else Load,
+        attended,
         out_full,
-        NN,
-        [hidden_in[0], row(out_bias), row(mid_gain), row(mid_shift)],
-        1,
-        0,
-        finish_mid,
-        "out_sum",
-    )
-    activated, slope = gelu_parts(mm(mid_low, up_full) + up_bias)
-    act_low = activated.astype(jnp.bfloat16)
-    grad_down = cotangent[0]
-    grad_pre = (slope * mm(grad_down, down_full, NT)).astype(jnp.bfloat16)
-    grad_branch, grad_residual, mid_sums = line_sum(
-        2,
-        mp_count,
-        [grad_pre],
-        up_full,
-        NT,
-        [residual, grad_down, row(mid_gain)],
-        1,
-        3,
-        finish_branch,
-        "mid_sum",
+        (row(out_bias), row(mid_gain), row(mid_shift), row(up_bias)),
+        hidden_in[0],
+        grad_down,
+        up_weight if ours else gathered(up_weight, 0),
+        down_weight if ours else gathered(down_weight, 1),
     )
     grad_attended = mm(grad_branch, out_full, NT).astype(jnp.bfloat16)
     hidden_out, dq, dk, dv, dks, dvs = line_sum(
@@ -1039,7 +1421,7 @@
         (3, dv, 3, 2 * width),
     )
     spread = Nothing()
-    if (item_count, seq_count) == (4, 2):
+    if ours:
         spread = Spread(lefts, columns)
     grad_input, pre_sums, *weight_grads = line_sum(
         4,
@@ -1069,7 +1451,7 @@
                 jnp.sum(mid_sums, axis=1),
                 jnp.sum(pre_sums, axis=1),
                 row(jnp.where(lax.axis_index("mp") == 0, total(grad_down), 0.0)),
-                total(grad_pre).reshape(-1, features),
+                total(up_sums).reshape(-1, features),
                 jnp.pad(qv_sums, (0, -qv_sums.shape[0] % features)).reshape(-1, features),
             ]
         ),

time: 803 us -> 737 us (0.918)
  matrix products: 63.6 us -> 22.2 us
  Pallas kernels: 622 us -> 598 us
    pallas_call x4 -> x2, Pallas kernels: 577 us -> 288 us  [line_sum(): pl.pallas_call(functools.partial(line_kernel, count, half, dims, len(left...]
    pallas_call x0 -> x1, Pallas kernels: none -> 266 us  [ffn_sums(): pl.pallas_call(functools.partial(ffn_kernel, count, half, weights_job), i...]
    dot_general x6 -> x4, matrix products: 63.6 us -> 22.2 us  [mm(): lax.dot_general(left, right, dims, preferred_element_type=jnp.float32)]
    all_gather x4 -> x2, waiting for transfers between devices: 32.4 us -> 29 us  [body(): lax.all_gather(weight, group, axis=axis, tiled=True)]
  transfers between devices with their start and end apart: 6 -> 4, of which waited for: 3 -> 2; matrix products, arithmetic and copies ran while one was open for 6% -> 5% of each run, Pallas kernels for 21% -> 3%
where the time goes in v4:
time: 737 us; the launch traced here: 729 us
  Pallas kernels  598 us (81%)
  waiting for transfers between devices  32.6 us (4%)
  other arithmetic  30.1 us (4%)
  local copies, waits for them, and re-layouts  24.2 us (3%)
  matrix products  22.2 us (3%)
  between operations  17.5 us (2%)
    pallas_call x2, Pallas kernels, line_sum(): pl.pallas_call(functools.partial(line_kernel, count, half, dims, len(left...  288 us
    pallas_call x1, Pallas kernels, ffn_sums(): pl.pallas_call(functools.partial(ffn_kernel, count, half, weights_job), i...  266 us
    all_gather x2, waiting for transfers between devices, body(): lax.all_gather(weight, group, axis=axis, tiled=True)  29 us
    pallas_call x1, Pallas kernels, attend(): pl.pallas_call(functools.partial(attend_kernel, query_block(rows), rows =...  25.5 us
    dot_general x4, matrix products, mm(): lax.dot_general(left, right, dims, preferred_element_type=jnp.float32)  22.2 us
    pallas_call x1, Pallas kernels, small_sum(): pl.pallas_call(functools.partial(small_kernel, stages, shared), in_specs=...  17.9 us
    unnamed x50, local copies, waits for them, and re-layouts  15.7 us
  transfers between devices with their start and end apart: 4, of which 2 were waited for; matrix products, arithmetic and copies ran while one was open for 5% of the time, Pallas kernels for 3%

profile of v4, /device:TPU:0, one launch (start us, length us, event | category | flops | bytes accessed | tf_op | source)
XLA Modules:
  0.0 728.9 jit_solution(17658218746334086947)
XLA Ops:
  7.2 0.0 all-gather.3.cloned.1.call-start
  7.2 1.4 copy.31
  8.6 1.2 copy.32
  9.8 0.0 all-gather.5.cloned.1.call-start
  9.9 0.7 all-gather.5.cloned.1.call-update
  10.6 3.4 convert_reduce_fusion
  14.0 0.6 copy-done.8
  14.7 1.5 fusion.2
  16.2 0.6 constant_dynamic-slice_fusion
  17.5 6.9 fusion.5.refs_10_
  24.4 0.1 pad_add_fusion.facts_ref.refs_4_
  26.4 3.3 convert_reduce_fusion.1
  29.8 29.0 %all-gather.3.cloned.1.call-done.refs_3_ = bf16[2048,1536]{1,0:T(8,128)(2,1)} async-done(((bf16[256,1536]{1,0:T(8,128)(2,1)}), bf16[2048,1536]{1,0:T(8,128)(2,1)}) %all-gather.3.cloned.1.call-update) | async-done | bytes 6291472 | tf_op jit(solution)/shard_map/all_gather | solution.py:1350
  58.7 6.2 convolution_convert_fusion.1.k_ref.refs_6_
  64.9 6.0 fusion.7.v_ref.refs_7_
  71.0 3.3 collective-permute-start
  74.4 2.9 fusion.6.q_ref.refs_5_
  77.4 25.5 %attend.1 = (bf16[1280,512]{1,0:T(8,128)(2,1)S(1)}, f32[4,2,1280]{2,1,0:T(2,128)S(1)}) custom-call(s32[3]{0:T(128)S(1)} %pad_add_fusion.facts_ref.refs_4_, bf16[1280,512]{1,0:T(8,128)(2,1)S(1)} %fusion.6.q_ref.refs_5_, bf16[1280,512]{1,0:T(8,128)(2,1)S(1)} %convolution_convert_fusion.1.k_ref.refs_6_, bf16[1280,512]{1,0:T(8,128)(2,1)S(1)} %fusion.7.v_ref.refs_7_, ...), custom_call_target="tpu_custom_call" | custom-call | flops 3355443200 | bytes 5242880 | tf_op jit(solution)/shard_map/attend/pallas_call | solution.py:109
  102.9 1.0 copy-done.2
  104.0 1.1 copy-done.6
  105.0 0.6 copy-done.7
  105.6 266.1 %ffn_sums.1 = (bf16[1280,2048]{1,0:T(8,128)(2,1)}, bf16[1280,2048]{1,0:T(8,128)(2,1)}, bf16[1280,2048]{1,0:T(8,128)(2,1)}, f32[640,2048]{1,0:T(8,128)}, bf16[128...) custom-call(bf16[1280,512]{1,0:T(8,128)(2,1)} %copy-done.2, ...), custom_call_target="tpu_custom_call" | custom-call | flops 32212254720 | bytes 78643200 | tf_op jit(solution)/shard_map/ffn_sums/pallas_call | solution.py:1215
  371.7 7.1 convolution_convert_fusion.refs_10_
  378.8 142.5 %down_sum.1 = (bf16[1280,2048]{1,0:T(8,128)(2,1)}, bf16[1280,512]{1,0:T(8,128)(2,1)}, bf16[1280,512]{1,0:T(8,128)(2,1)}, bf16[1280,512]{1,0:T(8,128)(2,1)}, f32[64,512]{1,0:T(8,128)}, /*index=5*/f32[64,512]{1,0:T(8,128)}) custom-call(bf16[1280,2048]{1,0:T(8,128)(2,1)} %get-tuple-element.38.refs_0_.refs_12_, bf16[2048,2048]{1,0:T(8,128)(2,1)} %get-tuple-element.39.refs_1_, ...), custom_call_target="tpu_custom_call" | custom-call | flops 10737418240 | bytes 10485760 | tf_op jit(solution)/shard_map/down_sum/pallas_call | solution.py:399
  521.3 1.0 pad_maximum_fusion.1
  522.2 1.3 collective-permute-start.1
  523.6 2.0 pad_maximum_fusion
  525.6 0.1 reduce_sum.74
  525.7 1.6 convert_reduce_fusion.3
  527.2 2.9 collective-permute-done.1
  530.1 0.9 add_convert_fusion
  531.0 0.7 dynamic_update_slice.3
  531.7 0.2 convert_reduce_fusion.2
  532.0 1.7 slice_bitcast_fusion
  533.6 145.7 %input_sum.1 = (bf16[1280,2048]{1,0:T(8,128)(2,1)}, f32[2,8,2048]{2,1,0:T(8,128)}, f32[256,2048]{1,0:T(8,128)}, f32[2048,256]{1,0:T(8,128)}, f32[512,256]{1,0:T(8,128)}, /*index=5*/f32[256,1536]{1,0:T(8,128)}) custom-call(bf16[1280,512]{1,0:T(8,128)(2,1)} %get-tuple-element.44.refs_0_.refs_14_, bf16[1280,512]{1,0:T(8,128)(2,1)} %get-tuple-element.89.refs_1_.refs_15_, ...), custom_call_target="tpu_custom_call" | custom-call | flops 8053063680 | bytes 10485760 | tf_op jit(solution)/shard_map/input_sum/pallas_call | solution.py:399
  679.4 1.0 reduce_sum.75
  680.4 0.7 concatenate.7.own_ref
  681.0 17.9 %small_sum.1 = f32[8,2048]{1,0:T(8,128)} custom-call(f32[8,2048]{1,0:T(8,128)} %concatenate.7.own_ref), custom_call_target="tpu_custom_call" | custom-call | tf_op jit(solution)/shard_map/small_sum/pallas_call | solution.py:1294
  698.9 1.8 fusion.13
  700.8 0.8 slice_reduce_fusion
  701.5 0.6 reshape.84
  702.1 8.1 %bitcast_convert_fusion = f32[1,1280,2048]{2,1,0:T(8,128)} fusion(bf16[1280,2048]{1,0:T(8,128)(2,1)} %get-tuple-element.52), kind=kLoop, calls=%fused_computation.9 | loop fusion | flops 2621440 | bytes 15728640 | tf_op jit(solution)/shard_map/broadcast_in_dim | solution.py:1464
  710.3 0.5 copy.33
  710.7 1.6 copy.34
  712.4 5.8 copy.40
  718.2 0.8 copy.41
  719.0 1.3 copy.42
  720.3 1.3 copy.43
  (53 shorter events, 0.2 us)
Async XLA Ops:
  7.2 51.5 %all-gather.3.cloned.1.call-start = ((), (), s32[]{:S(2)}) async-start(), calls=%async_computation | async-start | bytes 7077888 | tf_op jit(solution)/shard_map/all_gather | solution.py:1350
  9.8 95.8 %all-gather.5.cloned.1.call-start = ((), (), s32[]{:S(2)}) async-start(), calls=%async_computation.1 | async-start | bytes 2359296 | tf_op jit(solution)/shard_map/all_gather | solution.py:1350
  10.6 4.0 copy-start.8
  14.6 1.5 copy-start.18
  14.6 1.6 copy-start.19
  14.6 2.8 copy-start.16
  14.7 2.8 copy-start.17
  24.5 52.8 %copy-start.5 = (s32[3]{0:T(128)}, s32[3]{0:T(128)S(1)}, u32[]{:S(2)}) copy-start(s32[3]{0:T(128)S(1)} %pad_add_fusion.facts_ref.refs_4_) | copy-start | bytes 40
  58.7 6.2 copy-start.9
  64.9 12.4 %copy-start = (bf16[1280,512]{1,0:T(8,128)(2,1)}, bf16[1280,512]{1,0:T(8,128)(2,1)S(1)}, u32[]{:S(2)}) copy-start(bf16[1280,512]{1,0:T(8,128)(2,1)S(1)} %convolution_convert_fusion.1.k_ref.refs_6_) | copy-start | bytes 3932164
  64.9 9.4 %slice-start = ((s8[5242880]{0:T(1024)(128)(4,1)}), s8[4194304]{0:T(1024)(128)(4,1)S(1)}, s32[]{:S(2)}) async-start(s8[5242880]{0:T(1024)(128)(4,1)} %bitcast.61), calls=%async_computation.2 | async-start | bytes 8388608
  64.9 9.4 %slice-start.1 = ((s8[5242880]{0:T(1024)(128)(4,1)}), s8[1048576]{0:T(1024)(128)(4,1)S(1)}, s32[]{:S(2)}) async-start(s8[5242880]{0:T(1024)(128)(4,1)} %bitcast.61), calls=%async_computation.3 | async-start | bytes 2097152
  71.0 6.4 copy-start.1
  71.0 6.2 collective-permute-start
  77.3 25.6 %copy-start.3 = (bf16[64,512]{1,0:T(8,128)(2,1)}, bf16[64,512]{1,0:T(8,128)(2,1)S(1)}, u32[]{:S(2)}) copy-start(bf16[64,512]{1,0:T(8,128)(2,1)S(1)} %get-tuple-element.90.vs_ref.refs_9_) | copy-start | bytes 196612
  77.3 25.6 %copy-start.4 = (bf16[64,512]{1,0:T(8,128)(2,1)}, bf16[64,512]{1,0:T(8,128)(2,1)S(1)}, u32[]{:S(2)}) copy-start(bf16[64,512]{1,0:T(8,128)(2,1)S(1)} %get-tuple-element.91.ks_ref.refs_8_) | copy-start | bytes 196612
  102.9 1.1 copy-start.2
  104.0 1.1 copy-start.6
  105.0 0.6 copy-start.7
  522.2 7.9 %collective-permute-start.1 = (f32[2,50,512]{2,1,0:T(8,128)S(1)}, f32[2,50,512]{2,1,0:T(8,128)S(1)}, u32[]{:S(2)}, u32[]{:S(2)}) collective-permute-start(f32[2,50,512]{2,1,0:T(8,128)S(1)} %pad_maximum_fusion.1), channel_id=1, source_target_pairs={{4,0},{5,1},{6,2},{7,3},{12,8},{13,9},{14,10},{15,11},{20,16},{21,... | collective-permute-start | bytes 614408 | tf_op jit(solution)/shard_map/ppermute | solution.py:147
  523.5 2.0 copy-start.14
  523.5 2.1 copy-start.15
  702.1 8.1 %copy-start.12 = (f32[256,1536]{1,0:T(8,128)S(1)}, f32[256,1536]{1,0:T(8,128)}, u32[]{:S(2)}) copy-start(f32[256,1536]{1,0:T(8,128)} %get-tuple-element.56) | copy-start | bytes 4718596
  712.4 5.9 copy-start.13
  712.4 6.7 copy-start.11
  718.2 2.1 copy-start.10
Sparse Core Ops, SparseCore 0:
  10.5 48.2 all-gather.2
  60.6 28.1 all-gather.4

commit v5 on v4

--- a/solution.py
+++ b/solution.py
@@ -17,8 +17,6 @@
 PAIR = 2 * HDIM
 PIECE = 32
 SKEW = 2
-SECOND_STREAM = 19
-WEIGHTS_READY = 16
 MIB = 1 << 20
 MESH = pl.DeviceIdType.MESH
 MASKED = -1e30
@@ -175,7 +173,7 @@
     @staticmethod
     def scratch(half, features):
         pieces = half // PIECE
-        group = 5 * PIECE if pieces % 5 == 0 else PIECE
+        group = 160 if half % 160 == 0 else PIECE
         dma = lambda *shape: pltpu.SemaphoreType.DMA(shape)
         return [
             pltpu.VMEM((2, 2, group, features), jnp.float32),
@@ -336,41 +334,49 @@
     return multiply
 
 
-def line_kernel(count, half, dims, n_left, n_extra, n_owned, n_acc, finish, side, *refs):
+def line_kernel(count, half, dims, n_left, n_extra, n_owned, n_acc, finish, sides, *refs):
     refs = list(refs)
     take = lambda n: [refs.pop(0) for _ in range(n)]
-    lefts, (right,), extras, side_in = take(n_left), take(1), take(n_extra), take(side.n_in)
+    lefts, (right,), extras = take(n_left), take(1), take(n_extra)
+    side_in = [take(side.n_in) for side in sides]
     (out,), owned, accs = take(1), take(n_owned), take(1 if n_acc else 0)
-    side_out = take(side.n_out)
-    part, moving, sems, side_scratch = *take(2), take(5), refs
+    side_out = [take(side.n_out) for side in sides]
+    part, moving, sems = *take(2), take(5)
     multiply = group_product(lefts, right, dims, half, part.shape[2])
     ending = lambda flow, k, total: finish(flow, k, total, extras, owned, accs)
     line = Line(count, half, multiply, ending, out, part, moving, sems)
-    job = side(side_in, side_out, side_scratch)
+    jobs = [
+        side(ins, outs, take(len(side.scratch_shapes)), accs)
+        for side, ins, outs in zip(sides, side_in, side_out)
+    ]
     barrier = pltpu.get_barrier_semaphore()
     line.greet(barrier)
-    job.greet(barrier)
+    for job in jobs:
+        job.greet(barrier)
     if n_acc:
         accs[0][...] = jnp.zeros_like(accs[0])
-    job.first()
+    for job in jobs:
+        job.first()
     line.first()
-    line.meet(barrier, job.others)
+    line.meet(barrier, sum(job.others for job in jobs))
 
     def step(t, carry):
         line.step(t)
-        job.step(t)
+        for job in jobs:
+            job.step(t)
         return carry
 
-    lax.fori_loop(0, max(line.steps, job.steps), step, 0)
+    lax.fori_loop(0, max([line.steps] + [job.steps for job in jobs]), step, 0)
     line.settle()
-    job.settle()
+    for job in jobs:
+        job.settle()
 
 
 class Nothing:
     n_in = n_out = others = steps = 0
     operands, in_specs, out_shape, out_specs, scratch_shapes = (), (), (), (), ()
 
-    def __call__(self, ins, outs, scratch):
+    def __call__(self, ins, outs, scratch, accs):
         return self
 
     def greet(self, barrier):
@@ -391,7 +397,7 @@
 SMEM = pl.BlockSpec(memory_space=pltpu.SMEM)
 
 
-def line_sum(number, count, lefts, right, dims, extras, n_owned, n_acc, finish, name, side=Nothing()):
+def line_sum(number, count, lefts, right, dims, extras, n_owned, n_acc, finish, name, sides):
     rows = lefts[0].shape[0]
     features = right.shape[1 if dims == NN else 0]
     half = rows // 2
@@ -407,15 +413,15 @@
             n_owned,
             n_acc,
             finish,
-            side,
+            sides,
         ),
-        in_specs=[VMEM] * (len(lefts) + 1 + len(extras)) + list(side.in_specs),
-        out_specs=[ANY] + [VMEM] * (n_owned + len(acc)) + list(side.out_specs),
+        in_specs=[VMEM] * (len(lefts) + 1 + len(extras)) + [s for side in sides for s in side.in_specs],
+        out_specs=[ANY] + [VMEM] * (n_owned + len(acc)) + [s for side in sides for s in side.out_specs],
         out_shape=[jax.ShapeDtypeStruct((rows, features), jnp.bfloat16)]
         + [jax.ShapeDtypeStruct((half, features), jnp.float32)] * n_owned
         + acc
-        + list(side.out_shape),
-        scratch_shapes=Line.scratch(half, features) + list(side.scratch_shapes),
+        + [s for side in sides for s in side.out_shape],
+        scratch_shapes=Line.scratch(half, features) + [s for side in sides for s in side.scratch_shapes],
         compiler_params=pltpu.CompilerParams(
             collective_id=number, has_side_effects=True, vmem_limit_bytes=62 * MIB
         ),
@@ -425,7 +431,7 @@
             transcendentals=0,
         ),
         name=name,
-    )(*lefts, right, *extras, *side.operands)
+    )(*lefts, right, *extras, *[value for side in sides for value in side.operands])
 
 
 def piece_rows(flow, k, half):
@@ -475,7 +481,7 @@
         self.steps = self.pairs * self.blocks
         self.causal = rows == seg
 
-    def __call__(self, ins, outs, scratch):
+    def __call__(self, ins, outs, scratch, accs):
         self.ins, self.outs, self.scratch = ins, outs, scratch
         return self
 
@@ -595,7 +601,7 @@
             dma(3),
         )
 
-    def __call__(self, ins, outs, scratch):
+    def __call__(self, ins, outs, scratch, accs):
         self.lefts, self.rights, self.outs = ins[:4], ins[4:], outs
         (
             self.x_buf,
@@ -846,8 +852,8 @@
 class Gather:
     others = 3
 
-    def __init__(self, shards, fulls, sems):
-        self.shards, self.fulls = shards, fulls
+    def __init__(self, shards, fulls, sems, ready):
+        self.shards, self.fulls, self.ready = shards, fulls, ready
         self.sent, self.got, self.local = sems
         item, seq = lax.axis_index("item"), lax.axis_index("seq")
         self.core, self.x, self.y = item % 2, item // 2, seq
@@ -856,9 +862,9 @@
         self.to_y = {"seq": 1 - seq}
 
     @staticmethod
-    def sems():
+    def sems(count=2):
         dma = lambda *shape: pltpu.SemaphoreType.DMA(shape)
-        return [dma(2, 9), dma(2, 9), dma(2)]
+        return [dma(count, 9), dma(count, 9), dma(count)]
 
     def greet(self, barrier):
         for to in (self.to_core, self.to_x, self.to_y):
@@ -926,7 +932,7 @@
         )
 
     def first(self):
-        for w in range(2):
+        for w in range(len(self.shards)):
             self.mine(w).start()
 
     def begin(self):
@@ -934,28 +940,28 @@
             self.send(w, (1, 2, 0))
 
     def step(self, t):
-        for w, at in ((0, 5), (1, 9)):
+        for w, at in ((0, self.ready * 5 // 16), (1, self.ready * 9 // 16)):
 
             @pl.when(t == at)
             def _():
                 self.receive(w, (1, 2))
                 self.send(w, (3, 4, 5, 6))
 
-        for w, at in ((0, 12), (1, 15)):
+        for w, at in ((0, self.ready * 12 // 16), (1, self.ready * 15 // 16)):
 
             @pl.when(t == at)
             def _():
                 self.receive(w, (3, 4))
                 self.send(w, (7, 8))
 
-        @pl.when(t == WEIGHTS_READY)
+        @pl.when(t == self.ready)
         def _():
             for w in range(2):
                 self.receive(w, (0, 5, 6, 7, 8))
                 self.mine(w).wait()
 
     def settle(self):
-        for w in range(2):
+        for w in range(len(self.shards)):
             for out, _ in self.messages(w):
                 out.wait_send()
 
@@ -963,7 +969,8 @@
 class Load:
     others = 0
 
-    def __init__(self, shards, fulls, sems):
+    def __init__(self, shards, fulls, sems, ready):
+        self.ready = ready
         self.copies = [
             pltpu.make_async_copy(shard, full, sems[2].at[w])
             for w, (shard, full) in enumerate(zip(shards, fulls))
@@ -982,7 +989,7 @@
         pass
 
     def step(self, t):
-        @pl.when(t == WEIGHTS_READY)
+        @pl.when(t == self.ready)
         def _():
             for copy in self.copies:
                 copy.wait()
@@ -991,10 +998,87 @@
         pass
 
 
-def ffn_kernel(
+class Attend:
+    bq = 128
+
+    def __init__(self, half, facts, q, k, v, earlier, attended, lse):
+        self.half, self.facts, self.q, self.k, self.v = half, facts, q, k, v
+        self.earlier, self.attended, self.lse = earlier, attended, lse
+        self.pairs = q.shape[1] // PAIR
+        self.blocks = half // self.bq
+
+    def first(self):
+        def one(pair, carry):
+            for flow in range(2):
+                self.unit(pair, flow * self.blocks)
+            return carry
+
+        lax.fori_loop(0, self.pairs, one, 0)
+
+    def step(self, t):
+        def both(pair, block):
+            for flow in range(2):
+                self.unit(pair, flow * self.blocks + block)
+
+        @pl.when(t < 2)
+        def _():
+            each = self.pairs // 2
+
+            def one(i, carry):
+                both((t % 2) * each + i, 1)
+                return carry
+
+            lax.fori_loop(0, each, one, 0)
+
+        for block in range(2, self.blocks):
+            start = self.pairs * (block - 2) + 2
+
+            @pl.when((t >= start) & (t < start + self.pairs))
+            def _():
+                both(t - start, block)
+
+    def unit(self, pair, block):
+        bq, nk = self.bq, (block + 1) * self.bq
+        cols = pl.ds(pl.multiple_of(pair * PAIR, PAIR), PAIR)
+        here = slice(block * bq, nk)
+        query = block * bq + lax.broadcasted_iota(jnp.int32, (1, 2 * bq), 1) % bq
+        limit = jnp.minimum(query + 1, self.facts[1])
+        own = lax.broadcasted_iota(jnp.int32, (nk, 2 * bq), 0) < limit
+        earlier = lax.broadcasted_iota(jnp.int32, (SUMM_ROWS, 2 * bq), 0) < self.facts[2]
+        q = self.q[here, cols] * jnp.bfloat16(HDIM**-0.5)
+        q = jnp.concatenate([jnp.where(head_lanes(h), q, jnp.zeros_like(q)) for h in range(2)])
+        s = jnp.where(own, mm(self.k[:nk, cols], q, NT), MASKED)
+        s2 = jnp.where(earlier, mm(self.earlier[0, :, cols], q, NT), MASKED)
+        top = jnp.maximum(jnp.max(s, axis=0, keepdims=True), jnp.max(s2, axis=0, keepdims=True))
+        p = jnp.exp(s - top)
+        p2 = jnp.exp(s2 - top)
+        total = jnp.sum(p, axis=0, keepdims=True) + jnp.sum(p2, axis=0, keepdims=True)
+        out = mm(self.v[:nk, cols].T, p.astype(jnp.bfloat16))
+        out = (out + mm(self.earlier[1, :, cols].T, p2.astype(jnp.bfloat16))) / total
+        lse = top + jnp.log(total)
+        for head in range(2):
+            self.lse[pair, head : head + 1, here] = lse[:, head * bq : (head + 1) * bq]
+        low_half = lax.broadcasted_iota(jnp.int32, (PAIR, 1), 0) < HDIM
+        joined = jnp.where(low_half, out[:, :bq], out[:, bq:])
+        self.attended[here, cols] = joined.T.astype(jnp.bfloat16)
+
+
+def ffn_kernel(count, half, weights_job, n_attend, *refs):
+    if n_attend == 1:
+        ffn_body(count, half, weights_job, None, *refs)
+    else:
+        facts, q, k, v, earlier, *rest = refs
+        inputs, outputs, scratch = rest[:9], rest[9:20], rest[20:]
+        *outputs, attended, lse = outputs
+        job = Attend(half, facts, q, k, v, earlier, attended, lse)
+        ffn_body(count, half, weights_job, job, attended, *inputs, *outputs, *scratch)
+
+
+def ffn_body(
     count,
     half,
     weights_job,
+    attention,
     attended,
     out_w,
     out_bias,
@@ -1034,10 +1118,13 @@
     in_sem, residual_sem, grad_sem, mid_sem, cot_sem, act_sem, pre_sem, down_sem = sems
     me = lax.axis_index("mp")
     group = part2.shape[2]
+    blocks = 4
+    block = up.shape[1] // blocks
     per_group = group // PIECE
     pieces = half // PIECE
     last = count - 1
-    weights = weights_job((up_shard, down_shard), (up, down), weight_sems)
+    second = per_group + blocks + 2 * SKEW * (count - 1)
+    weights = weights_job((up_shard, down_shard), (up, down), weight_sems, second - blocks - 1)
     piece = lambda k: pl.ds(pl.multiple_of(k * PIECE, PIECE), PIECE)
     owner = (me == 0) | (me == last)
     my_flow = jnp.where(me == 0, 0, 1)
@@ -1103,30 +1190,37 @@
             pre_out.at[flow], grad_pre.at[group_rows(flow, g)], pre_sem.at[flow]
         )
 
-    def products(flow, g):
-        mid_fetch(flow, g, False).wait()
-        cot_fetch(flow, g).wait()
-
-        @pl.when(g > 0)
-        def _():
-            act_copy(flow, g - 1).wait()
-            pre_copy(flow, g - 1).wait()
-
-        block = 512
-        for number in range(up.shape[1] // block):
-            cols = slice(number * block, (number + 1) * block)
-            value, slope = gelu_parts(mm(mid_in[flow], up[:, cols]) + up_bias[:, cols])
-            act_out[flow, :, cols] = value.astype(jnp.bfloat16)
-            pre = (slope * mm(cot_in[flow], down[cols, :], NT)).astype(jnp.bfloat16)
-            pre_out[flow, :, cols] = pre
-            acc_up[:, cols] += fold(pre.astype(jnp.float32))
-            product = mm(pre, up[:, cols], NT)
-            if number == 0:
-                part2[flow, g % 2] = product
-            else:
-                part2[flow, g % 2] += product
-        act_copy(flow, g).start()
-        pre_copy(flow, g).start()
+    def products(flow, g, number):
+        @pl.when(number == 0)
+        def _():
+            mid_fetch(flow, g, False).wait()
+            cot_fetch(flow, g).wait()
+
+            @pl.when(g > 0)
+            def _():
+                act_copy(flow, g - 1).wait()
+                pre_copy(flow, g - 1).wait()
+
+        cols = pl.ds(pl.multiple_of(number * block, block), block)
+        value, slope = gelu_parts(mm(mid_in[flow], up[:, cols]) + up_bias[:, cols])
+        act_out[flow, :, cols] = value.astype(jnp.bfloat16)
+        pre = (slope * mm(cot_in[flow], down[cols, :], NT)).astype(jnp.bfloat16)
+        pre_out[flow, :, cols] = pre
+        acc_up[:, cols] += fold(pre.astype(jnp.float32))
+        product = mm(pre, up[:, cols], NT)
+
+        @pl.when(number == 0)
+        def _():
+            part2[flow, g % 2] = product
+
+        @pl.when(number > 0)
+        def _():
+            part2[flow, g % 2] += product
+
+        @pl.when(number == blocks - 1)
+        def _():
+            act_copy(flow, g).start()
+            pre_copy(flow, g).start()
 
     barrier = pltpu.get_barrier_semaphore()
     line1.greet(barrier)
@@ -1143,24 +1237,32 @@
 
         lax.fori_loop(0, pieces, one, 0)
 
-    line1.first()
-    line1.meet(barrier, weights.others)
-    weights.begin()
+    if attention is None:
+        line1.first()
+        line1.meet(barrier, weights.others)
+        weights.begin()
+    else:
+        line1.meet(barrier, weights.others)
+        weights.begin()
+        attention.first()
+        line1.first()
 
     def step(t, carry):
+        if attention is not None:
+            attention.step(t)
         line1.step(t)
-        line2.step(t - SECOND_STREAM)
+        line2.step(t - second)
         weights.step(t)
 
-        @pl.when(t == WEIGHTS_READY + 1)
+        @pl.when(t == weights.ready + 1)
         def _():
             pltpu.make_async_copy(down, down_out, down_sem.at[0]).start()
 
         for flow in range(2):
             place = line1.place(flow)
-            u = t - SECOND_STREAM - SKEW * place
-            fetch = u + 3
-            compute = u + 2
+            u = t - second - SKEW * place
+            fetch = u + blocks + 1
+            compute = u + blocks
 
             @pl.when((fetch >= 0) & (fetch % per_group == 0) & (fetch < pieces))
             def _():
@@ -1175,13 +1277,13 @@
                 def _():
                     mid_fetch(flow, g, False).start()
 
-            @pl.when((compute >= 0) & (compute % per_group == 0) & (compute < pieces))
+            @pl.when((compute >= 0) & (compute < pieces) & (compute % per_group < blocks))
             def _():
-                products(flow, compute // per_group)
+                products(flow, compute // per_group, compute % per_group)
 
         return carry
 
-    lax.fori_loop(0, SECOND_STREAM + line2.steps, step, 0)
+    lax.fori_loop(0, second + line2.steps, step, 0)
     line1.settle()
     line2.settle()
     weights.settle()
@@ -1199,23 +1301,27 @@
         lax.fori_loop(0, pieces, one, 0)
 
 
-def ffn_sums(number, count, weights_job, attended, out_w, vectors, hidden, cotangent, up_w, down_w):
+def ffn_sums(number, count, weights_job, attend_in, out_w, vectors, hidden, cotangent, up_w, down_w):
     rows, features = hidden.shape
     ff = up_w.shape[1]
     half = rows // 2
     pieces = half // PIECE
     low = lambda *shape: jax.ShapeDtypeStruct(shape, jnp.bfloat16)
     wide = lambda *shape: jax.ShapeDtypeStruct(shape, jnp.float32)
+    attend_out = []
+    if len(attend_in) > 1:
+        width = attend_in[1].shape[1]
+        attend_out = [low(rows, width), wide(width // PAIR, 2, rows)]
     first = Line.scratch(half, features)
-    small = 2 * PIECE if pieces % 2 == 0 else PIECE
+    small = 64 if half % 64 == 0 else PIECE
     first[0] = pltpu.VMEM((2, 2, small, features), jnp.float32)
     second = Line.scratch(half, features)
     group = second[0].shape[2]
     dma = lambda n: pltpu.SemaphoreType.DMA((n,))
     return pl.pallas_call(
-        functools.partial(ffn_kernel, count, half, weights_job),
-        in_specs=[VMEM] * 6 + [ANY] * 4,
-        out_specs=[ANY] * 7 + [VMEM] * 2,
+        functools.partial(ffn_kernel, count, half, weights_job, len(attend_in)),
+        in_specs=[SMEM, VMEM, VMEM, VMEM, VMEM][-len(attend_in) :] + [VMEM] * 5 + [ANY] * 4,
+        out_specs=[ANY] * 7 + [VMEM] * (2 + len(attend_out)),
         out_shape=[
             low(rows, features),
             low(rows, ff),
@@ -1226,7 +1332,8 @@
             low(ff, features),
             wide(3, 8, features),
             wide(8, ff),
-        ],
+        ]
+        + attend_out,
         scratch_shapes=first[:2]
         + second[:2]
         + [
@@ -1250,61 +1357,223 @@
             flops=6 * rows * features * ff, bytes_accessed=30 * rows * features, transcendentals=0
         ),
         name="ffn_sums",
-    )(attended, out_w, *vectors, hidden, cotangent, up_w, down_w)
-
-
-def small_kernel(stages, shared, own_ref, out_ref, sent, got, send_sem, recv_sem):
+    )(*attend_in, out_w, *vectors, hidden, cotangent, up_w, down_w)
+
+
+def start_kernel(
+    facts,
+    hidden,
+    gain,
+    shift,
+    bias,
+    shard,
+    out_shard,
+    q_ref,
+    k_ref,
+    v_ref,
+    earlier,
+    normed_out,
+    weight_out,
+    out_whole,
+    normed,
+    weight,
+    out_weight,
+    total,
+    summary,
+    *sems,
+):
+    gather = Gather((shard, out_shard), (weight, out_weight), sems[:3], 0)
+    summary_sent, summary_got, out_sems = sems[3:]
+    rows = hidden.shape[0]
+    width = q_ref.shape[1]
+    size = shard.shape[0]
+    chunk = 128
     barrier = pltpu.get_barrier_semaphore()
-
-    def partner(axis, bit):
+    gather.greet(barrier)
+    gather.first()
+    pl.semaphore_wait(barrier, gather.others)
+    gather.send(0, (1, 2, 0))
+
+    def norm(i, carry):
+        here = pl.ds(pl.multiple_of(i * chunk, chunk), chunk)
+        value = norm_stats(hidden[here, :].astype(jnp.float32))[0]
+        normed[here, :] = (value * gain[...] + shift[...]).astype(jnp.bfloat16)
+        return carry
+
+    lax.fori_loop(0, rows // chunk, norm, 0)
+    keep = pltpu.make_async_copy(normed, normed_out, out_sems.at[0])
+    keep.start()
+    c, x, y = gather.core, gather.x, gather.y
+
+    def add(places, first=False, last=False):
+        starts = [
+            pl.multiple_of(((2 * px + pc) * 2 + py) * size, size) for px, pc, py in places
+        ]
+
+        def rows_of(i, carry):
+            here = pl.ds(pl.multiple_of(i * chunk, chunk), chunk)
+            for j, out in enumerate((q_ref, k_ref, v_ref)):
+                cols = slice(j * width, (j + 1) * width)
+                value = None if first else total[here, cols]
+                for start in starts:
+                    at = pl.ds(start, size)
+                    product = mm(normed[here, at], weight[at, cols])
+                    value = product if value is None else value + product
+                if not last:
+                    total[here, cols] = value
+                elif j == 1:
+                    out[here, :] = value.astype(jnp.bfloat16)
+                else:
+                    out[here, :] = (value + bias[j // 2 : j // 2 + 1, :]).astype(jnp.bfloat16)
+            return carry
+
+        lax.fori_loop(0, rows // chunk, rows_of, 0)
+
+    gather.mine(0).wait()
+    gather.receive(0, (0,))
+    add(((x, c, y), (x, 1 - c, y)), first=True)
+    gather.receive(0, (1, 2))
+    gather.send(0, (3, 4, 5, 6))
+    gather.send(1, (1, 2, 0))
+    add(((1 - x, c, y), (x, c, 1 - y)))
+    gather.receive(0, (5, 6))
+    add(((1 - x, 1 - c, y), (x, 1 - c, 1 - y)))
+    gather.receive(0, (3, 4))
+    gather.send(0, (7, 8))
+    add(((1 - x, c, 1 - y),))
+    gather.receive(1, (1, 2))
+    gather.send(1, (3, 4, 5, 6))
+    gather.receive(0, (7, 8))
+    store = pltpu.make_async_copy(weight, weight_out, out_sems.at[1])
+    store.start()
+    add(((1 - x, 1 - c, 1 - y),), last=True)
+
+    shape = (SUMM_ROWS, rows)
+    chosen = lax.broadcasted_iota(jnp.int32, shape, 1) == (
+        facts[1] - SUMM + lax.broadcasted_iota(jnp.int32, shape, 0)
+    )
+    chosen = jnp.where(chosen, 1.0, 0.0).astype(jnp.bfloat16)
+    summary[0] = mm(chosen, k_ref[...]).astype(jnp.bfloat16)
+    summary[1] = mm(chosen, v_ref[...]).astype(jnp.bfloat16)
+    swap = pltpu.make_async_remote_copy(
+        src_ref=summary,
+        dst_ref=earlier,
+        send_sem=summary_sent.at[0],
+        recv_sem=summary_got.at[0],
+        device_id=gather.to_y,
+        device_id_type=MESH,
+    )
+    swap.start()
+    gather.receive(1, (3, 4))
+    gather.send(1, (7, 8))
+    gather.receive(1, (0, 5, 6, 7, 8))
+    gather.mine(1).wait()
+    store_out = pltpu.make_async_copy(out_weight, out_whole, out_sems.at[2])
+    store_out.start()
+    gather.settle()
+    keep.wait()
+    store.wait()
+    swap.wait()
+    store_out.wait()
+
+
+def start(number, facts, hidden, gain, shift, bias, shard, out_shard):
+    rows, features = hidden.shape
+    width = bias.shape[1]
+    low = lambda *shape: jax.ShapeDtypeStruct(shape, jnp.bfloat16)
+    dma = lambda n: pltpu.SemaphoreType.DMA((n,))
+    return pl.pallas_call(
+        start_kernel,
+        in_specs=[SMEM] + [VMEM] * 4 + [ANY] * 2,
+        out_specs=[VMEM] * 3 + [ANY] * 4,
+        out_shape=[low(rows, width)] * 3
+        + [low(2, SUMM_ROWS, width), low(rows, features), low(features, 3 * width)]
+        + [low(width, features)],
+        scratch_shapes=[
+            pltpu.VMEM((rows, features), jnp.bfloat16),
+            pltpu.VMEM((features, 3 * width), jnp.bfloat16),
+            pltpu.VMEM((width, features), jnp.bfloat16),
+            pltpu.VMEM((rows, 3 * width), jnp.float32),
+            pltpu.VMEM((2, SUMM_ROWS, width), jnp.bfloat16),
+        ]
+        + Gather.sems()
+        + [dma(1), dma(1), dma(3)],
+        compiler_params=pltpu.CompilerParams(
+            collective_id=number, has_side_effects=True, vmem_limit_bytes=60 * MIB
+        ),
+        cost_estimate=pl.CostEstimate(
+            flops=6 * rows * features * width, bytes_accessed=16 * rows * features, transcendentals=0
+        ),
+        name="start",
+    )(facts, hidden, gain, shift, bias, shard, out_shard)
+
+
+class SmallSums(Nothing):
+    n_in = n_out = 1
+
+    def __init__(self, sizes, shared, start, values):
+        self.stages = tuple(
+            (axis, 1 << bit) for axis, size in sizes for bit in range(size.bit_length() - 1)
+        )
+        self.shared, self.start = shared, start
+        self.others = len(self.stages)
+        self.steps = start + self.others + 1
+        self.operands = (values,)
+        self.in_specs = self.out_specs = (VMEM,)
+        self.out_shape = (jax.ShapeDtypeStruct(values.shape, jnp.float32),)
+        buffers = pltpu.VMEM((self.others, *values.shape), jnp.float32)
+        sems = pltpu.SemaphoreType.DMA((self.others,))
+        self.scratch_shapes = (buffers, buffers, sems, sems)
+
+    def __call__(self, ins, outs, scratch, accs):
+        (self.own,), (self.out,), (self.acc,) = ins, outs, accs
+        self.sent, self.got, self.send_sem, self.recv_sem = scratch
+        return self
+
+    def partner(self, axis, bit):
         index = lax.axis_index(axis)
         return {axis: index + bit - 2 * bit * ((index // bit) % 2)}
 
-    for axis, bit in stages:
-        pl.semaphore_signal(barrier, inc=1, device_id=partner(axis, bit), device_id_type=MESH)
-    pl.semaphore_wait(barrier, len(stages))
-    sent[0] = own_ref[...]
-    row = lax.broadcasted_iota(jnp.int32, own_ref.shape, 0)
-    for number, (axis, bit) in enumerate(stages):
-        copy = pltpu.make_async_remote_copy(
-            src_ref=sent.at[number],
-            dst_ref=got.at[number],
-            send_sem=send_sem.at[number],
-            recv_sem=recv_sem.at[number],
-            device_id=partner(axis, bit),
+    def greet(self, barrier):
+        for axis, bit in self.stages:
+            pl.semaphore_signal(
+                barrier, inc=1, device_id=self.partner(axis, bit), device_id_type=MESH
+            )
+
+    def copy(self, number):
+        return pltpu.make_async_remote_copy(
+            src_ref=self.sent.at[number],
+            dst_ref=self.got.at[number],
+            send_sem=self.send_sem.at[number],
+            recv_sem=self.recv_sem.at[number],
+            device_id=self.partner(*self.stages[number]),
             device_id_type=MESH,
         )
-        copy.start()
-        copy.wait()
-        total = sent[number] + got[number]
-        if axis == "mp":
-            total = jnp.where(row < shared, total, sent[number])
-        if number + 1 < len(stages):
-            sent[number + 1] = total
-        else:
-            out_ref[...] = total
-
-
-def small_sum(number, sizes, shared, values):
-    stages = tuple(
-        (axis, 1 << bit) for axis, size in sizes for bit in range(size.bit_length() - 1)
-    )
-    steps = len(stages)
-    vmem = pl.BlockSpec(memory_space=pltpu.VMEM)
-    return pl.pallas_call(
-        functools.partial(small_kernel, stages, shared),
-        in_specs=[vmem],
-        out_specs=vmem,
-        out_shape=jax.ShapeDtypeStruct(values.shape, jnp.float32),
-        scratch_shapes=[
-            pltpu.VMEM((steps, *values.shape), jnp.float32),
-            pltpu.VMEM((steps, *values.shape), jnp.float32),
-            pltpu.SemaphoreType.DMA((steps,)),
-            pltpu.SemaphoreType.DMA((steps,)),
-        ],
-        compiler_params=pltpu.CompilerParams(collective_id=number, has_side_effects=True),
-        name="small_sum",
-    )(values)
+
+    def step(self, t):
+        @pl.when(t == self.start)
+        def _():
+            self.sent[0] = self.own[...]
+            for number in range(self.acc.shape[0]):
+                self.sent[0, 3 + number : 4 + number, :] = jnp.sum(
+                    self.acc[number], axis=0, keepdims=True
+                )
+            self.copy(0).start()
+
+        row = lax.broadcasted_iota(jnp.int32, self.own.shape, 0)
+        for number, (axis, _) in enumerate(self.stages):
+
+            @pl.when(t == self.start + 1 + number)
+            def _():
+                self.copy(number).wait()
+                total = self.sent[number] + self.got[number]
+                if axis == "mp":
+                    total = jnp.where(row < self.shared, total, self.sent[number])
+                if number + 1 < len(self.stages):
+                    self.sent[number + 1] = total
+                    self.copy(number + 1).start()
+                else:
+                    self.out[...] = total
 
 
 def gradients_over(group, lefts, columns):
@@ -1348,8 +1617,6 @@
     group = ("item", "seq")
     width = qkv_weight.shape[2]
     gathered = lambda weight, axis: lax.all_gather(weight, group, axis=axis, tiled=True)
-    qkv_full = gathered(qkv_weight.reshape(-1, 3 * width), 0)
-    out_full = gathered(out_weight, 1)
     hidden = hidden_in[0].astype(jnp.float32)
     lengths = seg_lengths[0]
     rows = hidden.shape[0]
@@ -1363,16 +1630,27 @@
         ]
     ).astype(jnp.int32)
 
-    normed = (norm_stats(hidden)[0] * pre_gain + pre_shift).astype(jnp.bfloat16)
-    q = (mm(normed, qkv_full[:, :width]) + qv_bias[0]).astype(jnp.bfloat16)
-    k = mm(normed, qkv_full[:, width : 2 * width]).astype(jnp.bfloat16)
-    v = (mm(normed, qkv_full[:, 2 * width :]) + qv_bias[1]).astype(jnp.bfloat16)
-    own, summary = keys_for(jnp.stack([k, v]), lengths, seq_count)
-    tables = (own[0], own[1], summary[0], summary[1])
-    attended, log_total = attend(facts, q, *tables)
-
+    ours = (item_count, seq_count) == (4, 2) and rows == SLOT
     row = lambda vector: vector[None, :]
-    ours = (item_count, seq_count) == (4, 2)
+    shard = qkv_weight.reshape(-1, 3 * width)
+    if ours:
+        q, k, v, summary, normed, qkv_full, out_full = start(
+            5, facts, hidden_in[0], row(pre_gain), row(pre_shift), qv_bias, shard, out_weight
+        )
+        attend_in = (facts, q, k, v, summary)
+        tables = (k, v, summary[0], summary[1])
+    else:
+        qkv_full = gathered(shard, 0)
+        out_full = gathered(out_weight, 1)
+        normed = (norm_stats(hidden)[0] * pre_gain + pre_shift).astype(jnp.bfloat16)
+        q = (mm(normed, qkv_full[:, :width]) + qv_bias[0]).astype(jnp.bfloat16)
+        k = mm(normed, qkv_full[:, width : 2 * width]).astype(jnp.bfloat16)
+        v = (mm(normed, qkv_full[:, 2 * width :]) + qv_bias[1]).astype(jnp.bfloat16)
+        own, summary = keys_for(jnp.stack([k, v]), lengths, seq_count)
+        tables = (own[0], own[1], summary[0], summary[1])
+        attended, log_total = attend(facts, q, *tables)
+        attend_in = (attended,)
+
     grad_down = cotangent[0]
     (
         mid_low,
@@ -1384,11 +1662,12 @@
         down_full,
         mid_sums,
         up_sums,
+        *attend_out,
     ) = ffn_sums(
         1,
         mp_count,
         Gather if ours else Load,
-        attended,
+        attend_in,
         out_full,
         (row(out_bias), row(mid_gain), row(mid_shift), row(up_bias)),
         hidden_in[0],
@@ -1396,6 +1675,8 @@
         up_weight if ours else gathered(up_weight, 0),
         down_weight if ours else gathered(down_weight, 1),
     )
+    if ours:
+        attended, log_total = attend_out
     grad_attended = mm(grad_branch, out_full, NT).astype(jnp.bfloat16)
     hidden_out, dq, dk, dv, dks, dvs = line_sum(
         3,
@@ -1408,7 +1689,7 @@
         0,
         finish_out,
         "down_sum",
-        AttendBack(facts, q, *tables, grad_attended, log_total),
+        (AttendBack(facts, q, *tables, grad_attended, log_total),),
     )
     dk, dv = keys_back(jnp.stack([dk, dv]), jnp.stack([dks, dvs]), rows, lengths, seq_count)
     lefts = (mid_low, grad_down, grad_branch, normed)
@@ -1420,10 +1701,24 @@
         (3, dk, 3, width),
         (3, dv, 3, 2 * width),
     )
-    spread = Nothing()
-    if ours:
-        spread = Spread(lefts, columns)
-    grad_input, pre_sums, *weight_grads = line_sum(
+    total = lambda value: jnp.sum(value.astype(jnp.float32), axis=0)
+    features = hidden.shape[1]
+    qv_sums = jnp.concatenate([total(dq), total(dv)])
+    small = SmallSums(
+        [("item", item_count), ("seq", seq_count), ("mp", mp_count)],
+        6,
+        rows // 2 // PIECE + SKEW * (mp_count - 1),
+        jnp.concatenate(
+            [
+                jnp.sum(mid_sums, axis=1),
+                jnp.zeros((2, features), jnp.float32),
+                row(jnp.where(lax.axis_index("mp") == 0, total(grad_down), 0.0)),
+                total(up_sums).reshape(-1, features),
+                jnp.pad(qv_sums, (0, -qv_sums.shape[0] % features)).reshape(-1, features),
+            ]
+        ),
+    )
+    grad_input, _, *weight_grads, sums = line_sum(
         4,
         mp_count,
         [dq, dk, dv],
@@ -1434,28 +1729,11 @@
         2,
         finish_input,
         "input_sum",
-        spread,
+        ((Spread(lefts, columns),) if ours else ()) + (small,),
     )
     if not weight_grads:
         weight_grads = gradients_over(group, lefts, columns)
     up_grad, down_grad, out_grad, qkv_grad = weight_grads
-    total = lambda value: jnp.sum(value.astype(jnp.float32), axis=0)
-    features = hidden.shape[1]
-    qv_sums = jnp.concatenate([total(dq), total(dv)])
-    sums = small_sum(
-        5,
-        [("item", item_count), ("seq", seq_count), ("mp", mp_count)],
-        6,
-        jnp.concatenate(
-            [
-                jnp.sum(mid_sums, axis=1),
-                jnp.sum(pre_sums, axis=1),
-                row(jnp.where(lax.axis_index("mp") == 0, total(grad_down), 0.0)),
-                total(up_sums).reshape(-1, features),
-                jnp.pad(qv_sums, (0, -qv_sums.shape[0] % features)).reshape(-1, features),
-            ]
-        ),
-    )
     ff_rows = up_weight.shape[1] // features
     up_bias_grad = sums[6 : 6 + ff_rows].reshape(-1)
     qv_bias_grad = sums[6 + ff_rows :].reshape(-1)[: 2 * width].reshape(2, width)

time: 737 us -> 675 us (0.916)
  waiting for transfers between devices: 32.6 us -> 0.01 us
  Pallas kernels: 598 us -> 616 us
  matrix products: 22.2 us -> 7.14 us
  other arithmetic: 30.1 us -> 15.8 us
  between operations: 17.5 us -> 3.67 us
    all_gather x2 -> x0, waiting for transfers between devices: 29 us -> none  [body(): lax.all_gather(weight, group, axis=axis, tiled=True)]
    dot_general x4 -> x1, matrix products: 22.2 us -> 7.14 us  [mm(): lax.dot_general(left, right, dims, preferred_element_type=jnp.float32)]
    pallas_call x2, Pallas kernels: 288 us -> 297 us  [line_sum(): pl.pallas_call(functools.partial(line_kernel, count, half, dims, len(left...]
    pallas_call x3 -> x2, Pallas kernels: 309 us -> 318 us  [the longest x1 269 us: ffn_sums(): pl.pallas_call(functools.partial(ffn_kernel, count, half, weights_job, le...]
    unnamed x50 -> x26, local copies, waits for them, and re-layouts: 15.7 us -> 12.7 us
  transfers between devices with their start and end apart: 4 -> 1, of which waited for: 2 -> 0; matrix products, arithmetic and copies ran while one was open for 5% -> 1% of each run, Pallas kernels for 3% -> 0%
where the time goes in v5:
time: 675 us; the launch traced here: 666 us
  Pallas kernels  616 us (91%)
  local copies, waits for them, and re-layouts  22.4 us (3%)
  other arithmetic  15.8 us (2%)
  matrix products  7.14 us (1%)
    pallas_call x2, Pallas kernels, line_sum(): pl.pallas_call(functools.partial(line_kernel, count, half, dims, len(left...  297 us
    pallas_call x1, Pallas kernels, ffn_sums(): pl.pallas_call(functools.partial(ffn_kernel, count, half, weights_job, le...  269 us
    pallas_call x1, Pallas kernels, start(): pl.pallas_call(start_kernel, in_specs=[SMEM] + [VMEM] * 4 + [ANY] * 2, ou...  49 us
  transfers between devices with their start and end apart: 1, of which 0 were waited for; matrix products, arithmetic and copies ran while one was open for 1% of the time, Pallas kernels for 0%

profile of v5, /device:TPU:0, one launch (start us, length us, event | category | flops | bytes accessed | tf_op | source)
XLA Modules:
  0.0 666.1 jit_solution(15742333746504345739)
XLA Ops:
  0.6 0.0 copy-start.9
  0.7 1.4 copy.31
  2.1 1.2 copy.32.shard
  3.3 0.0 copy-done.9
  3.3 0.6 constant_dynamic-slice_fusion
  4.5 0.6 pad_add_fusion.facts.refs_0_.refs_4_
  5.1 49.0 %start.1 = (bf16[1280,512]{1,0:T(8,128)(2,1)}, bf16[1280,512]{1,0:T(8,128)(2,1)}, bf16[1280,512]{1,0:T(8,128)(2,1)}, bf16[2,64,512]{2,1,0:T(8,128)(2,1)}, bf16[1...) custom-call(s32[3]{0:T(128)} %pad_add_fusion.facts.refs_0_.refs_4_, ...), custom_call_target="tpu_custom_call" | custom-call | flops 8053063680 | bytes 41943040 | tf_op jit(solution)/shard_map/start/pallas_call | solution.py:1485
  54.1 1.5 slice_bitcast_fusion.2
  55.7 269.1 %ffn_sums.1 = (bf16[1280,2048]{1,0:T(8,128)(2,1)}, bf16[1280,2048]{1,0:T(8,128)(2,1)}, bf16[1280,2048]{1,0:T(8,128)(2,1)}, f32[640,2048]{1,0:T(8,128)}, bf16[128...) custom-call(s32[3]{0:T(128)} %pad_add_fusion.facts.refs_0_.refs_4_, ...), custom_call_target="tpu_custom_call" | custom-call | flops 32212254720 | bytes 78643200 | tf_op jit(solution)/shard_map/ffn_sums/pallas_call | solution.py:1321
  324.7 7.1 %convolution_convert_fusion.refs_10_ = bf16[1280,512]{1,0:T(8,128)(2,1)} fusion(bf16[1280,2048]{1,0:T(8,128)(2,1)} %get-tuple-element.52.refs_9_, bf16[512,2048]{1,0:T(8,128)(2,1)} %get-tuple-element.48.refs_5_), kind=kOutput, calls=%fused_computation.2 | convolution fusion | flops 2685009920 | bytes 8650752 | tf_op jit(solution)/shard_map/dot_general | solution.py:32
  331.9 143.7 %down_sum.1 = (bf16[1280,2048]{1,0:T(8,128)(2,1)}, bf16[1280,512]{1,0:T(8,128)(2,1)}, bf16[1280,512]{1,0:T(8,128)(2,1)}, bf16[1280,512]{1,0:T(8,128)(2,1)}, f32[64,512]{1,0:T(8,128)}, /*index=5*/f32[64,512]{1,0:T(8,128)}) custom-call(bf16[1280,2048]{1,0:T(8,128)(2,1)} %get-tuple-element.49.refs_0_.refs_12_, bf16[2048,2048]{1,0:T(8,128)(2,1)} %get-tuple-element.50.refs_1_, ...), custom_call_target="tpu_custom_call" | custom-call | flops 10737418240 | bytes 10485760 | tf_op jit(solution)/shard_map/down_sum/pallas_call | solution.py:405
  475.5 1.0 pad_maximum_fusion.1
  476.5 1.5 collective-permute-start
  479.3 0.0 copy-start
  479.3 0.0 copy-start.7
  479.3 0.0 copy-start.8
  479.3 3.4 convert_reduce_fusion
  482.7 0.0 copy-done
  482.7 0.2 convert_reduce_fusion.2
  483.0 0.0 copy-done.7
  483.0 0.1 reduce_sum.45
  483.0 0.0 copy-done.8
  483.7 0.0 copy-start.1
  483.7 0.0 copy-start.2
  483.7 2.1 pad_maximum_fusion
  485.9 0.0 collective-permute-done
  485.9 0.0 copy-done.1
  485.9 0.3 copy-done.2
  486.3 0.5 dynamic_update_slice.3
  486.8 0.2 convert_reduce_fusion.1
  487.0 1.7 slice_bitcast_fusion
  488.7 0.7 concatenate.7.refs_17_
  489.4 153.8 %input_sum.1 = (bf16[1280,2048]{1,0:T(8,128)(2,1)}, f32[2,8,2048]{2,1,0:T(8,128)}, f32[256,2048]{1,0:T(8,128)}, f32[2048,256]{1,0:T(8,128)}, f32[512,256]{1,0:T(...) custom-call(bf16[1280,512]{1,0:T(8,128)(2,1)} %get-tuple-element.55.refs_0_.refs_14_, ...), custom_call_target="tpu_custom_call" | custom-call | flops 8053063680 | bytes 10485760 | tf_op jit(solution)/shard_map/input_sum/pallas_call | solution.py:405
  643.2 1.8 fusion.1
  645.0 0.8 slice_reduce_fusion
  645.8 0.0 copy-start.5
  645.8 8.1 %bitcast_convert_fusion = f32[1,1280,2048]{2,1,0:T(8,128)} fusion(bf16[1280,2048]{1,0:T(8,128)(2,1)} %get-tuple-element.68), kind=kLoop, calls=%fused_computation.1 | loop fusion | flops 2621440 | bytes 15728640 | tf_op jit(solution)/shard_map/broadcast_in_dim | solution.py:1742
  653.9 0.0 copy-done.5
  653.9 0.5 copy.33
  654.4 1.6 copy.34
  656.0 0.6 reshape.70
  656.6 5.8 copy.40
  662.4 0.0 copy-done.6
  662.5 0.8 copy.41
  663.2 0.0 copy-done.4
  663.2 1.3 copy.42
  664.6 0.0 copy-done.3
  664.6 1.3 copy.43
  (8 shorter events, 0.1 us)
Async XLA Ops:
  0.6 2.6 copy-start.9
  476.5 9.4 %collective-permute-start = (f32[2,50,512]{2,1,0:T(8,128)S(1)}, f32[2,50,512]{2,1,0:T(8,128)S(1)}, u32[]{:S(2)}, u32[]{:S(2)}) collective-permute-start(f32[2,50,512]{2,1,0:T(8,128)S(1)} %pad_maximum_fusion.1), channel_id=1, source_target_pairs={{4,0},{5,1},{6,2},{7,3},{12,8},{13,9},{14,10},{15,11},{20,16},{21,... | collective-permute-start | bytes 614408 | tf_op jit(solution)/shard_map/ppermute | solution.py:145
  479.3 3.4 copy-start
  479.3 3.7 copy-start.7
  479.3 3.7 copy-start.8
  483.7 2.2 copy-start.1
  483.7 2.5 copy-start.2
  645.8 8.2 %copy-start.5 = (f32[256,1536]{1,0:T(8,128)S(1)}, f32[256,1536]{1,0:T(8,128)}, u32[]{:S(2)}) copy-start(f32[256,1536]{1,0:T(8,128)} %get-tuple-element.70) | copy-start | bytes 4718596
  656.6 5.9 copy-start.6
  656.6 6.7 copy-start.4
  662.4 2.1 copy-start.3

commit v6 on v5

--- a/solution.py
+++ b/solution.py
@@ -161,8 +161,9 @@
 
 
 class Line:
-    def __init__(self, count, half, multiply, finish, out, part, moving, sems):
+    def __init__(self, count, half, multiply, finish, out, part, moving, sems, late=False):
         self.count, self.half, self.multiply, self.finish = count, half, multiply, finish
+        self.late = late
         self.out, self.part, self.moving = out, part, moving
         self.up_sent, self.up_got, self.down_sent, self.down_got, self.local = sems
         self.me = lax.axis_index("mp")
@@ -177,7 +178,7 @@
         dma = lambda *shape: pltpu.SemaphoreType.DMA(shape)
         return [
             pltpu.VMEM((2, 2, group, features), jnp.float32),
-            pltpu.VMEM((2, half, features), jnp.bfloat16),
+            pltpu.VMEM((2 * half, features), jnp.bfloat16),
             dma(2, pieces),
             dma(2, pieces),
             dma(2, pieces),
@@ -215,7 +216,7 @@
             self.part[flow, 0] = self.multiply(flow, 0)
 
     def onward(self, flow, k):
-        here = self.moving.at[flow, pl.ds(k * PIECE, PIECE)]
+        here = self.moving.at[pl.ds(flow * self.half + k * PIECE, PIECE)]
         return pltpu.make_async_remote_copy(
             src_ref=here,
             dst_ref=here,
@@ -228,7 +229,7 @@
     def back(self, flow, k, owner):
         rows = self.out.at[pl.ds(flow * self.half + k * PIECE, PIECE)]
         return pltpu.make_async_remote_copy(
-            src_ref=self.moving.at[flow, pl.ds(k * PIECE, PIECE)] if owner else rows,
+            src_ref=self.moving.at[pl.ds(flow * self.half + k * PIECE, PIECE)] if owner else rows,
             dst_ref=rows,
             send_sem=self.down_sent.at[flow, k],
             recv_sem=self.down_got.at[flow, k],
@@ -238,7 +239,7 @@
 
     def keep(self, flow, k):
         return pltpu.make_async_copy(
-            self.moving.at[flow, pl.ds(k * PIECE, PIECE)],
+            self.moving.at[pl.ds(flow * self.half + k * PIECE, PIECE)],
             self.out.at[pl.ds(flow * self.half + k * PIECE, PIECE)],
             self.local.at[k],
         )
@@ -248,7 +249,7 @@
         for flow in range(2):
             place = self.place(flow)
             k = t - SKEW * place
-            here = pl.ds(pl.multiple_of(k * PIECE, PIECE), PIECE)
+            here = pl.ds(pl.multiple_of(flow * self.half + k * PIECE, PIECE), PIECE)
             busy = (k >= 0) & (k < self.pieces)
 
             def mine():
@@ -258,21 +259,21 @@
 
             @pl.when(busy & (place == 0))
             def _():
-                self.moving[flow, here, :] = mine().astype(jnp.bfloat16)
+                self.moving[here, :] = mine().astype(jnp.bfloat16)
                 self.onward(flow, k).start()
 
             @pl.when(busy & (place > 0) & (place < last))
             def _():
                 self.onward(flow, k).wait_recv()
-                total = mine() + self.moving[flow, here, :].astype(jnp.float32)
-                self.moving[flow, here, :] = total.astype(jnp.bfloat16)
+                total = mine() + self.moving[here, :].astype(jnp.float32)
+                self.moving[here, :] = total.astype(jnp.bfloat16)
                 self.onward(flow, k).start()
 
             @pl.when(busy & (place == last))
             def _():
                 self.onward(flow, k).wait_recv()
-                total = mine() + self.moving[flow, here, :].astype(jnp.float32)
-                self.moving[flow, here, :] = self.finish(flow, k, total).astype(jnp.bfloat16)
+                total = mine() + self.moving[here, :].astype(jnp.float32)
+                self.moving[here, :] = self.finish(flow, k, total).astype(jnp.bfloat16)
                 self.back(flow, k, True).start()
                 self.keep(flow, k).start()
 
@@ -291,6 +292,12 @@
         for flow in range(2 if self.multiply else 0):
             k = t - SKEW * self.place(flow)
             g = k // self.per_group + 1
+
+            if self.late:
+
+                @pl.when(k == -1)
+                def _():
+                    self.part[flow, 0] = self.multiply(flow, 0)
 
             @pl.when((k >= 0) & (k % self.per_group == 0) & (g < self.pieces // self.per_group))
             def _():
@@ -539,72 +546,24 @@
             dv_ref[:, cols] = dv_acc[...].astype(jnp.bfloat16)
 
 
-class Spread(Nothing):
+class Spread:
     others = 3
-    n_in, n_out = 10, 4
     block = 256
     lag = (2, 5, 8)
-
-    def __init__(self, factors, columns):
-        rows, features = factors[0].shape
-        block, half = self.block, self.block // 2
-        assert features == 8 * block
-        self.rows = rows
-        self.operands = tuple(factors) + tuple(right for _, right, _, _ in columns)
-        self.in_specs = (ANY,) * self.n_in
-        self.table, self.phases = [], {}
-        at, widths = 0, [0] * 4
+    across = (True, False, False, True)
+
+    def __init__(self, lefts, columns, outs, left_now, scratch, start):
+        self.lefts, self.outs, self.x_buf, self.start = lefts, outs, left_now, start
+        self.table, self.phases, self.rights = [], {}, []
+        at = 0
         for number, (left, right, result, place) in enumerate(columns):
             self.phases.setdefault(left, at)
-            self.table.append((number, at, at + right.shape[1] // block, result, place))
-            at += right.shape[1] // block
-            widths[result] += right.shape[1]
+            self.table.append((number, at, at + right.shape[1] // self.block, result, place))
+            self.rights.append(right)
+            at += right.shape[1] // self.block
         self.chunks = at
-        self.steps = at + self.lag[2]
-        self.across = (True, False, False, True)
-        self.out_shape = tuple(
-            jax.ShapeDtypeStruct((block, n) if across else (n, block), jnp.float32)
-            for n, across in zip(widths, self.across)
-        )
-        self.out_specs = (ANY,) * 4
-        low = lambda *shape: pltpu.VMEM(shape, jnp.bfloat16)
-        wide = lambda *shape: pltpu.VMEM(shape, jnp.float32)
-        dma = lambda n: pltpu.SemaphoreType.DMA((n,))
-        self.scratch_shapes = (
-            low(2, rows, features),
-            low(2, rows, block),
-            low(3, 2, block, 2 * block),
-            wide(3, 2, block, 2 * block),
-            low(4, 2, block, 2 * block),
-            low(3, half, 2 * block),
-            low(3, 2, half, block),
-            wide(3, half, 2 * block),
-            wide(3, 2, half, block),
-            low(6, half, 2 * block),
-            low(6, 2, half, block),
-            low(3, 2, half, block),
-            wide(3, 2, half, block),
-            low(6, 2, half, block),
-            wide(3, block, block),
-            dma(2),
-            dma(2),
-            dma(3),
-            dma(4),
-            dma(3),
-            dma(6),
-            dma(3),
-            dma(6),
-            dma(3),
-            dma(6),
-            dma(3),
-            dma(6),
-            dma(3),
-        )
-
-    def __call__(self, ins, outs, scratch, accs):
-        self.lefts, self.rights, self.outs = ins[:4], ins[4:], outs
+        self.steps = start + at + self.lag[2]
         (
-            self.x_buf,
             self.y_buf,
             self.s1,
             self.own,
@@ -638,7 +597,28 @@
         self.to_core = {"item": item + 1 - 2 * self.core}
         self.to_x = {"item": item + 2 - 4 * self.x}
         self.to_y = {"seq": 1 - seq}
-        return self
+
+    @classmethod
+    def scratch(cls, rows):
+        block, half = cls.block, cls.block // 2
+        low = lambda *shape: pltpu.VMEM(shape, jnp.bfloat16)
+        wide = lambda *shape: pltpu.VMEM(shape, jnp.float32)
+        return [
+            low(2, rows, block),
+            low(3, 2, block, 2 * block),
+            wide(3, 2, block, 2 * block),
+            low(4, 2, block, 2 * block),
+            low(3, half, 2 * block),
+            low(3, 2, half, block),
+            wide(3, half, 2 * block),
+            wide(3, 2, half, block),
+            low(6, half, 2 * block),
+            low(6, 2, half, block),
+            low(3, 2, half, block),
+            wide(3, 2, half, block),
+            low(6, 2, half, block),
+            wide(3, block, block),
+        ] + [pltpu.SemaphoreType.DMA((n,)) for n in (1, 2, 3, 4, 3, 6, 3, 6, 3, 6, 3, 6, 3)]
 
     def greet(self, barrier):
         for to in (self.to_core, self.to_x, self.to_y):
@@ -646,8 +626,7 @@
 
 
     def left_copy(self, left):
-        slot = list(self.phases).index(left) % 2
-        return pltpu.make_async_copy(self.lefts[left], self.x_buf.at[slot], self.x_sem.at[slot])
+        return pltpu.make_async_copy(self.lefts[left], self.x_buf, self.x_sem.at[0])
 
     def right_copy(self, m, act):
         for number, start, stop, _, _ in self.table:
@@ -723,28 +702,27 @@
             ),
         )
 
-    def first(self):
-        for left in list(self.phases)[:2]:
-            self.left_copy(left).start()
-        self.right_copy(0, lambda copy: copy.start())
-
     def step(self, t):
+        @pl.when(t == self.start - 1)
+        def _():
+            self.left_copy(0).start()
+            self.right_copy(0, lambda copy: copy.start())
+
         for stage, lag in ((self.fourth, 8), (self.third, 5), (self.second, 2), (self.multiply, 0)):
-            m = t - lag
+            m = t - self.start - lag
 
             @pl.when((m >= 0) & (m < self.chunks))
             def _():
                 stage(m)
 
     def multiply(self, m):
-        order = list(self.phases)
-        for number, left in enumerate(order):
-
-            @pl.when(m == self.phases[left])
+        for left, start in self.phases.items():
+
+            @pl.when(m == start)
             def _():
+                if start > 0:
+                    self.left_copy(left).start()
                 self.left_copy(left).wait()
-                if 1 <= number < len(order) - 1:
-                    self.left_copy(order[number + 1]).start()
 
         @pl.when(m + 1 < self.chunks)
         def _():
@@ -756,13 +734,12 @@
         def _():
             self.first_copy(m - 3).wait_send()
 
-        phase = sum((m >= start).astype(jnp.int32) for start in self.phases.values()) - 1
         turned = self.y_buf[m % 2].T
         wide = 2 * self.block
 
         def product(x, core):
             cols = pl.ds(pl.multiple_of(x * 2 * wide + core * wide, wide), wide)
-            return mm(turned, self.x_buf[phase % 2, :, cols])
+            return mm(turned, self.x_buf[:, cols])
 
         for x in range(2):
             self.s1[m % 3, x] = product(x, 1 - self.core).astype(jnp.bfloat16)
@@ -1068,7 +1045,7 @@
         ffn_body(count, half, weights_job, None, *refs)
     else:
         facts, q, k, v, earlier, *rest = refs
-        inputs, outputs, scratch = rest[:9], rest[9:20], rest[20:]
+        inputs, outputs, scratch = rest[:9], rest[9:21], rest[21:]
         *outputs, attended, lse = outputs
         job = Attend(half, facts, q, k, v, earlier, attended, lse)
         ffn_body(count, half, weights_job, job, attended, *inputs, *outputs, *scratch)
@@ -1098,6 +1075,7 @@
     down_out,
     acc,
     acc_up,
+    acc_down,
     part1,
     moving1,
     part2,
@@ -1171,8 +1149,7 @@
         return pl.ds(pl.multiple_of(flow * half + g * group, 16), group)
 
     def mid_fetch(flow, g, here):
-        rows = pl.ds(pl.multiple_of(g * group, 16), group)
-        source = moving1.at[flow, rows] if here else mid.at[group_rows(flow, g)]
+        source = moving1.at[group_rows(flow, g)] if here else mid.at[group_rows(flow, g)]
         return pltpu.make_async_copy(source, mid_in.at[flow], mid_sem.at[flow])
 
     def cot_fetch(flow, g):
@@ -1195,6 +1172,7 @@
         def _():
             mid_fetch(flow, g, False).wait()
             cot_fetch(flow, g).wait()
+            acc_down[...] += fold(cot_in[flow].astype(jnp.float32))
 
             @pl.when(g > 0)
             def _():
@@ -1227,6 +1205,7 @@
     weights.greet(barrier)
     acc[...] = jnp.zeros_like(acc)
     acc_up[...] = jnp.zeros_like(acc_up)
+    acc_down[...] = jnp.zeros_like(acc_down)
     weights.first()
 
     @pl.when(owner)
@@ -1321,7 +1300,7 @@
     return pl.pallas_call(
         functools.partial(ffn_kernel, count, half, weights_job, len(attend_in)),
         in_specs=[SMEM, VMEM, VMEM, VMEM, VMEM][-len(attend_in) :] + [VMEM] * 5 + [ANY] * 4,
-        out_specs=[ANY] * 7 + [VMEM] * (2 + len(attend_out)),
+        out_specs=[ANY] * 7 + [VMEM] * (3 + len(attend_out)),
         out_shape=[
             low(rows, features),
             low(rows, ff),
@@ -1332,6 +1311,7 @@
             low(ff, features),
             wide(3, 8, features),
             wide(8, ff),
+            wide(8, features),
         ]
         + attend_out,
         scratch_shapes=first[:2]
@@ -1534,6 +1514,12 @@
         index = lax.axis_index(axis)
         return {axis: index + bit - 2 * bit * ((index // bit) % 2)}
 
+    def extra(self, row, start, grad):
+        cols = slice(start, start + grad.shape[1])
+        self.sent[0, row : row + 1, cols] = jnp.sum(
+            grad[...].astype(jnp.float32), axis=0, keepdims=True
+        )
+
     def greet(self, barrier):
         for axis, bit in self.stages:
             pl.semaphore_signal(
@@ -1550,10 +1536,12 @@
             device_id_type=MESH,
         )
 
+    def first(self):
+        self.sent[0] = self.own[...]
+
     def step(self, t):
         @pl.when(t == self.start)
         def _():
-            self.sent[0] = self.own[...]
             for number in range(self.acc.shape[0]):
                 self.sent[0, 3 + number : 4 + number, :] = jnp.sum(
                     self.acc[number], axis=0, keepdims=True
@@ -1574,6 +1562,322 @@
                     self.copy(number + 1).start()
                 else:
                     self.out[...] = total
+
+
+class Columns:
+    def __init__(self, ref, start, width):
+        self.ref, self.start, self.shape = ref, start, (ref.shape[0], width)
+
+    def __getitem__(self, index):
+        rows, cols = index
+        start = pl.multiple_of(self.start + cols.start, PAIR)
+        return self.ref[rows, pl.ds(start, cols.size)]
+
+
+class Ring:
+    depth = 4
+
+    def __init__(self, source, buffer, sems, pieces, offset):
+        self.source, self.buffer, self.sems = source, buffer, sems
+        self.pieces, self.offset = pieces, offset
+
+    @classmethod
+    def scratch(cls, features, dtype):
+        return [
+            pltpu.VMEM((cls.depth, PIECE, features), dtype),
+            pltpu.SemaphoreType.DMA((cls.depth,)),
+        ]
+
+    def copy(self, k):
+        rows = pl.ds(self.offset + k * PIECE, PIECE)
+        slot = k % self.depth
+        return pltpu.make_async_copy(
+            self.source.at[rows], self.buffer.at[slot], self.sems.at[slot]
+        )
+
+    def fill(self):
+        for k in range(min(self.depth, self.pieces)):
+            self.copy(k).start()
+
+    def take(self, k):
+        self.copy(k).wait()
+        value = self.buffer[k % self.depth].astype(jnp.float32)
+
+        @pl.when(k + self.depth < self.pieces)
+        def _():
+            self.copy(k + self.depth).start()
+
+        return value
+
+
+def back_kernel(
+    count,
+    half,
+    sizes,
+    facts,
+    lse,
+    earlier,
+    down_bias,
+    pre_gain,
+    small_own,
+    q_in,
+    k_in,
+    v_in,
+    do_in,
+    act,
+    down_in,
+    residual,
+    hidden,
+    grad_in,
+    qkv_in,
+    mid,
+    cotangent,
+    branch,
+    normed,
+    grad_pre,
+    attended,
+    hidden_out,
+    input_grad,
+    up_grad,
+    down_grad,
+    out_grad,
+    qkv_grad,
+    sums_out,
+    part,
+    moving1,
+    moving2,
+    down,
+    qkv_w,
+    dq,
+    dk,
+    dv,
+    dk_acc,
+    dv_acc,
+    k_t,
+    dks,
+    dvs,
+    swap_out,
+    swap_in,
+    act_in,
+    acc,
+    small_sent,
+    small_got,
+    *rest,
+):
+    rest = list(rest)
+    take = lambda n: [rest.pop(0) for _ in range(n)]
+    rings = take(6)
+    sems1, sems2 = take(5), take(5)
+    small_sems = take(2)
+    load_sem, act_sem, swap_sent, swap_got = take(4)
+    rows, width = 2 * half, dq.shape[1]
+    pieces = half // PIECE
+    me = lax.axis_index("mp")
+    owner = (me == 0) | (me == count - 1)
+    offset = jnp.where(me == 0, 0, half)
+    residual_ring = Ring(residual, *rings[0:2], pieces, 0)
+    grad_ring = Ring(grad_in, *rings[2:4], pieces, 0)
+    hidden_ring = Ring(hidden, *rings[4:6], pieces, offset)
+    group = part.shape[2]
+
+    def act_copy(flow, g):
+        return pltpu.make_async_copy(
+            act.at[pl.ds(pl.multiple_of(flow * half + g * group, 16), group)],
+            act_in.at[flow],
+            act_sem.at[flow],
+        )
+
+    def multiply_down(flow, g):
+        act_copy(flow, g).wait()
+        product = mm(act_in[flow], down[...])
+
+        @pl.when(g + 1 < half // group)
+        def _():
+            act_copy(flow, g + 1).start()
+
+        return product
+
+    def finish_first(flow, k, total):
+        return residual_ring.take(k) + total + down_bias[...]
+
+    def finish_second(flow, k, total):
+        values, inverse = norm_stats(hidden_ring.take(k))
+        acc[0] += fold(total * values)
+        acc[1] += fold(total)
+        return grad_ring.take(k) + norm_back(total, values, inverse, pre_gain[...])
+
+    line1 = Line(count, half, multiply_down, finish_first, hidden_out, part, moving1, sems1)
+    multiply_back = group_product([dq, dk, dv], qkv_w, NT, half, group)
+    line2 = Line(
+        count, half, multiply_back, finish_second, input_grad, part, moving2, sems2, late=True
+    )
+    heads = AttendBack.__new__(AttendBack)
+    heads.bq = query_block(rows)
+    heads.blocks = rows // heads.bq
+    heads.pairs = width // PAIR
+    heads.steps = heads.pairs * heads.blocks
+    heads.causal = True
+    views = [Columns(moving2, j * width, width) for j in range(4)]
+    tables = [earlier.at[0], earlier.at[1]]
+    heads.ins = (facts, *views[:3], *tables, views[3], lse)
+    heads.outs = (dq, dk, dv, dks, dvs)
+    heads.scratch = (dk_acc, dv_acc, k_t)
+    second = heads.steps + 2
+    columns = (
+        (0, grad_pre, 0, 0),
+        (1, act, 1, 0),
+        (2, attended, 2, 0),
+        (3, dq, 3, 0),
+        (3, dk, 3, width),
+        (3, dv, 3, 2 * width),
+    )
+    spread = Spread(
+        (mid, cotangent, branch, normed),
+        columns,
+        (up_grad, down_grad, out_grad, qkv_grad),
+        down.at[pl.ds(0, rows)],
+        rest,
+        heads.steps - 2,
+    )
+    small = SmallSums(sizes, 6, second + pieces + SKEW * (count - 1), small_own)
+    small((small_own,), (sums_out,), (small_sent, small_got, *small_sems), (acc,))
+    loads = [
+        pltpu.make_async_copy(source, target, load_sem.at[number])
+        for number, (source, target) in enumerate(
+            [(down_in, down), (qkv_in, qkv_w)]
+            + [
+                (source, moving2.at[:, pl.ds(j * width, width)])
+                for j, source in enumerate((q_in, k_in, v_in, do_in))
+            ]
+        )
+    ]
+    swap = pltpu.make_async_remote_copy(
+        src_ref=swap_out,
+        dst_ref=swap_in,
+        send_sem=swap_sent.at[0],
+        recv_sem=swap_got.at[0],
+        device_id=spread.to_y,
+        device_id_type=MESH,
+    )
+
+    barrier = pltpu.get_barrier_semaphore()
+    line1.greet(barrier)
+    spread.greet(barrier)
+    small.greet(barrier)
+    for flow in range(2):
+        act_copy(flow, 0).start()
+    for load in loads:
+        load.start()
+
+    @pl.when(owner)
+    def _():
+        for ring in (residual_ring, grad_ring, hidden_ring):
+            ring.fill()
+
+    acc[...] = jnp.zeros_like(acc)
+    small.first()
+    loads[0].wait()
+    line1.first()
+    line1.meet(barrier, spread.others + small.others)
+    for load in loads[1:]:
+        load.wait()
+
+    def step(t, carry):
+        line1.step(t)
+        heads.step(t)
+
+        @pl.when(t == heads.steps)
+        def _():
+            swap_out[0] = dks[...].astype(jnp.bfloat16)
+            swap_out[1] = dvs[...].astype(jnp.bfloat16)
+            swap.start()
+
+        @pl.when(t == heads.steps + 1)
+        def _():
+            swap.wait()
+            shape = (rows, SUMM_ROWS)
+            chosen = lax.broadcasted_iota(jnp.int32, shape, 0) == (
+                facts[1] - SUMM + lax.broadcasted_iota(jnp.int32, shape, 1)
+            )
+            chosen = jnp.where(chosen, 1.0, 0.0).astype(jnp.bfloat16)
+            for number, grad in enumerate((dk, dv)):
+                added = grad[...].astype(jnp.float32) + mm(chosen, swap_in[number])
+                grad[...] = added.astype(jnp.bfloat16)
+            for number, grad in enumerate((dq, dv)):
+                small.extra(6 + down_in.shape[0] // down_in.shape[1], number * width, grad)
+
+        line2.step(t - second)
+        spread.step(t)
+        small.step(t)
+        return carry
+
+    lax.fori_loop(0, max(second + line2.steps, spread.steps, small.steps), step, 0)
+    line1.settle()
+    line2.settle()
+    spread.settle()
+
+
+def back_sums(number, count, sizes, small_in, whole_in, vmem_in):
+    rows, width = whole_in[0].shape
+    features = whole_in[5].shape[1]
+    ff = whole_in[5].shape[0]
+    half = rows // 2
+    low = lambda *shape: pltpu.VMEM(shape, jnp.bfloat16)
+    wide = lambda *shape: pltpu.VMEM(shape, jnp.float32)
+    dma = lambda *shape: pltpu.SemaphoreType.DMA(shape)
+    lines = Line.scratch(half, features)
+    group = lines[0].shape[2]
+    stages = sum(size.bit_length() - 1 for _, size in sizes)
+    block = Spread.block
+    return pl.pallas_call(
+        functools.partial(back_kernel, count, half, sizes),
+        in_specs=[SMEM] + [VMEM] * 5 + [ANY] * len(whole_in),
+        out_specs=[ANY] * 6 + [VMEM],
+        out_shape=[
+            jax.ShapeDtypeStruct((rows, features), jnp.bfloat16),
+            jax.ShapeDtypeStruct((rows, features), jnp.bfloat16),
+            jax.ShapeDtypeStruct((block, ff), jnp.float32),
+            jax.ShapeDtypeStruct((ff, block), jnp.float32),
+            jax.ShapeDtypeStruct((width, block), jnp.float32),
+            jax.ShapeDtypeStruct((block, 3 * width), jnp.float32),
+            jax.ShapeDtypeStruct(small_in.shape, jnp.float32),
+        ],
+        scratch_shapes=[
+            lines[0],
+            lines[1],
+            lines[1],
+            low(ff, features),
+            low(features, 3 * width),
+            low(rows, width),
+            low(rows, width),
+            low(rows, width),
+            wide(rows, PAIR),
+            wide(rows, PAIR),
+            low(PAIR, rows),
+            wide(SUMM_ROWS, width),
+            wide(SUMM_ROWS, width),
+            low(2, SUMM_ROWS, width),
+            low(2, SUMM_ROWS, width),
+            low(2, group, ff),
+            wide(2, 8, features),
+            wide(stages, *small_in.shape),
+            wide(stages, *small_in.shape),
+        ]
+        + Ring.scratch(features, jnp.float32)
+        + Ring.scratch(features, jnp.float32)
+        + Ring.scratch(features, jnp.bfloat16)
+        + lines[2:]
+        + lines[2:]
+        + [dma(stages), dma(stages), dma(6), dma(2), dma(1), dma(1)]
+        + Spread.scratch(rows),
+        compiler_params=pltpu.CompilerParams(
+            collective_id=number, has_side_effects=True, vmem_limit_bytes=63 * MIB
+        ),
+        cost_estimate=pl.CostEstimate(
+            flops=12 * rows * features * ff, bytes_accessed=60 * rows * features, transcendentals=0
+        ),
+        name="back_sums",
+    )(*vmem_in, small_in, *whole_in)
 
 
 def gradients_over(group, lefts, columns):
@@ -1662,6 +1966,7 @@
         down_full,
         mid_sums,
         up_sums,
+        down_sums,
         *attend_out,
     ) = ffn_sums(
         1,
@@ -1678,62 +1983,73 @@
     if ours:
         attended, log_total = attend_out
     grad_attended = mm(grad_branch, out_full, NT).astype(jnp.bfloat16)
-    hidden_out, dq, dk, dv, dks, dvs = line_sum(
-        3,
-        mp_count,
-        [act_low],
-        down_full,
-        NN,
-        [residual, row(down_bias)],
-        0,
-        0,
-        finish_out,
-        "down_sum",
-        (AttendBack(facts, q, *tables, grad_attended, log_total),),
-    )
-    dk, dv = keys_back(jnp.stack([dk, dv]), jnp.stack([dks, dvs]), rows, lengths, seq_count)
-    lefts = (mid_low, grad_down, grad_branch, normed)
-    columns = (
-        (0, grad_pre, 0, 0),
-        (1, act_low, 1, 0),
-        (2, attended, 2, 0),
-        (3, dq, 3, 0),
-        (3, dk, 3, width),
-        (3, dv, 3, 2 * width),
-    )
     total = lambda value: jnp.sum(value.astype(jnp.float32), axis=0)
     features = hidden.shape[1]
-    qv_sums = jnp.concatenate([total(dq), total(dv)])
-    small = SmallSums(
-        [("item", item_count), ("seq", seq_count), ("mp", mp_count)],
-        6,
-        rows // 2 // PIECE + SKEW * (mp_count - 1),
-        jnp.concatenate(
-            [
-                jnp.sum(mid_sums, axis=1),
-                jnp.zeros((2, features), jnp.float32),
-                row(jnp.where(lax.axis_index("mp") == 0, total(grad_down), 0.0)),
-                total(up_sums).reshape(-1, features),
-                jnp.pad(qv_sums, (0, -qv_sums.shape[0] % features)).reshape(-1, features),
-            ]
-        ),
+    sizes = [("item", item_count), ("seq", seq_count), ("mp", mp_count)]
+    once = lambda value: jnp.where(lax.axis_index("mp") == 0, value, 0.0)
+    small_in = lambda qv_sums: jnp.concatenate(
+        [
+            jnp.sum(mid_sums, axis=1),
+            jnp.zeros((2, features), jnp.float32),
+            row(once(total(down_sums))),
+            total(up_sums).reshape(-1, features),
+            jnp.pad(qv_sums, (0, -qv_sums.shape[0] % features)).reshape(-1, features),
+        ]
     )
-    grad_input, _, *weight_grads, sums = line_sum(
-        4,
-        mp_count,
-        [dq, dk, dv],
-        qkv_full,
-        NT,
-        [hidden_in[0], grad_residual, row(pre_gain)],
-        0,
-        2,
-        finish_input,
-        "input_sum",
-        ((Spread(lefts, columns),) if ours else ()) + (small,),
-    )
-    if not weight_grads:
-        weight_grads = gradients_over(group, lefts, columns)
-    up_grad, down_grad, out_grad, qkv_grad = weight_grads
+    if ours:
+        hidden_out, grad_input, up_grad, down_grad, out_grad, qkv_grad, sums = back_sums(
+            2,
+            mp_count,
+            sizes,
+            small_in(jnp.zeros((2 * width,), jnp.float32)),
+            (q, k, v, grad_attended, act_low, down_full, residual, hidden_in[0], grad_residual)
+            + (qkv_full, mid_low, grad_down, grad_branch, normed, grad_pre, attended),
+            (facts, log_total, summary, row(down_bias), row(pre_gain)),
+        )
+    else:
+        hidden_out, dq, dk, dv, dks, dvs = line_sum(
+            3,
+            mp_count,
+            [act_low],
+            down_full,
+            NN,
+            [residual, row(down_bias)],
+            0,
+            0,
+            finish_out,
+            "down_sum",
+            (AttendBack(facts, q, *tables, grad_attended, log_total),),
+        )
+        dk, dv = keys_back(jnp.stack([dk, dv]), jnp.stack([dks, dvs]), rows, lengths, seq_count)
+        small = SmallSums(
+            sizes,
+            6,
+            rows // 2 // PIECE + SKEW * (mp_count - 1),
+            small_in(jnp.concatenate([total(dq), total(dv)])),
+        )
+        grad_input, _, sums = line_sum(
+            4,
+            mp_count,
+            [dq, dk, dv],
+            qkv_full,
+            NT,
+            [hidden_in[0], grad_residual, row(pre_gain)],
+            0,
+            2,
+            finish_input,
+            "input_sum",
+            (small,),
+        )
+        lefts = (mid_low, grad_down, grad_branch, normed)
+        columns = (
+            (0, grad_pre, 0, 0),
+            (1, act_low, 1, 0),
+            (2, attended, 2, 0),
+            (3, dq, 3, 0),
+            (3, dk, 3, width),
+            (3, dv, 3, 2 * width),
+        )
+        up_grad, down_grad, out_grad, qkv_grad = gradients_over(group, lefts, columns)
     ff_rows = up_weight.shape[1] // features
     up_bias_grad = sums[6 : 6 + ff_rows].reshape(-1)
     qv_bias_grad = sums[6 + ff_rows :].reshape(-1)[: 2 * width].reshape(2, width)

time: 675 us -> 625 us (0.926)
  Pallas kernels: 616 us -> 586 us
    pallas_call x2 -> x1, Pallas kernels: 297 us -> 268 us  [back_sums(): pl.pallas_call(functools.partial(back_kernel, count, half, sizes), in_spe...]
  transfers between devices with their start and end apart: 1 -> 0, of which waited for: 0 -> 0; matrix products, arithmetic and copies ran while one was open for 1% -> 0% of each run, Pallas kernels for 0% -> 0%
where the time goes in v6:
time: 625 us; the launch traced here: 622 us
  Pallas kernels  586 us (94%)
  local copies, waits for them, and re-layouts  16.5 us (3%)
  other arithmetic  10.8 us (2%)
  matrix products  7.17 us (1%)
    pallas_call x1, Pallas kernels, ffn_sums(): pl.pallas_call(functools.partial(ffn_kernel, count, half, weights_job, le...  269 us
    pallas_call x1, Pallas kernels, back_sums(): pl.pallas_call(functools.partial(back_kernel, count, half, sizes), in_spe...  268 us
    pallas_call x1, Pallas kernels, start(): pl.pallas_call(start_kernel, in_specs=[SMEM] + [VMEM] * 4 + [ANY] * 2, ou...  49.1 us

profile of v6, /device:TPU:0, one launch (start us, length us, event | category | flops | bytes accessed | tf_op | source)
XLA Modules:
  0.0 621.5 jit_solution(16653826168574735912)
XLA Ops:
  0.7 1.2 fusion.1
  1.9 1.2 pad_add_fusion.facts.refs_0_
  3.2 1.4 copy.31
  4.6 1.2 copy.32.shard
  5.7 49.1 %start.1 = (bf16[1280,512]{1,0:T(8,128)(2,1)}, bf16[1280,512]{1,0:T(8,128)(2,1)}, bf16[1280,512]{1,0:T(8,128)(2,1)}, bf16[2,64,512]{2,1,0:T(8,128)(2,1)}, bf16[1...) custom-call(s32[3]{0:T(128)} %pad_add_fusion.facts.refs_0_, ...), custom_call_target="tpu_custom_call" | custom-call | flops 8053063680 | bytes 41943040 | tf_op jit(solution)/shard_map/start/pallas_call | solution.py:1465
  54.9 269.1 %ffn_sums.1 = (bf16[1280,2048]{1,0:T(8,128)(2,1)}, bf16[1280,2048]{1,0:T(8,128)(2,1)}, bf16[1280,2048]{1,0:T(8,128)(2,1)}, f32[640,2048]{1,0:T(8,128)}, bf16[128...) custom-call(s32[3]{0:T(128)} %pad_add_fusion.facts.refs_0_, ...), custom_call_target="tpu_custom_call" | custom-call | flops 32212254720 | bytes 78643200 | tf_op jit(solution)/shard_map/ffn_sums/pallas_call | solution.py:1300
  323.9 0.0 copy-start.5
  323.9 0.0 copy-start.4
  323.9 0.0 copy-start.3
  324.0 7.2 %convolution_convert_fusion.do_in = bf16[1280,512]{1,0:T(8,128)(2,1)} fusion(bf16[1280,2048]{1,0:T(8,128)(2,1)} %get-tuple-element.49.branch, bf16[512,2048]{1,0:T(8,128)(2,1)} %get-tuple-element.44.refs_5_), kind=kOutput, calls=%fused_computation.1 | convolution fusion | flops 2685009920 | bytes 8650752 | tf_op jit(solution)/shard_map/dot_general | solution.py:32
  331.1 0.0 copy-done.5
  331.2 0.0 copy-done.4
  331.2 0.0 copy-done.3
  331.2 0.1 reduce_sum.27
  331.3 0.7 concatenate.3.small_own
  332.0 267.9 %back_sums.1 = (bf16[1280,2048]{1,0:T(8,128)(2,1)}, bf16[1280,2048]{1,0:T(8,128)(2,1)}, f32[256,2048]{1,0:T(8,128)}, f32[2048,256]{1,0:T(8,128)}, f32[512,256]{1...) custom-call(s32[3]{0:T(128)} %pad_add_fusion.facts.refs_0_, f32[4,2,1280]{2,1,0:T(2,128)} %get-tuple-element.45.lse, ...), custom_call_target="tpu_custom_call" | custom-call | flops 64424509440 | bytes 157286400 | tf_op jit(solution)/shard_map/back_sums/pallas_call | solution.py:1832
  599.9 0.8 slice_reduce_fusion
  600.6 2.1 fusion
  602.7 0.6 reshape.68
  603.3 1.9 copy.33
  605.2 0.0 slice-start
  605.2 1.6 copy.34
  606.8 0.0 slice-start.1
  606.8 8.2 %bitcast_convert_fusion = f32[1,1280,2048]{2,1,0:T(8,128)} fusion(bf16[1280,2048]{1,0:T(8,128)(2,1)} %get-tuple-element.60), kind=kLoop, calls=%fused_computation | loop fusion | flops 2621440 | bytes 15728640 | tf_op jit(solution)/shard_map/broadcast_in_dim | solution.py:2058
  615.0 0.0 slice-done
  615.0 0.0 slice-done.1
  615.0 0.0 copy-start.2
  615.0 0.0 copy-start.1
  615.0 2.7 copy.39
  617.7 0.0 copy-done.2
  617.7 0.0 copy-start
  617.7 0.8 copy.40
  618.5 0.2 copy-done.1
  618.7 1.3 copy.41
  620.0 0.0 copy-done
  620.0 1.3 copy.42
  (7 shorter events, 0.1 us)
Async XLA Ops:
  323.9 7.2 %copy-start.5 = (f32[8,2048]{1,0:T(8,128)S(1)}, f32[8,2048]{1,0:T(8,128)}, u32[]{:S(2)}) copy-start(f32[8,2048]{1,0:T(8,128)} %get-tuple-element.47) | copy-start | bytes 196612
  323.9 7.2 %copy-start.4 = (f32[8,2048]{1,0:T(8,128)S(1)}, f32[8,2048]{1,0:T(8,128)}, u32[]{:S(2)}) copy-start(f32[8,2048]{1,0:T(8,128)} %get-tuple-element.48) | copy-start | bytes 196612
  323.9 7.3 %copy-start.3 = (f32[3,8,2048]{2,1,0:T(8,128)S(1)}, f32[3,8,2048]{2,1,0:T(8,128)}, u32[]{:S(2)}) copy-start(f32[3,8,2048]{2,1,0:T(8,128)} %get-tuple-element.46) | copy-start | bytes 589828
  605.2 9.8 %slice-start = ((s8[5242880]{0:T(1024)(128)(4,1)}), s8[1048576]{0:T(1024)(128)(4,1)S(1)}, s32[]{:S(2)}) async-start(s8[5242880]{0:T(1024)(128)(4,1)} %bitcast.31), calls=%async_computation | async-start | bytes 2097152
  606.8 8.2 %slice-start.1 = ((s8[5242880]{0:T(1024)(128)(4,1)}), s8[4194304]{0:T(1024)(128)(4,1)S(1)}, s32[]{:S(2)}) async-start(s8[5242880]{0:T(1024)(128)(4,1)} %bitcast.31), calls=%async_computation.1 | async-start | bytes 8388608
  615.0 2.7 copy-start.2
  615.0 3.7 copy-start.1
  617.7 2.3 copy-start

commit v7 on v6

--- a/solution.py
+++ b/solution.py
@@ -17,6 +17,8 @@
 PAIR = 2 * HDIM
 PIECE = 32
 SKEW = 2
+LEAD = 2
+GATHER_STEPS = (7, 11, 13, 15)
 MIB = 1 << 20
 MESH = pl.DeviceIdType.MESH
 MASKED = -1e30
@@ -62,6 +64,15 @@
     own = lax.broadcasted_iota(jnp.int32, (nk, bq), 0) < limit
     earlier = lax.broadcasted_iota(jnp.int32, (SUMM_ROWS, bq), 0) < facts_ref[2]
     return own, earlier
+
+
+class Facts:
+    def __init__(self, lengths):
+        segment = lax.axis_index("seq")
+        self.values = (0, lengths[0, segment] + SUMM, jnp.where(segment > 0, SUMM, 0))
+
+    def __getitem__(self, index):
+        return self.values[index]
 
 
 def head_lanes(head):
@@ -178,12 +189,12 @@
         dma = lambda *shape: pltpu.SemaphoreType.DMA(shape)
         return [
             pltpu.VMEM((2, 2, group, features), jnp.float32),
-            pltpu.VMEM((2 * half, features), jnp.bfloat16),
+            pltpu.VMEM((2 * (half + LEAD * PIECE), features), jnp.bfloat16),
             dma(2, pieces),
             dma(2, pieces),
             dma(2, pieces),
             dma(2, pieces),
-            dma(pieces),
+            dma(2, pieces),
         ]
 
     def place(self, flow):
@@ -215,8 +226,18 @@
         for flow in range(2):
             self.part[flow, 0] = self.multiply(flow, 0)
 
+    def spot(self, flow, k):
+        return flow * (self.half + LEAD * PIECE) + k * PIECE
+
+    def spots(self, flow, k, size=PIECE):
+        return pl.ds(pl.multiple_of(self.spot(flow, k), PIECE), size)
+
+    def finished(self, flow, k, size):
+        mine = self.place(flow) == self.count - 1
+        return self.spots(flow, jnp.where(mine, k + LEAD, k), size)
+
     def onward(self, flow, k):
-        here = self.moving.at[pl.ds(flow * self.half + k * PIECE, PIECE)]
+        here = self.moving.at[self.spots(flow, k + LEAD)]
         return pltpu.make_async_remote_copy(
             src_ref=here,
             dst_ref=here,
@@ -227,29 +248,36 @@
         )
 
     def back(self, flow, k, owner):
-        rows = self.out.at[pl.ds(flow * self.half + k * PIECE, PIECE)]
+        here = self.moving.at[self.spots(flow, k)]
         return pltpu.make_async_remote_copy(
-            src_ref=self.moving.at[pl.ds(flow * self.half + k * PIECE, PIECE)] if owner else rows,
-            dst_ref=rows,
+            src_ref=self.moving.at[self.spots(flow, k + LEAD)] if owner else here,
+            dst_ref=here,
             send_sem=self.down_sent.at[flow, k],
             recv_sem=self.down_got.at[flow, k],
             device_id={"mp": self.me + 1 if flow == 0 else self.me - 1},
             device_id_type=MESH,
         )
 
-    def keep(self, flow, k):
+    def keep(self, flow, k, owner):
         return pltpu.make_async_copy(
-            self.moving.at[pl.ds(flow * self.half + k * PIECE, PIECE)],
+            self.moving.at[self.spots(flow, k + LEAD if owner else k)],
             self.out.at[pl.ds(flow * self.half + k * PIECE, PIECE)],
-            self.local.at[k],
-        )
+            self.local.at[flow, k],
+        )
+
+    def send_on(self, flow, k):
+        @pl.when(k >= LEAD)
+        def _():
+            self.onward(flow, k - LEAD).wait_send()
+
+        self.onward(flow, k).start()
 
     def step(self, t):
         last = self.count - 1
         for flow in range(2):
             place = self.place(flow)
             k = t - SKEW * place
-            here = pl.ds(pl.multiple_of(flow * self.half + k * PIECE, PIECE), PIECE)
+            here = self.spots(flow, k + LEAD)
             busy = (k >= 0) & (k < self.pieces)
 
             def mine():
@@ -260,14 +288,14 @@
             @pl.when(busy & (place == 0))
             def _():
                 self.moving[here, :] = mine().astype(jnp.bfloat16)
-                self.onward(flow, k).start()
+                self.send_on(flow, k)
 
             @pl.when(busy & (place > 0) & (place < last))
             def _():
                 self.onward(flow, k).wait_recv()
                 total = mine() + self.moving[here, :].astype(jnp.float32)
                 self.moving[here, :] = total.astype(jnp.bfloat16)
-                self.onward(flow, k).start()
+                self.send_on(flow, k)
 
             @pl.when(busy & (place == last))
             def _():
@@ -275,7 +303,7 @@
                 total = mine() + self.moving[here, :].astype(jnp.float32)
                 self.moving[here, :] = self.finish(flow, k, total).astype(jnp.bfloat16)
                 self.back(flow, k, True).start()
-                self.keep(flow, k).start()
+                self.keep(flow, k, True).start()
 
         for flow in range(2):
             place = self.place(flow)
@@ -289,6 +317,8 @@
                 def _():
                     self.back(flow, j, False).start()
 
+                self.keep(flow, j, False).start()
+
         for flow in range(2 if self.multiply else 0):
             k = t - SKEW * self.place(flow)
             g = k // self.per_group + 1
@@ -304,22 +334,28 @@
                 self.part[flow, g % 2] = self.multiply(flow, g)
 
     def settle(self):
+        last = self.count - 1
+
         def one(k, carry):
             for flow in range(2):
                 place = self.place(flow)
 
-                @pl.when(place < self.count - 1)
+                @pl.when((place < last) & (k >= self.pieces - LEAD))
                 def _():
                     self.onward(flow, k).wait_send()
 
-                    @pl.when(place > 0)
-                    def _():
-                        self.back(flow, k, False).wait_send()
-
-                @pl.when(place == self.count - 1)
+                @pl.when((place > 0) & (place < last))
+                def _():
+                    self.back(flow, k, False).wait_send()
+
+                @pl.when(place < last)
+                def _():
+                    self.keep(flow, k, False).wait()
+
+                @pl.when(place == last)
                 def _():
                     self.back(flow, k, True).wait_send()
-                    self.keep(flow, k).wait()
+                    self.keep(flow, k, True).wait()
 
             return carry
 
@@ -496,7 +532,7 @@
         pair = t // self.blocks
         for block in range(self.blocks):
 
-            @pl.when((t < self.steps) & (t % self.blocks == block))
+            @pl.when((t >= 0) & (t < self.steps) & (t % self.blocks == block))
             def _():
                 self.unit(pair, block)
 
@@ -871,10 +907,10 @@
             device_id_type=MESH,
         )
 
-    def messages(self, w):
+    def plan(self, w):
         c, x, y = self.core, self.x, self.y
         own, spot = self.shards[w].at[...], functools.partial(self.spot, w)
-        plan = (
+        return (
             (own, spot(x, c, y), spot(x, 1 - c, y), self.to_core),
             (own, spot(x, c, y), spot(1 - x, c, y), self.to_x),
             (own, spot(x, c, y), spot(x, c, 1 - y), self.to_y),
@@ -885,23 +921,17 @@
             (None, spot(1 - x, c, 1 - y, 0), spot(1 - x, 1 - c, 1 - y, 0), self.to_core),
             (None, spot(1 - x, c, 1 - y, 1), spot(1 - x, 1 - c, 1 - y, 1), self.to_core),
         )
-        return [
-            (
-                self.message(w, number, out if src is None else src, out, to),
-                self.message(w, number, landing, landing, to),
-            )
-            for number, (src, out, landing, to) in enumerate(plan)
-        ]
-
     def send(self, w, numbers):
-        messages = self.messages(w)
+        plan = self.plan(w)
         for number in numbers:
-            messages[number][0].start()
+            src, out, _, to = plan[number]
+            self.message(w, number, out if src is None else src, out, to).start()
 
     def receive(self, w, numbers):
-        messages = self.messages(w)
+        plan = self.plan(w)
         for number in numbers:
-            messages[number][1].wait_recv()
+            _, _, landing, to = plan[number]
+            self.message(w, number, landing, landing, to).wait_recv()
 
     def mine(self, w):
         return pltpu.make_async_copy(
@@ -917,14 +947,14 @@
             self.send(w, (1, 2, 0))
 
     def step(self, t):
-        for w, at in ((0, self.ready * 5 // 16), (1, self.ready * 9 // 16)):
+        for w, at in ((0, GATHER_STEPS[0]), (1, GATHER_STEPS[1])):
 
             @pl.when(t == at)
             def _():
                 self.receive(w, (1, 2))
                 self.send(w, (3, 4, 5, 6))
 
-        for w, at in ((0, self.ready * 12 // 16), (1, self.ready * 15 // 16)):
+        for w, at in ((0, GATHER_STEPS[2]), (1, GATHER_STEPS[3])):
 
             @pl.when(t == at)
             def _():
@@ -939,8 +969,8 @@
 
     def settle(self):
         for w in range(len(self.shards)):
-            for out, _ in self.messages(w):
-                out.wait_send()
+            for number, (src, out, _, to) in enumerate(self.plan(w)):
+                self.message(w, number, out if src is None else src, out, to).wait_send()
 
 
 class Load:
@@ -997,7 +1027,7 @@
             for flow in range(2):
                 self.unit(pair, flow * self.blocks + block)
 
-        @pl.when(t < 2)
+        @pl.when((t >= 0) & (t < 2))
         def _():
             each = self.pairs // 2
 
@@ -1044,10 +1074,18 @@
     if n_attend == 1:
         ffn_body(count, half, weights_job, None, *refs)
     else:
-        facts, q, k, v, earlier, *rest = refs
-        inputs, outputs, scratch = rest[:9], rest[9:21], rest[21:]
+        lengths, earlier, *rest = refs
+        sources, rest = rest[:3], rest[3:]
+        inputs, outputs, scratch = rest[:9], rest[9:22], rest[22:]
         *outputs, attended, lse = outputs
-        job = Attend(half, facts, q, k, v, earlier, attended, lse)
+        *scratch, q, k, v, sems = scratch
+        job = Attend(half, Facts(lengths), q, k, v, earlier, attended, lse)
+        job.loads = [
+            pltpu.make_async_copy(source, target, sems.at[number])
+            for number, (source, target) in enumerate(zip(sources, (q, k, v)))
+        ]
+        for load in job.loads:
+            load.start()
         ffn_body(count, half, weights_job, job, attended, *inputs, *outputs, *scratch)
 
 
@@ -1076,6 +1114,7 @@
     acc,
     acc_up,
     acc_down,
+    grad_attended,
     part1,
     moving1,
     part2,
@@ -1084,16 +1123,17 @@
     residual,
     up,
     down,
-    mid_in,
     cot_in,
     act_out,
     pre_out,
+    attended_out,
     *sems,
 ):
     sems = list(sems)
     take = lambda n: [sems.pop(0) for _ in range(n)]
     sems1, sems2, weight_sems = take(5), take(5), take(3)
-    in_sem, residual_sem, grad_sem, mid_sem, cot_sem, act_sem, pre_sem, down_sem = sems
+    in_sem, residual_sem, grad_sem, cot_sem, act_sem, pre_sem, down_sem = sems[:7]
+    (attended_sem,) = sems[7:]
     me = lax.axis_index("mp")
     group = part2.shape[2]
     blocks = 4
@@ -1148,10 +1188,6 @@
     def group_rows(flow, g):
         return pl.ds(pl.multiple_of(flow * half + g * group, 16), group)
 
-    def mid_fetch(flow, g, here):
-        source = moving1.at[group_rows(flow, g)] if here else mid.at[group_rows(flow, g)]
-        return pltpu.make_async_copy(source, mid_in.at[flow], mid_sem.at[flow])
-
     def cot_fetch(flow, g):
         return pltpu.make_async_copy(
             cotangent.at[group_rows(flow, g)], cot_in.at[flow], cot_sem.at[flow]
@@ -1170,7 +1206,6 @@
     def products(flow, g, number):
         @pl.when(number == 0)
         def _():
-            mid_fetch(flow, g, False).wait()
             cot_fetch(flow, g).wait()
             acc_down[...] += fold(cot_in[flow].astype(jnp.float32))
 
@@ -1180,7 +1215,7 @@
                 pre_copy(flow, g - 1).wait()
 
         cols = pl.ds(pl.multiple_of(number * block, block), block)
-        value, slope = gelu_parts(mm(mid_in[flow], up[:, cols]) + up_bias[:, cols])
+        value, slope = gelu_parts(mm(moving1[line1.finished(flow, g * per_group, group), :], up[:, cols]) + up_bias[:, cols])
         act_out[flow, :, cols] = value.astype(jnp.bfloat16)
         pre = (slope * mm(cot_in[flow], down[cols, :], NT)).astype(jnp.bfloat16)
         pre_out[flow, :, cols] = pre
@@ -1199,6 +1234,19 @@
         def _():
             act_copy(flow, g).start()
             pre_copy(flow, g).start()
+
+    def attended_copy(flow, g):
+        return pltpu.make_async_copy(
+            attended_out.at[flow], grad_attended.at[group_rows(flow, g)], attended_sem.at[flow]
+        )
+
+    def through_out(flow, g):
+        @pl.when(g > 0)
+        def _():
+            attended_copy(flow, g - 1).wait()
+
+        attended_out[flow] = mm(moving2[line2.finished(flow, g * per_group, group), :], out_w[...], NT).astype(jnp.bfloat16)
+        attended_copy(flow, g).start()
 
     barrier = pltpu.get_barrier_semaphore()
     line1.greet(barrier)
@@ -1223,6 +1271,8 @@
     else:
         line1.meet(barrier, weights.others)
         weights.begin()
+        for load in attention.loads:
+            load.wait()
         attention.first()
         line1.first()
 
@@ -1245,20 +1295,17 @@
 
             @pl.when((fetch >= 0) & (fetch % per_group == 0) & (fetch < pieces))
             def _():
-                g = fetch // per_group
-                cot_fetch(flow, g).start()
-
-                @pl.when(place == last)
-                def _():
-                    mid_fetch(flow, g, True).start()
-
-                @pl.when(place < last)
-                def _():
-                    mid_fetch(flow, g, False).start()
+                cot_fetch(flow, fetch // per_group).start()
 
             @pl.when((compute >= 0) & (compute < pieces) & (compute % per_group < blocks))
             def _():
                 products(flow, compute // per_group, compute % per_group)
+
+            here = t - second - SKEW * (2 * last - place)
+
+            @pl.when((here >= 0) & (here < pieces) & (here % per_group == per_group - 1))
+            def _():
+                through_out(flow, here // per_group)
 
         return carry
 
@@ -1270,6 +1317,7 @@
     for flow in range(2):
         act_copy(flow, pieces // per_group - 1).wait()
         pre_copy(flow, pieces // per_group - 1).wait()
+        attended_copy(flow, pieces // per_group - 1).wait()
 
     @pl.when(owner)
     def _():
@@ -1287,9 +1335,11 @@
     pieces = half // PIECE
     low = lambda *shape: jax.ShapeDtypeStruct(shape, jnp.bfloat16)
     wide = lambda *shape: jax.ShapeDtypeStruct(shape, jnp.float32)
-    attend_out = []
+    attend_out, attend_scratch = [], []
     if len(attend_in) > 1:
-        width = attend_in[1].shape[1]
+        width = attend_in[2].shape[1]
+        attend_scratch = [pltpu.VMEM((rows, width), jnp.bfloat16)] * 3
+        attend_scratch += [pltpu.SemaphoreType.DMA((3,))]
         attend_out = [low(rows, width), wide(width // PAIR, 2, rows)]
     first = Line.scratch(half, features)
     small = 64 if half % 64 == 0 else PIECE
@@ -1299,8 +1349,8 @@
     dma = lambda n: pltpu.SemaphoreType.DMA((n,))
     return pl.pallas_call(
         functools.partial(ffn_kernel, count, half, weights_job, len(attend_in)),
-        in_specs=[SMEM, VMEM, VMEM, VMEM, VMEM][-len(attend_in) :] + [VMEM] * 5 + [ANY] * 4,
-        out_specs=[ANY] * 7 + [VMEM] * (3 + len(attend_out)),
+        in_specs=([SMEM, VMEM] + [ANY] * 3 if len(attend_in) > 1 else [VMEM]) + [VMEM] * 5 + [ANY] * 4,
+        out_specs=[ANY] * 7 + [VMEM] * 3 + [ANY] + [VMEM] * len(attend_out),
         out_shape=[
             low(rows, features),
             low(rows, ff),
@@ -1312,6 +1362,7 @@
             wide(3, 8, features),
             wide(8, ff),
             wide(8, features),
+            low(rows, out_w.shape[0]),
         ]
         + attend_out,
         scratch_shapes=first[:2]
@@ -1322,14 +1373,16 @@
             pltpu.VMEM((features, ff), jnp.bfloat16),
             pltpu.VMEM((ff, features), jnp.bfloat16),
             pltpu.VMEM((2, group, features), jnp.bfloat16),
-            pltpu.VMEM((2, group, features), jnp.bfloat16),
             pltpu.VMEM((2, group, ff), jnp.bfloat16),
             pltpu.VMEM((2, group, ff), jnp.bfloat16),
+            pltpu.VMEM((2, group, out_w.shape[0]), jnp.bfloat16),
         ]
         + first[2:]
         + second[2:]
         + Gather.sems()
-        + [dma(pieces), dma(pieces), dma(pieces), dma(2), dma(2), dma(2), dma(2), dma(1)],
+        + [dma(pieces), dma(pieces), dma(pieces), dma(2), dma(2), dma(2), dma(1)]
+        + [dma(2)]
+        + attend_scratch,
         compiler_params=pltpu.CompilerParams(
             collective_id=number, has_side_effects=True, vmem_limit_bytes=62 * MIB
         ),
@@ -1341,11 +1394,11 @@
 
 
 def start_kernel(
-    facts,
-    hidden,
+    lengths,
     gain,
     shift,
     bias,
+    hidden_in,
     shard,
     out_shard,
     q_ref,
@@ -1360,8 +1413,10 @@
     out_weight,
     total,
     summary,
+    hidden,
     *sems,
 ):
+    facts = Facts(lengths)
     gather = Gather((shard, out_shard), (weight, out_weight), sems[:3], 0)
     summary_sent, summary_got, out_sems = sems[3:]
     rows = hidden.shape[0]
@@ -1370,6 +1425,8 @@
     chunk = 128
     barrier = pltpu.get_barrier_semaphore()
     gather.greet(barrier)
+    load = pltpu.make_async_copy(hidden_in, hidden, out_sems.at[3])
+    load.start()
     gather.first()
     pl.semaphore_wait(barrier, gather.others)
     gather.send(0, (1, 2, 0))
@@ -1380,6 +1437,7 @@
         normed[here, :] = (value * gain[...] + shift[...]).astype(jnp.bfloat16)
         return carry
 
+    load.wait()
     lax.fori_loop(0, rows // chunk, norm, 0)
     keep = pltpu.make_async_copy(normed, normed_out, out_sems.at[0])
     keep.start()
@@ -1457,14 +1515,14 @@
     store_out.wait()
 
 
-def start(number, facts, hidden, gain, shift, bias, shard, out_shard):
+def start(number, lengths, hidden, gain, shift, bias, shard, out_shard):
     rows, features = hidden.shape
     width = bias.shape[1]
     low = lambda *shape: jax.ShapeDtypeStruct(shape, jnp.bfloat16)
     dma = lambda n: pltpu.SemaphoreType.DMA((n,))
     return pl.pallas_call(
         start_kernel,
-        in_specs=[SMEM] + [VMEM] * 4 + [ANY] * 2,
+        in_specs=[SMEM] + [VMEM] * 3 + [ANY] * 3,
         out_specs=[VMEM] * 3 + [ANY] * 4,
         out_shape=[low(rows, width)] * 3
         + [low(2, SUMM_ROWS, width), low(rows, features), low(features, 3 * width)]
@@ -1475,9 +1533,10 @@
             pltpu.VMEM((width, features), jnp.bfloat16),
             pltpu.VMEM((rows, 3 * width), jnp.float32),
             pltpu.VMEM((2, SUMM_ROWS, width), jnp.bfloat16),
+            pltpu.VMEM((rows, features), jnp.bfloat16),
         ]
         + Gather.sems()
-        + [dma(1), dma(1), dma(3)],
+        + [dma(1), dma(1), dma(4)],
         compiler_params=pltpu.CompilerParams(
             collective_id=number, has_side_effects=True, vmem_limit_bytes=60 * MIB
         ),
@@ -1485,7 +1544,7 @@
             flops=6 * rows * features * width, bytes_accessed=16 * rows * features, transcendentals=0
         ),
         name="start",
-    )(facts, hidden, gain, shift, bias, shard, out_shard)
+    )(lengths, gain, shift, bias, hidden, shard, out_shard)
 
 
 class SmallSums(Nothing):
@@ -1548,7 +1607,7 @@
                 )
             self.copy(0).start()
 
-        row = lax.broadcasted_iota(jnp.int32, self.own.shape, 0)
+        row = lax.broadcasted_iota(jnp.int32, self.out.shape, 0)
         for number, (axis, _) in enumerate(self.stages):
 
             @pl.when(t == self.start + 1 + number)
@@ -1575,7 +1634,7 @@
 
 
 class Ring:
-    depth = 4
+    depth = 2
 
     def __init__(self, source, buffer, sems, pieces, offset):
         self.source, self.buffer, self.sems = source, buffer, sems
@@ -1614,12 +1673,14 @@
     count,
     half,
     sizes,
-    facts,
+    lengths,
     lse,
     earlier,
     down_bias,
     pre_gain,
-    small_own,
+    mid_sums,
+    up_sums,
+    down_sums,
     q_in,
     k_in,
     v_in,
@@ -1665,6 +1726,7 @@
     *rest,
 ):
     rest = list(rest)
+    facts = Facts(lengths)
     take = lambda n: [rest.pop(0) for _ in range(n)]
     rings = take(6)
     sems1, sems2 = take(5), take(5)
@@ -1717,7 +1779,8 @@
     heads.pairs = width // PAIR
     heads.steps = heads.pairs * heads.blocks
     heads.causal = True
-    views = [Columns(moving2, j * width, width) for j in range(4)]
+    first = moving2.at[pl.ds(0, rows)]
+    views = [Columns(first, j * width, width) for j in range(4)]
     tables = [earlier.at[0], earlier.at[1]]
     heads.ins = (facts, *views[:3], *tables, views[3], lse)
     heads.outs = (dq, dk, dv, dks, dvs)
@@ -1739,14 +1802,17 @@
         rest,
         heads.steps - 2,
     )
-    small = SmallSums(sizes, 6, second + pieces + SKEW * (count - 1), small_own)
-    small((small_own,), (sums_out,), (small_sent, small_got, *small_sems), (acc,))
+    small = SmallSums(sizes, 6, second + pieces + SKEW * (count - 1), sums_out)
+    small((None,), (sums_out,), (small_sent, small_got, *small_sems), (acc,))
+    column_sums = lambda values: jnp.sum(values, axis=0, keepdims=True)
+    features = down_in.shape[1]
+    ff_rows = down_in.shape[0] // features
     loads = [
         pltpu.make_async_copy(source, target, load_sem.at[number])
         for number, (source, target) in enumerate(
             [(down_in, down), (qkv_in, qkv_w)]
             + [
-                (source, moving2.at[:, pl.ds(j * width, width)])
+                (source, first.at[:, pl.ds(j * width, width)])
                 for j, source in enumerate((q_in, k_in, v_in, do_in))
             ]
         )
@@ -1775,11 +1841,17 @@
             ring.fill()
 
     acc[...] = jnp.zeros_like(acc)
-    small.first()
+    small_sent[0] = jnp.zeros_like(small_sent[0])
+    for number in range(3):
+        small_sent[0, number : number + 1, :] = mid_sums[number : number + 1, :]
+    small_sent[0, 5:6, :] = jnp.where(me == 0, column_sums(down_sums[...]), 0.0)
+    for number in range(ff_rows):
+        cols = slice(number * features, (number + 1) * features)
+        small_sent[0, 6 + number : 7 + number, :] = column_sums(up_sums[:, cols])
     loads[0].wait()
     line1.first()
     line1.meet(barrier, spread.others + small.others)
-    for load in loads[1:]:
+    for load in loads[2:]:
         load.wait()
 
     def step(t, carry):
@@ -1795,6 +1867,7 @@
         @pl.when(t == heads.steps + 1)
         def _():
             swap.wait()
+            loads[1].wait()
             shape = (rows, SUMM_ROWS)
             chosen = lax.broadcasted_iota(jnp.int32, shape, 0) == (
                 facts[1] - SUMM + lax.broadcasted_iota(jnp.int32, shape, 1)
@@ -1804,7 +1877,7 @@
                 added = grad[...].astype(jnp.float32) + mm(chosen, swap_in[number])
                 grad[...] = added.astype(jnp.bfloat16)
             for number, grad in enumerate((dq, dv)):
-                small.extra(6 + down_in.shape[0] // down_in.shape[1], number * width, grad)
+                small.extra(6 + ff_rows, number * width, grad)
 
         line2.step(t - second)
         spread.step(t)
@@ -1817,7 +1890,7 @@
     spread.settle()
 
 
-def back_sums(number, count, sizes, small_in, whole_in, vmem_in):
+def back_sums(number, count, sizes, whole_in, vmem_in):
     rows, width = whole_in[0].shape
     features = whole_in[5].shape[1]
     ff = whole_in[5].shape[0]
@@ -1829,9 +1902,10 @@
     group = lines[0].shape[2]
     stages = sum(size.bit_length() - 1 for _, size in sizes)
     block = Spread.block
+    sums_shape = (6 + ff // features + -(-2 * width // features), features)
     return pl.pallas_call(
         functools.partial(back_kernel, count, half, sizes),
-        in_specs=[SMEM] + [VMEM] * 5 + [ANY] * len(whole_in),
+        in_specs=[SMEM] + [VMEM] * 7 + [ANY] * len(whole_in),
         out_specs=[ANY] * 6 + [VMEM],
         out_shape=[
             jax.ShapeDtypeStruct((rows, features), jnp.bfloat16),
@@ -1840,7 +1914,7 @@
             jax.ShapeDtypeStruct((ff, block), jnp.float32),
             jax.ShapeDtypeStruct((width, block), jnp.float32),
             jax.ShapeDtypeStruct((block, 3 * width), jnp.float32),
-            jax.ShapeDtypeStruct(small_in.shape, jnp.float32),
+            jax.ShapeDtypeStruct(sums_shape, jnp.float32),
         ],
         scratch_shapes=[
             lines[0],
@@ -1860,8 +1934,8 @@
             low(2, SUMM_ROWS, width),
             low(2, group, ff),
             wide(2, 8, features),
-            wide(stages, *small_in.shape),
-            wide(stages, *small_in.shape),
+            wide(stages, *sums_shape),
+            wide(stages, *sums_shape),
         ]
         + Ring.scratch(features, jnp.float32)
         + Ring.scratch(features, jnp.float32)
@@ -1877,7 +1951,7 @@
             flops=12 * rows * features * ff, bytes_accessed=60 * rows * features, transcendentals=0
         ),
         name="back_sums",
-    )(*vmem_in, small_in, *whole_in)
+    )(*vmem_in, *whole_in)
 
 
 def gradients_over(group, lefts, columns):
@@ -1939,9 +2013,9 @@
     shard = qkv_weight.reshape(-1, 3 * width)
     if ours:
         q, k, v, summary, normed, qkv_full, out_full = start(
-            5, facts, hidden_in[0], row(pre_gain), row(pre_shift), qv_bias, shard, out_weight
-        )
-        attend_in = (facts, q, k, v, summary)
+            5, seg_lengths, hidden_in[0], row(pre_gain), row(pre_shift), qv_bias, shard, out_weight
+        )
+        attend_in = (seg_lengths, summary, q, k, v)
         tables = (k, v, summary[0], summary[1])
     else:
         qkv_full = gathered(shard, 0)
@@ -1967,6 +2041,7 @@
         mid_sums,
         up_sums,
         down_sums,
+        grad_attended,
         *attend_out,
     ) = ffn_sums(
         1,
@@ -1982,7 +2057,6 @@
     )
     if ours:
         attended, log_total = attend_out
-    grad_attended = mm(grad_branch, out_full, NT).astype(jnp.bfloat16)
     total = lambda value: jnp.sum(value.astype(jnp.float32), axis=0)
     features = hidden.shape[1]
     sizes = [("item", item_count), ("seq", seq_count), ("mp", mp_count)]
@@ -2001,10 +2075,10 @@
             2,
             mp_count,
             sizes,
-            small_in(jnp.zeros((2 * width,), jnp.float32)),
             (q, k, v, grad_attended, act_low, down_full, residual, hidden_in[0], grad_residual)
             + (qkv_full, mid_low, grad_down, grad_branch, normed, grad_pre, attended),
-            (facts, log_total, summary, row(down_bias), row(pre_gain)),
+            (seg_lengths, log_total, summary, row(down_bias), row(pre_gain))
+            + (jnp.sum(mid_sums, axis=1), up_sums, down_sums),
         )
     else:
         hidden_out, dq, dk, dv, dks, dvs = line_sum(

time: 625 us -> 616 us (0.986); the launches traced: 622 us -> 620 us
  Pallas kernels: 586 us -> 594 us
  matrix products: 7.17 us -> 0 us
    pallas_call x1, Pallas kernels: 269 us -> 277 us  [ffn_sums(): pl.pallas_call(functools.partial(ffn_kernel, count, half, weights_job, le...]
    dot_general x1 -> x0, matrix products: 7.17 us -> none  [mm(): lax.dot_general(left, right, dims, preferred_element_type=jnp.float32)]
where the time goes in v7:
time: 616 us; the launch traced here: 620 us
  Pallas kernels  594 us (96%)
  local copies, waits for them, and re-layouts  15.5 us (3%)
  other arithmetic  9.77 us (2%)
    pallas_call x1, Pallas kernels, ffn_sums(): pl.pallas_call(functools.partial(ffn_kernel, count, half, weights_job, le...  277 us
    pallas_call x1, Pallas kernels, back_sums(): pl.pallas_call(functools.partial(back_kernel, count, half, sizes), in_spe...  269 us
    pallas_call x1, Pallas kernels, start(): pl.pallas_call(start_kernel, in_specs=[SMEM] + [VMEM] * 3 + [ANY] * 3, ou...  47.4 us

profile of v7, /device:TPU:0, one launch (start us, length us, event | category | flops | bytes accessed | tf_op | source)
XLA Modules:
  0.0 619.9 jit_solution(18318169928091202609)
XLA Ops:
  0.6 1.4 copy.31
  2.1 1.2 copy.32.shard
  3.2 47.4 %start.1 = (bf16[1280,512]{1,0:T(8,128)(2,1)}, bf16[1280,512]{1,0:T(8,128)(2,1)}, bf16[1280,512]{1,0:T(8,128)(2,1)}, bf16[2,64,512]{2,1,0:T(8,128)(2,1)}, bf16[1...) custom-call(s32[1,2]{1,0:T(1,128)} %lengths.3, f32[1,2048]{1,0:T(1,128)} %bitcast.44, ...), custom_call_target="tpu_custom_call" | custom-call | flops 8053063680 | bytes 41943040 | tf_op jit(solution)/shard_map/start/pallas_call | solution.py:1523
  50.6 277.2 %ffn_sums.1 = (bf16[1280,2048]{1,0:T(8,128)(2,1)}, bf16[1280,2048]{1,0:T(8,128)(2,1)}, bf16[1280,2048]{1,0:T(8,128)(2,1)}, f32[640,2048]{1,0:T(8,128)}, bf16[128...) custom-call(s32[1,2]{1,0:T(1,128)} %lengths.3, ...), custom_call_target="tpu_custom_call" | custom-call | flops 32212254720 | bytes 78643200 | tf_op jit(solution)/shard_map/ffn_sums/pallas_call | solution.py:1350
  327.9 1.6 reduce_sum.9.mid_sums
  329.5 269.0 %back_sums.1 = (bf16[1280,2048]{1,0:T(8,128)(2,1)}, bf16[1280,2048]{1,0:T(8,128)(2,1)}, f32[256,2048]{1,0:T(8,128)}, f32[2048,256]{1,0:T(8,128)}, f32[512,256]{1...) custom-call(s32[1,2]{1,0:T(1,128)} %lengths.3, f32[4,2,1280]{2,1,0:T(2,128)} %get-tuple-element.46.lse, ...), custom_call_target="tpu_custom_call" | custom-call | flops 64424509440 | bytes 157286400 | tf_op jit(solution)/shard_map/back_sums/pallas_call | solution.py:1906
  598.5 0.8 slice_reduce_fusion
  599.3 1.8 fusion
  601.1 0.6 reshape.45
  601.7 1.9 copy.33
  603.5 0.0 slice-start
  603.6 1.6 copy.34
  605.2 0.0 slice-start.1
  605.2 8.2 %bitcast_convert_fusion = f32[1,1280,2048]{2,1,0:T(8,128)} fusion(bf16[1280,2048]{1,0:T(8,128)(2,1)} %get-tuple-element.62), kind=kLoop, calls=%fused_computation | loop fusion | flops 2621440 | bytes 15728640 | tf_op jit(solution)/shard_map/broadcast_in_dim | solution.py:2132
  613.3 0.0 slice-done
  613.3 0.0 slice-done.1
  613.4 0.0 copy-start.2
  613.4 0.0 copy-start.1
  613.4 2.7 copy.39
  616.0 0.0 copy-done.2
  616.0 0.0 copy-start
  616.0 0.8 copy.40
  616.8 0.2 copy-done.1
  617.0 1.3 copy.41
  618.3 0.0 copy-done
  618.3 1.3 copy.42
  (1 shorter events, 0.0 us)
Async XLA Ops:
  603.5 9.8 %slice-start = ((s8[5242880]{0:T(1024)(128)(4,1)}), s8[1048576]{0:T(1024)(128)(4,1)S(1)}, s32[]{:S(2)}) async-start(s8[5242880]{0:T(1024)(128)(4,1)} %bitcast.23), calls=%async_computation | async-start | bytes 2097152
  605.2 8.2 %slice-start.1 = ((s8[5242880]{0:T(1024)(128)(4,1)}), s8[4194304]{0:T(1024)(128)(4,1)S(1)}, s32[]{:S(2)}) async-start(s8[5242880]{0:T(1024)(128)(4,1)} %bitcast.23), calls=%async_computation.1 | async-start | bytes 8388608
  613.4 2.7 copy-start.2
  613.4 3.7 copy-start.1
  616.0 2.3 copy-start

commit v8 on v7

--- a/solution.py
+++ b/solution.py
@@ -18,7 +18,7 @@
 PIECE = 32
 SKEW = 2
 LEAD = 2
-GATHER_STEPS = (7, 11, 13, 15)
+GATHER_STEPS = (10, 11, 14, 15)
 MIB = 1 << 20
 MESH = pl.DeviceIdType.MESH
 MASKED = -1e30
@@ -172,9 +172,9 @@
 
 
 class Line:
-    def __init__(self, count, half, multiply, finish, out, part, moving, sems, late=False):
+    def __init__(self, count, half, multiply, finish, out, part, moving, sems, late=False, wide=None):
         self.count, self.half, self.multiply, self.finish = count, half, multiply, finish
-        self.late = late
+        self.late, self.wide = late, wide
         self.out, self.part, self.moving = out, part, moving
         self.up_sent, self.up_got, self.down_sent, self.down_got, self.local = sems
         self.me = lax.axis_index("mp")
@@ -259,11 +259,23 @@
         )
 
     def keep(self, flow, k, owner):
+        spots = self.moving.at[self.spots(flow, k + LEAD if owner else k)]
         return pltpu.make_async_copy(
-            self.moving.at[self.spots(flow, k + LEAD if owner else k)],
+            spots if self.wide is None else self.wide.at[flow],
             self.out.at[pl.ds(flow * self.half + k * PIECE, PIECE)],
             self.local.at[flow, k],
         )
+
+    def store(self, flow, k, owner):
+        if self.wide is not None:
+
+            @pl.when(k >= 1)
+            def _():
+                self.keep(flow, k - 1, owner).wait()
+
+            spots = self.spots(flow, k + LEAD if owner else k)
+            self.wide[flow] = self.moving[spots, :].astype(jnp.float32)
+        self.keep(flow, k, owner).start()
 
     def send_on(self, flow, k):
         @pl.when(k >= LEAD)
@@ -303,7 +315,7 @@
                 total = mine() + self.moving[here, :].astype(jnp.float32)
                 self.moving[here, :] = self.finish(flow, k, total).astype(jnp.bfloat16)
                 self.back(flow, k, True).start()
-                self.keep(flow, k, True).start()
+                self.store(flow, k, True)
 
         for flow in range(2):
             place = self.place(flow)
@@ -317,7 +329,7 @@
                 def _():
                     self.back(flow, j, False).start()
 
-                self.keep(flow, j, False).start()
+                self.store(flow, j, False)
 
         for flow in range(2 if self.multiply else 0):
             k = t - SKEW * self.place(flow)
@@ -348,14 +360,13 @@
                 def _():
                     self.back(flow, k, False).wait_send()
 
-                @pl.when(place < last)
-                def _():
-                    self.keep(flow, k, False).wait()
-
                 @pl.when(place == last)
                 def _():
                     self.back(flow, k, True).wait_send()
-                    self.keep(flow, k, True).wait()
+
+                @pl.when((k == self.pieces - 1) | (self.wide is None))
+                def _():
+                    self.keep(flow, k, False).wait()
 
             return carry
 
@@ -641,7 +652,7 @@
         wide = lambda *shape: pltpu.VMEM(shape, jnp.float32)
         return [
             low(2, rows, block),
-            low(3, 2, block, 2 * block),
+            low(2, 2, block, 2 * block),
             wide(3, 2, block, 2 * block),
             low(4, 2, block, 2 * block),
             low(3, half, 2 * block),
@@ -654,7 +665,7 @@
             wide(3, 2, half, block),
             low(6, 2, half, block),
             wide(3, block, block),
-        ] + [pltpu.SemaphoreType.DMA((n,)) for n in (1, 2, 3, 4, 3, 6, 3, 6, 3, 6, 3, 6, 3)]
+        ] + [pltpu.SemaphoreType.DMA((n,)) for n in (1, 2, 2, 4, 3, 6, 3, 6, 3, 6, 3, 6, 3)]
 
     def greet(self, barrier):
         for to in (self.to_core, self.to_x, self.to_y):
@@ -695,9 +706,9 @@
 
     def first_copy(self, m):
         return self.remote(
-            self.s1.at[m % 3],
+            self.s1.at[m % 2],
             self.r1.at[m % 4],
-            self.s1_sem.at[m % 3],
+            self.s1_sem.at[m % 2],
             self.r1_sem.at[m % 4],
             self.to_core,
         )
@@ -766,9 +777,9 @@
 
         self.right_copy(m, lambda copy: copy.wait())
 
-        @pl.when(m >= 3)
-        def _():
-            self.first_copy(m - 3).wait_send()
+        @pl.when(m >= 2)
+        def _():
+            self.first_copy(m - 2).wait_send()
 
         turned = self.y_buf[m % 2].T
         wide = 2 * self.block
@@ -778,7 +789,7 @@
             return mm(turned, self.x_buf[:, cols])
 
         for x in range(2):
-            self.s1[m % 3, x] = product(x, 1 - self.core).astype(jnp.bfloat16)
+            self.s1[m % 2, x] = product(x, 1 - self.core).astype(jnp.bfloat16)
         self.first_copy(m).start()
         for x in range(2):
             self.own[m % 3, x] = product(x, self.core)
@@ -856,7 +867,8 @@
 
     def settle(self):
         for m in range(self.chunks - 3, self.chunks):
-            self.first_copy(m).wait_send()
+            if m >= self.chunks - 2:
+                self.first_copy(m).wait_send()
             for copy in self.second_copies(m) + self.third_copies(m):
                 copy.wait_send()
             self.out_copy(jnp.int32(m), lambda copy: copy.wait())
@@ -1269,12 +1281,12 @@
         line1.meet(barrier, weights.others)
         weights.begin()
     else:
-        line1.meet(barrier, weights.others)
-        weights.begin()
         for load in attention.loads:
             load.wait()
         attention.first()
         line1.first()
+        line1.meet(barrier, weights.others)
+        weights.begin()
 
     def step(t, carry):
         if attention is not None:
@@ -1723,6 +1735,7 @@
     acc,
     small_sent,
     small_got,
+    wide_out,
     *rest,
 ):
     rest = list(rest)
@@ -1771,7 +1784,7 @@
     line1 = Line(count, half, multiply_down, finish_first, hidden_out, part, moving1, sems1)
     multiply_back = group_product([dq, dk, dv], qkv_w, NT, half, group)
     line2 = Line(
-        count, half, multiply_back, finish_second, input_grad, part, moving2, sems2, late=True
+        count, half, multiply_back, finish_second, input_grad, part, moving2, sems2, late=True, wide=wide_out
     )
     heads = AttendBack.__new__(AttendBack)
     heads.bq = query_block(rows)
@@ -1909,7 +1922,7 @@
         out_specs=[ANY] * 6 + [VMEM],
         out_shape=[
             jax.ShapeDtypeStruct((rows, features), jnp.bfloat16),
-            jax.ShapeDtypeStruct((rows, features), jnp.bfloat16),
+            jax.ShapeDtypeStruct((rows, features), jnp.float32),
             jax.ShapeDtypeStruct((block, ff), jnp.float32),
             jax.ShapeDtypeStruct((ff, block), jnp.float32),
             jax.ShapeDtypeStruct((width, block), jnp.float32),
@@ -1936,6 +1949,7 @@
             wide(2, 8, features),
             wide(stages, *sums_shape),
             wide(stages, *sums_shape),
+            wide(2, PIECE, features),
         ]
         + Ring.scratch(features, jnp.float32)
         + Ring.scratch(features, jnp.float32)

time: 616 us -> 616 us (level)
  local copies, waits for them, and re-layouts: 15.5 us -> 24.5 us
  other arithmetic: 9.77 us -> 1.6 us
    pallas_call x1, Pallas kernels: 277 us -> 263 us  [ffn_sums(): pl.pallas_call(functools.partial(ffn_kernel, count, half, weights_job, le...]
    pallas_call x1, Pallas kernels: 269 us -> 281 us  [back_sums(): pl.pallas_call(functools.partial(back_kernel, count, half, sizes), in_spe...]
    unnamed x16 -> x15, local copies, waits for them, and re-layouts: 9.31 us -> 18.3 us
    broadcast_in_dim x1 -> x0, other arithmetic: 8.17 us -> none  [body(): grad_input.astype(jnp.float32)[None]]
where the time goes in v8:
time: 616 us; the launch traced here: 619 us
  Pallas kernels  592 us (96%)
  local copies, waits for them, and re-layouts  24.5 us (4%)
    pallas_call x1, Pallas kernels, back_sums(): pl.pallas_call(functools.partial(back_kernel, count, half, sizes), in_spe...  281 us
    pallas_call x1, Pallas kernels, ffn_sums(): pl.pallas_call(functools.partial(ffn_kernel, count, half, weights_job, le...  263 us
    pallas_call x1, Pallas kernels, start(): pl.pallas_call(start_kernel, in_specs=[SMEM] + [VMEM] * 3 + [ANY] * 3, ou...  47.4 us
    unnamed x15, local copies, waits for them, and re-layouts  18.3 us

profile of v8, /device:TPU:0, one launch (start us, length us, event | category | flops | bytes accessed | tf_op | source)
XLA Modules:
  0.0 618.6 jit_solution(10986768047515605856)
XLA Ops:
  0.6 1.4 copy.31
  2.1 1.2 copy.32.shard
  3.2 47.4 %start.1 = (bf16[1280,512]{1,0:T(8,128)(2,1)}, bf16[1280,512]{1,0:T(8,128)(2,1)}, bf16[1280,512]{1,0:T(8,128)(2,1)}, bf16[2,64,512]{2,1,0:T(8,128)(2,1)}, bf16[1...) custom-call(s32[1,2]{1,0:T(1,128)} %lengths.3, f32[1,2048]{1,0:T(1,128)} %bitcast.41, ...), custom_call_target="tpu_custom_call" | custom-call | flops 8053063680 | bytes 41943040 | tf_op jit(solution)/shard_map/start/pallas_call | solution.py:1535
  50.7 263.3 %ffn_sums.1 = (bf16[1280,2048]{1,0:T(8,128)(2,1)}, bf16[1280,2048]{1,0:T(8,128)(2,1)}, bf16[1280,2048]{1,0:T(8,128)(2,1)}, f32[640,2048]{1,0:T(8,128)}, bf16[128...) custom-call(s32[1,2]{1,0:T(1,128)} %lengths.3, ...), custom_call_target="tpu_custom_call" | custom-call | flops 32212254720 | bytes 78643200 | tf_op jit(solution)/shard_map/ffn_sums/pallas_call | solution.py:1362
  314.0 1.6 reduce_sum.9.mid_sums
  315.6 280.8 %back_sums.1 = (bf16[1280,2048]{1,0:T(8,128)(2,1)}, f32[1280,2048]{1,0:T(8,128)}, f32[256,2048]{1,0:T(8,128)}, f32[2048,256]{1,0:T(8,128)}, f32[512,256]{1,0:T(8...) custom-call(s32[1,2]{1,0:T(1,128)} %lengths.3, f32[4,2,1280]{2,1,0:T(2,128)} %get-tuple-element.46.lse, ...), custom_call_target="tpu_custom_call" | custom-call | flops 64424509440 | bytes 157286400 | tf_op jit(solution)/shard_map/back_sums/pallas_call | solution.py:1919
  596.5 0.8 slice_reduce_fusion
  597.2 1.8 fusion
  599.0 0.6 reshape.45
  599.6 1.9 copy.33
  601.5 1.6 copy.34
  603.1 0.0 copy-start
  603.1 6.2 copy.40
  609.3 1.3 copy-done
  610.6 0.0 copy-start.3
  610.6 0.0 copy-start.2
  610.6 4.4 copy.41
  615.0 0.0 copy-done.3
  615.0 0.0 copy-start.1
  615.0 0.8 copy.42
  615.8 0.0 copy-done.2
  615.8 1.3 copy.43
  617.1 0.0 copy-done.1
  617.1 1.3 copy.44
Async XLA Ops:
  603.1 7.4 %copy-start = (f32[1280,2048]{1,0:T(8,128)S(1)}, f32[1280,2048]{1,0:T(8,128)}, u32[]{:S(2)}) copy-start(f32[1280,2048]{1,0:T(8,128)} %get-tuple-element.62) | copy-start | bytes 31457284
  610.6 4.4 copy-start.3
  610.6 5.2 copy-start.2
  615.0 2.1 copy-start.1

commit v9 on v7

--- a/solution.py
+++ b/solution.py
@@ -1401,9 +1401,9 @@
     hidden_in,
     shard,
     out_shard,
-    q_ref,
-    k_ref,
-    v_ref,
+    q_out,
+    k_out,
+    v_out,
     earlier,
     normed_out,
     weight_out,
@@ -1414,6 +1414,9 @@
     total,
     summary,
     hidden,
+    q_ref,
+    k_ref,
+    v_ref,
     *sems,
 ):
     facts = Facts(lengths)
@@ -1485,6 +1488,14 @@
     store = pltpu.make_async_copy(weight, weight_out, out_sems.at[1])
     store.start()
     add(((1 - x, 1 - c, 1 - y),), last=True)
+    results = [
+        pltpu.make_async_copy(source, target, out_sems.at[4 + number])
+        for number, (source, target) in enumerate(
+            ((q_ref, q_out), (k_ref, k_out), (v_ref, v_out))
+        )
+    ]
+    for result in results:
+        result.start()
 
     shape = (SUMM_ROWS, rows)
     chosen = lax.broadcasted_iota(jnp.int32, shape, 1) == (
@@ -1513,6 +1524,8 @@
     store.wait()
     swap.wait()
     store_out.wait()
+    for result in results:
+        result.wait()
 
 
 def start(number, lengths, hidden, gain, shift, bias, shard, out_shard):
@@ -1523,7 +1536,7 @@
     return pl.pallas_call(
         start_kernel,
         in_specs=[SMEM] + [VMEM] * 3 + [ANY] * 3,
-        out_specs=[VMEM] * 3 + [ANY] * 4,
+        out_specs=[ANY] * 7,
         out_shape=[low(rows, width)] * 3
         + [low(2, SUMM_ROWS, width), low(rows, features), low(features, 3 * width)]
         + [low(width, features)],
@@ -1535,8 +1548,9 @@
             pltpu.VMEM((2, SUMM_ROWS, width), jnp.bfloat16),
             pltpu.VMEM((rows, features), jnp.bfloat16),
         ]
+        + [pltpu.VMEM((rows, width), jnp.bfloat16)] * 3
         + Gather.sems()
-        + [dma(1), dma(1), dma(4)],
+        + [dma(1), dma(1), dma(7)],
         compiler_params=pltpu.CompilerParams(
             collective_id=number, has_side_effects=True, vmem_limit_bytes=60 * MIB
         ),

time: 616 us -> 614 us (level)
  no operation moved by 1% of the time
where the time goes in v9:
time: 614 us; the launch traced here: 618 us
  Pallas kernels  592 us (96%)
  local copies, waits for them, and re-layouts  15.5 us (3%)
  other arithmetic  9.77 us (2%)
    pallas_call x1, Pallas kernels, ffn_sums(): pl.pallas_call(functools.partial(ffn_kernel, count, half, weights_job, le...  277 us
    pallas_call x1, Pallas kernels, back_sums(): pl.pallas_call(functools.partial(back_kernel, count, half, sizes), in_spe...  269 us
    pallas_call x1, Pallas kernels, start(): pl.pallas_call(start_kernel, in_specs=[SMEM] + [VMEM] * 3 + [ANY] * 3, ou...  45.5 us

profile of v9, /device:TPU:0, one launch (start us, length us, event | category | flops | bytes accessed | tf_op | source)
XLA Modules:
  0.0 618.0 jit_solution(4391177589980939353)
XLA Ops:
  0.6 1.4 copy.31
  2.1 1.2 copy.32.shard
  3.2 45.5 %start.1 = (bf16[1280,512]{1,0:T(8,128)(2,1)}, bf16[1280,512]{1,0:T(8,128)(2,1)}, bf16[1280,512]{1,0:T(8,128)(2,1)}, bf16[2,64,512]{2,1,0:T(8,128)(2,1)}, bf16[1...) custom-call(s32[1,2]{1,0:T(1,128)} %lengths.3, f32[1,2048]{1,0:T(1,128)} %bitcast.44, ...), custom_call_target="tpu_custom_call" | custom-call | flops 8053063680 | bytes 41943040 | tf_op jit(solution)/shard_map/start/pallas_call | solution.py:1536
  48.7 277.2 %ffn_sums.1 = (bf16[1280,2048]{1,0:T(8,128)(2,1)}, bf16[1280,2048]{1,0:T(8,128)(2,1)}, bf16[1280,2048]{1,0:T(8,128)(2,1)}, f32[640,2048]{1,0:T(8,128)}, bf16[128...) custom-call(s32[1,2]{1,0:T(1,128)} %lengths.3, ...), custom_call_target="tpu_custom_call" | custom-call | flops 32212254720 | bytes 78643200 | tf_op jit(solution)/shard_map/ffn_sums/pallas_call | solution.py:1350
  326.0 1.6 reduce_sum.9.mid_sums
  327.6 269.0 %back_sums.1 = (bf16[1280,2048]{1,0:T(8,128)(2,1)}, bf16[1280,2048]{1,0:T(8,128)(2,1)}, f32[256,2048]{1,0:T(8,128)}, f32[2048,256]{1,0:T(8,128)}, f32[512,256]{1...) custom-call(s32[1,2]{1,0:T(1,128)} %lengths.3, f32[4,2,1280]{2,1,0:T(2,128)} %get-tuple-element.46.lse, ...), custom_call_target="tpu_custom_call" | custom-call | flops 64424509440 | bytes 157286400 | tf_op jit(solution)/shard_map/back_sums/pallas_call | solution.py:1920
  596.6 0.8 slice_reduce_fusion
  597.3 1.8 fusion
  599.1 0.6 reshape.45
  599.7 1.9 copy.33
  601.6 0.0 slice-start
  601.6 1.6 copy.34
  603.2 0.0 slice-start.1
  603.2 8.2 %bitcast_convert_fusion = f32[1,1280,2048]{2,1,0:T(8,128)} fusion(bf16[1280,2048]{1,0:T(8,128)(2,1)} %get-tuple-element.62), kind=kLoop, calls=%fused_computation | loop fusion | flops 2621440 | bytes 15728640 | tf_op jit(solution)/shard_map/broadcast_in_dim | solution.py:2146
  611.4 0.0 slice-done
  611.4 0.0 slice-done.1
  611.4 0.0 copy-start.2
  611.4 0.0 copy-start.1
  611.4 2.7 copy.39
  614.1 0.0 copy-done.2
  614.1 0.0 copy-start
  614.1 0.8 copy.40
  614.9 0.2 copy-done.1
  615.1 1.3 copy.41
  616.4 0.0 copy-done
  616.4 1.3 copy.42
  (1 shorter events, 0.0 us)
Async XLA Ops:
  601.6 9.8 %slice-start = ((s8[5242880]{0:T(1024)(128)(4,1)}), s8[1048576]{0:T(1024)(128)(4,1)S(1)}, s32[]{:S(2)}) async-start(s8[5242880]{0:T(1024)(128)(4,1)} %bitcast.23), calls=%async_computation | async-start | bytes 2097152
  603.2 8.2 %slice-start.1 = ((s8[5242880]{0:T(1024)(128)(4,1)}), s8[4194304]{0:T(1024)(128)(4,1)S(1)}, s32[]{:S(2)}) async-start(s8[5242880]{0:T(1024)(128)(4,1)} %bitcast.23), calls=%async_computation.1 | async-start | bytes 8388608
  611.4 2.7 copy-start.2
  611.4 3.7 copy-start.1
  614.1 2.3 copy-start
